TPU v7x, 128 devices: a whole 4x4x4 slice. The times are simulated.
128 devices in a mesh: row: 16 (over z, y), col: 8 (over x, core).
Axes of the slice: x: 4, y: 4, z: 4, core: 2. Of those that a mesh axis runs over, the one named last changes fastest.
Arguments:
- sample: float32 [2, 8192, 8192], P(None, 'row', 'col'), may hold values from -6 to 6
- probe_field: float32 [2, 256, 256], replicated, may hold values from -6 to 6
- patterns: float32 [2048, 256, 256], P(('row', 'col')), may hold values from 1 to 16
- positions: int32 [2048, 2], P(('row', 'col')), may hold values from 0 to 8191, as said below
- counts: int32 [128], replicated, may hold values from 1 to 16, as said below
Outputs:
- object_grad: float32 [2, 8192, 8192], P(None, 'row', 'col')
- probe_grad: float32 [2, 256, 256], replicated
- mean_misfit: float32 [], replicated
Inputs may be any that keep to these rules, and one draw needn't show every extreme that they name: `positions`: slot s lies in the block of slots of tile s // 16 (tiles in row-major order over the object's 16 x 8 tiles), and its top-left pixel lies inside that tile. `counts`: some tile has all 16 slots live.
All inputs are finite; a program needn't handle non-finite values.
Results may differ from a plain program's by a relative error of at most 0.0003.
Values sent between devices are 32-bit elements; how exact they have to be, the bound alone decides.
A program may use at most 128 MiB of HBM per device.

v0:
```python
import math

import jax
import jax.numpy as jnp
from jax import lax
from jax.sharding import PartitionSpec as P


def passed_along(value, axis, steps):
    count = lax.axis_size(axis)
    first, last = (max(0, -steps), min(count, count - steps))
    return lax.ppermute(value, axis, [(source, source + steps) for source in range(first, last)])


def dft_tables(pixels):
    index_line = jnp.arange(pixels, dtype=jnp.int32)
    product = index_line[:, None] * index_line[None, :] % pixels
    angle = product.astype(jnp.float32) * (2.0 * math.pi / pixels)
    factor = 1.0 / math.sqrt(pixels)
    return (jnp.cos(angle) * factor, -jnp.sin(angle) * factor)


def transform(real_part, imag_part, cosine, sine_table):
    high = lax.Precision.HIGHEST
    left_re = jnp.einsum("kn,snm->skm", cosine, real_part, precision=high) - jnp.einsum(
        "kn,snm->skm", sine_table, imag_part, precision=high
    )
    left_im = jnp.einsum("kn,snm->skm", cosine, imag_part, precision=high) + jnp.einsum(
        "kn,snm->skm", sine_table, real_part, precision=high
    )
    out_re = jnp.einsum("skn,nm->skm", left_re, cosine, precision=high) - jnp.einsum(
        "skn,nm->skm", left_im, sine_table, precision=high
    )
    out_im = jnp.einsum("skn,nm->skm", left_re, sine_table, precision=high) + jnp.einsum(
        "skn,nm->skm", left_im, cosine, precision=high
    )
    return (out_re, out_im)


def body(sample, probe_field, patterns, positions, counts):
    tile_rows = sample.shape[1]
    tile_cols = sample.shape[2]
    pixels = probe_field.shape[1]
    capacity = patterns.shape[0]
    col_devices = lax.axis_size("col")
    row_at = lax.axis_index("row")
    col_at = lax.axis_index("col")
    own_count = counts[row_at * col_devices + col_at]
    live = (jnp.arange(capacity, dtype=jnp.int32) < own_count).astype(jnp.float32)
    visits = jnp.sum(counts).astype(jnp.float32)
    offset = jnp.stack([row_at * tile_rows, col_at * tile_cols])
    anchor = positions - offset[None, :]
    right = passed_along(sample[:, :, :pixels], "col", -1)
    widened = jnp.concatenate([sample, right], axis=2)
    lower = passed_along(widened[:, :pixels, :], "row", -1)
    extended = jnp.concatenate([widened, lower], axis=1)

    def window(corner):
        return lax.dynamic_slice(
            extended, (jnp.int32(0), corner[0], corner[1]), (2, pixels, pixels)
        )

    patches = jax.vmap(window)(anchor)
    patch_re = patches[:, 0]
    patch_im = patches[:, 1]
    probe_re = probe_field[0]
    probe_im = probe_field[1]
    cosine, sine_table = dft_tables(pixels)
    wave_re = probe_re * patch_re - probe_im * patch_im
    wave_im = probe_re * patch_im + probe_im * patch_re
    far_re, far_im = transform(wave_re, wave_im, cosine, sine_table)
    intensity = far_re * far_re + far_im * far_im
    resid = (intensity - patterns) * live[:, None, None]
    back_re, back_im = transform(resid * far_re, resid * far_im, cosine, -sine_table)
    updates = jnp.stack(
        [probe_re * back_re + probe_im * back_im, probe_re * back_im - probe_im * back_re], axis=1
    )
    probe_acc = jnp.stack(
        [
            jnp.sum(patch_re * back_re + patch_im * back_im, axis=0),
            jnp.sum(patch_re * back_im - patch_im * back_re, axis=0),
        ]
    )
    misfit = jnp.sum(resid * resid)
    measured = jnp.sum(jnp.sum(patterns, axis=(1, 2)) * live)

    def place(index, field):
        corner = anchor[index]
        start = (jnp.int32(0), corner[0], corner[1])
        current = lax.dynamic_slice(field, start, (2, pixels, pixels))
        return lax.dynamic_update_slice(field, current + updates[index], start)

    grad_field = lax.fori_loop(0, capacity, place, jnp.zeros_like(extended))
    came_down = passed_along(grad_field[:, tile_rows:, :], "row", 1)
    upper = grad_field[:, :tile_rows, :]
    upper = upper.at[:, :pixels, :].add(came_down)
    came_right = passed_along(upper[:, :, tile_cols:], "col", 1)
    summed = upper[:, :, :tile_cols]
    summed = summed.at[:, :, :pixels].add(came_right)
    measured_total = lax.psum(measured, ("row", "col"))
    mean_level = measured_total / (pixels * pixels * visits)
    coeff = 4.0 / (mean_level * mean_level)
    probe_grad, misfit_total = lax.psum((probe_acc * (coeff / visits), misfit), ("row", "col"))
    object_grad = summed * coeff
    mean_misfit = misfit_total / (mean_level * mean_level * pixels * pixels * visits)
    return (object_grad, probe_grad, mean_misfit)


def solution(mesh):
    in_specs = (
        P(None, "row", "col"),
        P(),
        P(("row", "col"), None, None),
        P(("row", "col"), None),
        P(),
    )
    out_specs = (P(None, "row", "col"), P(), P())
    return jax.shard_map(body, mesh=mesh, in_specs=in_specs, out_specs=out_specs, check_vma=False)
```

profile of v0, /device:TPU:1, one launch (start us, length us, event | category | flops | bytes accessed | tf_op | source)
XLA Modules:
  0.0 830.6 jit_solution(6514741300459013367)
XLA Ops:
  14.4 11.5 %collective-permute-done = f32[2,512,256]{2,1,0:T(8,128)S(1)} collective-permute-done((f32[2,512,256]{2,1,0:T(8,128)S(1)}, f32[2,512,256]{2,1,0:T(8,128)S(1)}, u32[]{:S(2)}, u32[]{:S(2)}) %collective-permute-start) | collective-permute-done | bytes 1048608 | tf_op jit(solution)/shard_map/ppermute | solution.py:12
  32.3 45.8 %collective-permute-done.1 = f32[2,256,1280]{2,1,0:T(8,128)} collective-permute-done((f32[2,256,1280]{2,1,0:T(8,128)S(1)}, f32[2,256,1280]{2,1,0:T(8,128)}, u32[]{:S(2)}, u32[]{:S(2)}) %collective-permute-start.1) | collective-permute-done | bytes 2621472 | tf_op jit(solution)/shard_map/ppermute | solution.py:12
  85.0 66.7 %while.17 = (s32[]{:T(128)}, f32[2,768,1280]{2,1,0:T(8,128)}, s32[16,3]{0,1:T(4,128)S(1)}, f32[16,2,256,256]{3,2,0,1:T(8,128)}, s32[]{:T(128)}) while((s32[]{:T(128)}, f32[2,768,1280]{2,1,0:T(8,128)}, s32[16,3]{0,1:T(4,128)S(1)}, f32[16,2,256,256]{3,2,0,1:T(8,128)}, s32[]{:T(128)}) %tuple.67), condition=%wide.while_cond.2, body=%wide.while_body.2.sunk | while | flops 2 | bytes 1050217 | solution.py:59
  151.7 11.7 %fusion.45 = f32[16,256,256]{2,1,0:T(8,128)S(1)} fusion(f32[16,2,256,256]{3,2,0,1:T(8,128)} %get-tuple-element.114, f32[256,256]{1,0:T(8,128)S(1)} %get-tuple-element.151, f32[256,256]{1,0:T(8,128)S(1)} %get-tuple-element.150), kind=kOutput, calls=%fused_computation.59 | convolution fusion | flops 3225354240 | bytes 13107200 | tf_op jit(solution)/shard_map/kn,snm->skm/dot_general | solution.py:25
  163.4 8.2 fusion.41
  171.6 8.8 %convolution_add_fusion.1 = f32[16,256,256]{2,1,0:T(8,128)S(1)} fusion(f32[16,256,256]{2,1,0:T(8,128)S(1)} %fusion.41, f32[16,2,256,256]{3,2,0,1:T(8,128)S(1)} %copy-done, f32[256,256]{1,0:T(8,128)S(1)} %get-tuple-element.151, f32[256,256]{1,0:T(8,128)S(1)} %get-tuple-element.150), kind=kOutput, calls=%fused_computation.47 | convolution fusion | flops 3226468352 | bytes 17301504 | tf_op jit(solution)/shard_map/kn,snm->skm/dot_general | solution.py:28
  180.4 8.0 fusion.10
  188.5 10.5 %fusion.8 = f32[16,256,256]{2,1,0:T(8,128)} fusion(f32[16,256,256]{2,1,0:T(8,128)S(1)} %convolution_add_fusion.1), kind=kOutput, calls=%fused_computation.14 | convolution fusion | flops 3222208512 | bytes 8388608 | tf_op jit(solution)/shard_map/skn,nm->skm/dot_general | solution.py:34
  199.0 8.3 convolution_subtract_fusion.1
  207.3 8.4 %fusion.22 = f32[16,256,256]{2,1,0:T(8,128)S(1)} fusion(f32[16,256,256]{2,1,0:T(8,128)S(1)} %fusion.10, f32[16,256,256]{2,1,0:T(8,128)S(1)} %convolution_subtract_fusion.1), kind=kOutput, calls=%fused_computation.41 | convolution fusion | flops 3223257088 | bytes 12582912 | tf_op jit(solution)/shard_map/skn,nm->skm/dot_general | solution.py:31
  215.7 13.6 %multiply_reduce_fusion = (f32[]{:T(128)}, f32[16,256,256]{2,1,0:T(8,128)S(1)}, f32[16]{0:T(128)S(1)}, f32[16,256,256]{2,1,0:T(8,128)S(1)}) fusion(f32[16]{0:T(128)S(1)} %compare_convert_fusion, f32[16,256,256]{2,1,0:T(8,128)} %param.13, f32[16,256,256]{2,1,0:T(8,128)S(1)} %fusion.22, f32[16,256,256]{2,1,0:T(8,128)} %fusion.8, ...), kind=kOutput, calls=%fused_computation.36 | convolution fusion | flops 3231711232 | bytes 25165956 | tf_op jit(solution)/shard_map/skn,nm->skm/dot_general | solution.py:34
  229.3 10.1 %fusion.38 = f32[16,256,256]{2,1,0:T(8,128)} fusion(f32[16,256,256]{2,1,0:T(8,128)S(1)} %get-tuple-element.140, f32[16,256,256]{2,1,0:T(8,128)S(1)} %fusion.22), kind=kOutput, calls=%fused_computation.54 | convolution fusion | flops 3223257088 | bytes 12582912 | tf_op jit(solution)/shard_map/kn,snm->skm/dot_general | solution.py:25
  239.3 8.1 fusion.34
  247.4 8.7 %convolution_add_fusion = f32[16,256,256]{2,1,0:T(8,128)S(1)} fusion(f32[16,256,256]{2,1,0:T(8,128)S(1)} %fusion.34, f32[16,256,256]{2,1,0:T(8,128)S(1)} %get-tuple-element.140, f32[16,256,256]{2,1,0:T(8,128)S(1)} %fusion.22), kind=kOutput, calls=%fused_computation.45 | convolution fusion | flops 3224436736 | bytes 16777216 | tf_op jit(solution)/shard_map/kn,snm->skm/dot_general | solution.py:28
  256.1 10.3 %fusion = f32[16,256,256]{2,1,0:T(8,128)} fusion(f32[16,256,256]{2,1,0:T(8,128)S(1)} %convolution_add_fusion), kind=kOutput, calls=%fused_computation.6 | convolution fusion | flops 3222208512 | bytes 8388608 | tf_op jit(solution)/shard_map/skn,nm->skm/dot_general | solution.py:34
  266.5 8.2 fusion.2
  274.7 11.2 %convolution_subtract_fusion = f32[16,256,256]{2,1,0:T(8,128)S(1)} fusion(f32[16,256,256]{2,1,0:T(8,128)} %fusion.38, f32[16,256,256]{2,1,0:T(8,128)S(1)} %get-tuple-element.140, f32[16,256,256]{2,1,0:T(8,128)S(1)} %get-tuple-element.154), kind=kOutput, calls=%fused_computation.46 | convolution fusion | flops 3224436736 | bytes 16777216 | tf_op jit(solution)/shard_map/kn,snm->skm/dot_general | solution.py:25
  285.9 8.2 fusion.31
  294.1 16.0 %fusion.19 = (f32[256,256]{1,0:T(8,128)}, f32[256,256]{1,0:T(8,128)}, f32[16,1,256,256]{3,2,0,1:T(8,128)}, f32[16,1,256,256]{3,2,0,1:T(8,128)}) fusion(f32[16,256,256]{2,1,0:T(8,128)S(1)} %fusion.31, f32[16,2,256,256]{3,2,0,1:T(8,128)S(1)} %copy-done, f32[256,256]{1,0:T(8,128)} %copy-done.6, f32[256,256]{1,0:T(8,128)} %copy-done.4, ...), kind=kOutput, calls=%fused_computation.29 | convolution fusion | flops 3237806080 | bytes 30408704 | tf_op jit(solution)/shard_map/skn,nm->skm/dot_general | solution.py:31
  321.3 201.7 %while.16 = (s32[]{:T(128)}, f32[2,768,1280]{2,1,0:T(8,128)}, s32[16,2]{0,1:T(2,128)S(1)}, f32[16,2,256,256]{3,2,0,1:T(8,128)}, s32[]{:T(128)}, /*index=5*/s32[]{:T(128)}, s32[]{:T(128)}, s32[]{:T(128)}) while((s32[]{:T(128)}, f32[2,768,1280]{2,1,0:T(8,128)}, s32[16,2]{0,1:T(2,128)S(1)}, f32[16,2,256,256]{3,2,0,1:T(8,128)}, s32[]{:T(128)}, ...), condition=%wide.region_1.2_spmd, body=%wide.region_0.0_spmd.sunk | while | flops 131080 | bytes 2621645 | solution.py:93
  531.2 43.0 %collective-permute-done.2 = f32[2,256,1280]{2,1,0:T(8,128)S(1)} collective-permute-done((f32[2,256,1280]{2,1,0:T(8,128)S(1)}, f32[2,256,1280]{2,1,0:T(8,128)S(1)}, u32[]{:S(2)}, u32[]{:S(2)}) %collective-permute-start.2) | collective-permute-done | bytes 2621472 | tf_op jit(solution)/shard_map/ppermute | solution.py:12
  578.7 23.8 %collective-permute-start.3 = (f32[2,512,256]{2,1,0:T(8,128)S(1)}, f32[2,512,256]{2,1,0:T(8,128)S(1)}, u32[]{:S(2)}, u32[]{:S(2)}) collective-permute-start(f32[2,512,256]{2,1,0:T(8,128)S(1)} %slice.134), channel_id=1, source_target_pairs={{0,1},{1,2},{2,3},{3,4},{4,5},{5,6},{6,7},{8,9},{9,10},{10,11},{11... | collective-permute-start | bytes 3145736 | tf_op jit(solution)/shard_map/ppermute | solution.py:12
  605.1 70.9 %all-reduce = (f32[]{:T(128)}, f32[]{:T(128)}) all-reduce(f32[]{:T(128)} %fusion.73, f32[]{:T(128)} %get-tuple-element.139), channel_id=1, replica_groups=mesh['row'=16,'col'=8] {'row','col'}, use_global_device_ids=true, to_apply=%region_4.5 | all-reduce | flops 2 | bytes 16 | tf_op jit(solution)/shard_map/psum | solution.py:100
  684.7 135.7 %all-reduce.3.cloned.1.call-done = f32[2,256,256]{2,1,0:T(8,128)} async-done(((f32[2,256,256]{2,1,0:T(8,128)}), f32[2,256,256]{2,1,0:T(8,128)}) %all-reduce.3.cloned.1.call-update) | async-done | bytes 524304 | tf_op jit(solution)/shard_map/psum | solution.py:103
  (169 shorter events, 261.3 us)
Async XLA Ops:
  7.2 813.2 %all-reduce.3.cloned.1.call-start = ((), (), s32[]{:S(2)}) async-start(), calls=%async_computation | async-start | bytes 1048576 | tf_op jit(solution)/shard_map/psum | solution.py:103
  8.5 17.4 %collective-permute-start = (f32[2,512,256]{2,1,0:T(8,128)S(1)}, f32[2,512,256]{2,1,0:T(8,128)S(1)}, u32[]{:S(2)}, u32[]{:S(2)}) collective-permute-start(f32[2,512,256]{2,1,0:T(8,128)S(1)} %slice.103), channel_id=1, source_target_pairs={{1,0},{2,1},{3,2},{4,3},{5,4},{6,5},{7,6},{9,8},{10,9},{11,10},{12... | collective-permute-start | bytes 3145736 | tf_op jit(solution)/shard_map/ppermute | solution.py:12
  14.4 15.3 %copy-start.11 = (s32[128]{0:T(128)S(1)}, s32[128]{0:T(128)}, u32[]{:S(2)}) copy-start(s32[128]{0:T(128)} %param.15) | copy-start | bytes 1540
  14.4 16.7 %copy-start.10 = (s32[16,2]{0,1:T(2,128)S(1)}, s32[16,2]{0,1:T(2,128)}, u32[]{:S(2)}) copy-start(s32[16,2]{0,1:T(2,128)} %param.14) | copy-start | bytes 388
  26.0 2.3 copy-start.1
  28.4 49.6 %collective-permute-start.1 = (f32[2,256,1280]{2,1,0:T(8,128)S(1)}, f32[2,256,1280]{2,1,0:T(8,128)}, u32[]{:S(2)}, u32[]{:S(2)}) collective-permute-start(f32[2,256,1280]{2,1,0:T(8,128)S(1)} %slice.131), channel_id=1, source_target_pairs={{8,0},{16,8},{24,16},{32,24},{40,32},{48,40},{56,48},{64,56},{72,6... | collective-permute-start | bytes 7864328 | tf_op jit(solution)/shard_map/ppermute | solution.py:12
  32.3 139.3 %copy-start.4 = (f32[256,256]{1,0:T(8,128)}, f32[256,256]{1,0:T(8,128)S(1)}, u32[]{:S(2)}) copy-start(f32[256,256]{1,0:T(8,128)S(1)} %get-tuple-element.150) | copy-start | bytes 786436
  32.3 139.3 %copy-start.6 = (f32[256,256]{1,0:T(8,128)}, f32[256,256]{1,0:T(8,128)S(1)}, u32[]{:S(2)}) copy-start(f32[256,256]{1,0:T(8,128)S(1)} %get-tuple-element.151) | copy-start | bytes 786436
  151.7 11.7 %copy-start = (f32[16,2,256,256]{3,2,0,1:T(8,128)S(1)}, f32[16,2,256,256]{3,2,0,1:T(8,128)}, u32[]{:S(2)}) copy-start(f32[16,2,256,256]{3,2,0,1:T(8,128)} %get-tuple-element.114) | copy-start | bytes 25165828
  188.4 10.6 %copy-start.5 = (f32[256,256]{1,0:T(8,128)S(1)}, f32[256,256]{1,0:T(8,128)}, u32[]{:S(2)}) copy-start(f32[256,256]{1,0:T(8,128)} %copy-done.4) | copy-start | bytes 786436
  188.4 10.6 %copy-start.7 = (f32[256,256]{1,0:T(8,128)S(1)}, f32[256,256]{1,0:T(8,128)}, u32[]{:S(2)}) copy-start(f32[256,256]{1,0:T(8,128)} %copy-done.6) | copy-start | bytes 786436
  274.7 11.2 %copy-start.3 = (f32[16,256,256]{2,1,0:T(8,128)S(1)}, f32[16,256,256]{2,1,0:T(8,128)}, u32[]{:S(2)}) copy-start(f32[16,256,256]{2,1,0:T(8,128)} %fusion) | copy-start | bytes 12582916
  524.9 49.3 %collective-permute-start.2 = (f32[2,256,1280]{2,1,0:T(8,128)S(1)}, f32[2,256,1280]{2,1,0:T(8,128)S(1)}, u32[]{:S(2)}, u32[]{:S(2)}) collective-permute-start(f32[2,256,1280]{2,1,0:T(8,128)S(1)} %slice.112), channel_id=1, source_target_pairs={{0,8},{8,16},{16,24},{24,32},{32,40},{40,48},{48,56},{56,64},{64,7... | collective-permute-start | bytes 7864328 | tf_op jit(solution)/shard_map/ppermute | solution.py:12
  531.2 145.5 %copy-start.8 = (f32[256,256]{1,0:T(8,128)S(1)}, f32[256,256]{1,0:T(8,128)}, u32[]{:S(2)}) copy-start(f32[256,256]{1,0:T(8,128)} %get-tuple-element.119) | copy-start | bytes 786436
  531.2 145.5 %copy-start.9 = (f32[256,256]{1,0:T(8,128)S(1)}, f32[256,256]{1,0:T(8,128)}, u32[]{:S(2)}) copy-start(f32[256,256]{1,0:T(8,128)} %get-tuple-element.120) | copy-start | bytes 786436
  576.3 2.3 copy-start.2
  578.7 102.1 %collective-permute-start.3 = (f32[2,512,256]{2,1,0:T(8,128)S(1)}, f32[2,512,256]{2,1,0:T(8,128)S(1)}, u32[]{:S(2)}, u32[]{:S(2)}) collective-permute-start(f32[2,512,256]{2,1,0:T(8,128)S(1)} %slice.134), channel_id=1, source_target_pairs={{0,1},{1,2},{2,3},{3,4},{4,5},{5,6},{6,7},{8,9},{9,10},{10,11},{11... | collective-permute-start | bytes 3145736 | tf_op jit(solution)/shard_map/ppermute | solution.py:12
Sparse Core Ops, SparseCore 0:
  677.7 142.5 all-reduce.2
where the time goes:
time: 842 us; the launch traced here: 831 us
  waiting for transfers between devices  236 us (28%)
  local copies, waits for them, and re-layouts  205 us (24%)
  matrix products  158 us (19%)
  blocking collectives  70.9 us (8%)
  loops' own time  62.3 us (7%)
  other arithmetic  48.4 us (6%)
  starting transfers between devices  31.9 us (4%)
  between operations  18 us (2%)
    psum x1, waiting for transfers between devices, body(): lax.psum((probe_acc * (coeff / visits), misfit), ('row', 'col'))  136 us
    dynamic_update_slice x16, local copies, waits for them, and re-layouts, place(): return lax.dynamic_update_slice(field, current + updates[index], start)  105 us
    ppermute x4, waiting for transfers between devices, passed_along(): lax.ppermute(value, axis, [(source, source + steps) for source in range(f...  100 us
    psum x1, blocking collectives, body(): measured_total = lax.psum(measured, ('row', 'col'))  70.9 us
    gather x48, local copies, waits for them, and re-layouts  66.7 us
    another operation x1, loops' own time, body(): grad_field = lax.fori_loop(0, capacity, place, jnp.zeros_like(extended))  62.2 us
    ppermute x4, starting transfers between devices, passed_along(): lax.ppermute(value, axis, [(source, source + steps) for source in range(f...  31.9 us
    add x16, other arithmetic, place(): return lax.dynamic_update_slice(field, current + updates[index], start)  24.5 us
  transfers between devices with their start and end apart: 5, of which 4 were waited for; matrix products, arithmetic and copies ran while one was open for 2% of the time, Pallas kernels for 0%

commit v1 on v0

v1 whole, which is shorter than its diff:
```python
import math

import jax
import jax.numpy as jnp
import numpy as np
from jax import lax
from jax.experimental import pallas as pl
from jax.experimental.pallas import tpu as pltpu
from jax.sharding import PartitionSpec as P

F32 = jnp.float32
BF16 = jnp.bfloat16
M = 256
H = 128
CAP = 16


def split_table(table):
    high = table.astype(np.float32).astype(jnp.bfloat16)
    low = (table - high.astype(np.float64)).astype(np.float32).astype(jnp.bfloat16)
    return high, low


def dft_tables():
    n = np.arange(H)[:, None]
    m = np.arange(H)[None, :]
    right, left = [], []
    for sign in (-1.0, 1.0):
        for odd in (0, 1):
            if sign < 0:
                angle = 2 * math.pi * (n * (2 * m + odd) % M) / M
            else:
                angle = 2 * math.pi * ((2 * n + odd) * m % M) / M
            re, im = np.cos(angle) / 16.0, sign * np.sin(angle) / 16.0
            high, low = split_table(np.block([[re, im], [-im, re]]))
            right.append(np.concatenate([high, high, low], axis=0))
            re, im = re.T, im.T
            high, low = split_table(np.block([[re, -im], [im, re]]))
            left.append(np.concatenate([high, low, high], axis=1))
    order = np.zeros((M, M), np.float32)
    k = np.arange(M)
    order[k, k // 2 + H * (k % 2)] = 1.0
    order = np.concatenate([order, order], axis=0).astype(jnp.bfloat16)
    return np.stack(right), np.stack(left), order


def split(value):
    high = value.astype(BF16)
    return high, (value - high.astype(F32)).astype(BF16)


def dot(a, b):
    return jnp.dot(a, b, preferred_element_type=F32)


def right_dot(value, table):
    high, low = split(value)
    return dot(jnp.concatenate([high, low, high], axis=1), table)


def left_dot(table, value):
    high, low = split(value)
    return dot(table, jnp.concatenate([high, high, low], axis=0))


def lanes(a, b):
    return jnp.concatenate([a, b], axis=1)


def rows(a, b):
    return jnp.concatenate([a, b], axis=0)


def one_window(top, j0, dc, ext, acc, pat, probe, right, left, order, pacc, mis, rolled, patch):
    mask = lax.broadcasted_iota(jnp.int32, (M, H), 1) >= dc

    def turned(a, b, shift, keep):
        a, b = pltpu.roll(a, shift, 1), pltpu.roll(b, shift, 1)
        return jnp.where(keep, a, b), jnp.where(keep, b, a)

    for p in range(2):
        a, b = turned(probe[p, :, :H], probe[p, :, H:], dc, mask)
        rolled[p, :, :H] = a
        rolled[p, :, H:] = b
        at = pl.ds(top, M)
        patch[p, :, :H] = jnp.where(mask, ext[p, j0, at, :], ext[p, j0 + 2, at, :])
        patch[p, :, H:] = ext[p, j0 + 1, at, :]
    wave_re = rolled[0] * patch[0] - rolled[1] * patch[1]
    wave_im = rolled[0] * patch[1] + rolled[1] * patch[0]
    sum_re, sum_im = wave_re[:, :H] + wave_re[:, H:], wave_im[:, :H] + wave_im[:, H:]
    dif_re, dif_im = wave_re[:, :H] - wave_re[:, H:], wave_im[:, :H] - wave_im[:, H:]
    even = right_dot(lanes(sum_re, sum_im), right[0])
    odd = right_dot(lanes(dif_re, dif_im), right[1])
    even_s, even_d = even[:H] + even[H:], even[:H] - even[H:]
    odd_s, odd_d = odd[:H] + odd[H:], odd[:H] - odd[H:]
    back = []
    for parity, (e, o) in enumerate(((even_s, odd_s), (even_d, odd_d))):
        far = left_dot(left[parity], rows(lanes(e[:, :H], o[:, :H]), lanes(e[:, H:], o[:, H:])))
        far_re, far_im = far[:H], far[H:]
        every = pl.ds(parity, H, 2)
        high, low = split(lanes(pat[0, every, :], pat[1, every, :]))
        measured = dot(lanes(high, low), order[...])
        resid = far_re * far_re + far_im * far_im - measured
        mis[...] += jnp.sum((resid * resid).reshape(16, 8, M), axis=0)
        back.append(left_dot(left[2 + parity], rows(resid * far_re, resid * far_im)))
    half_s, half_d = back[0] + back[1], back[0] - back[1]
    mid_re = rows(half_s[:H], half_d[:H])
    mid_im = rows(half_s[H:], half_d[H:])
    even = right_dot(lanes(mid_re[:, :H], mid_im[:, :H]), right[2])
    odd = right_dot(lanes(mid_re[:, H:], mid_im[:, H:]), right[3])
    first, second = even + odd, even - odd
    back_re = lanes(first[:, :H], second[:, :H])
    back_im = lanes(first[:, H:], second[:, H:])
    unmask = lax.broadcasted_iota(jnp.int32, (M, H), 1) < H - dc
    undo = lax.rem(H - dc, H)
    for p in range(2):
        if p == 0:
            update = rolled[0] * back_re + rolled[1] * back_im
            grad = patch[0] * back_re + patch[1] * back_im
        else:
            update = rolled[0] * back_im - rolled[1] * back_re
            grad = patch[0] * back_im - patch[1] * back_re
        acc[p, j0, at, :] += jnp.where(mask, update[:, :H], 0.0)
        acc[p, j0 + 2, at, :] += jnp.where(mask, 0.0, update[:, :H])
        acc[p, j0 + 1, at, :] += update[:, H:]
        a, b = turned(grad[:, :H], grad[:, H:], undo, unmask)
        pacc[p, :, :H] += a
        pacc[p, :, H:] += b


def windows_kernel(plan, *refs):
    names = plan["names"]
    at = dict(zip(names, refs))
    ext, acc = at["ext"], at["acc"]
    pos, count = at["pos"], at["count"]
    n_pieces, n_carry = len(plan["pieces"]), len(plan["carry"])
    nblk = plan["nblk"]

    def here(s):
        o, c = pos[s, 0], pos[s, 1]
        return (s < count[0]) & plan["cond"](o, c)

    copies = []

    def begin(src, dst):
        copy = pltpu.make_async_copy(src, dst, at["sems"].at[len(copies)])
        copy.start()
        copies.append(copy)

    def pattern_copies(s):
        return [
            pltpu.make_async_copy(at["patterns"].at[s, :, pl.ds(k * H, H)], at["pat"].at[s, k], at["pat_sems"].at[s, k])
            for k in range(2)
        ]

    for ref, (r0, c0, nr, nc, dr, db) in zip(at["pieces"], plan["pieces"]):
        for k in range(nc // H):
            begin(ref.at[:, pl.ds(r0, nr), pl.ds(c0 + k * H, H)], ext.at[:, db + k, pl.ds(dr, nr), :])
    for ref, (r0, nr, nc, dr, db) in zip(at["carry"], plan["carry"]):
        for k in range(nc // H):
            begin(ref.at[:, pl.ds(r0, nr), pl.ds(k * H, H)], acc.at[:, db + k, pl.ds(dr, nr), :])

    @pl.loop(0, CAP)
    def _(s):
        @pl.when(here(s))
        def _():
            for copy in pattern_copies(s):
                copy.start()

    for b in range(nblk):
        kept = plan["carried"].get(b, 0)
        if kept:
            acc[:, b, :-kept] = jnp.zeros_like(acc[:, b, :-kept])
        else:
            acc[:, b] = jnp.zeros_like(acc[:, b])
    at["pacc"][...] = at["pacc_in"][...]
    at["mis"][...] = at["mis_in"][...]
    for copy in copies:
        copy.wait()

    @pl.loop(0, CAP)
    def _(s):
        @pl.when(here(s))
        def _():
            for copy in pattern_copies(s):
                copy.wait()
            o, c = pos[s, 0] - plan["row0"], pos[s, 1] - plan["col0"]
            one_window(o, c // H, c % H, ext, acc, at["pat"].at[s], at["probe"], at["right"], at["left"],
                       at["order"], at["pacc"], at["mis"], at["rolled"], at["patch"])

    ends = []
    for ref, (r0, nr, nc, db) in zip(at["outs"], plan["outs"]):
        for k in range(nc // H):
            copy = pltpu.make_async_copy(acc.at[:, db + k, pl.ds(r0, nr), :], ref.at[:, :, pl.ds(k * H, H)],
                                         at["sems"].at[len(copies) + len(ends)])
            copy.start()
            ends.append(copy)
    for copy in ends:
        copy.wait()


def windows(name, pos, count, patterns, probe, tables, pacc, mis, pieces, carry, outs, nblk, nrows, row0, col0, cond, cost=8):
    right, left, order = tables
    vm = pl.BlockSpec(memory_space=pltpu.VMEM)
    sm = pl.BlockSpec(memory_space=pltpu.SMEM)
    hbm = pl.BlockSpec(memory_space=pl.ANY)
    plan = dict(
        pieces=[p[1:] for p in pieces], carry=[c[1:] for c in carry], outs=outs, nblk=nblk, row0=row0, col0=col0, cond=cond,
        carried={c[5] + k: c[2] for c in carry for k in range(c[3] // H)},
    )
    n_p, n_c, n_o = len(pieces), len(carry), len(outs)
    n_sems = sum(p[4] // H for p in pieces) + sum(c[3] // H for c in carry) + sum(o[2] // H for o in outs)

    def kernel(*refs):
        it = iter(refs)
        take = lambda n: [next(it) for _ in range(n)]
        at = {}
        at["pos"], at["count"], at["patterns"], at["probe"], at["right"], at["left"], at["order"], at["pacc_in"], at["mis_in"] = take(9)
        at["pieces"], at["carry"], at["outs"] = take(n_p), take(n_c), take(n_o)
        at["pacc"], at["mis"] = take(2)
        at["ext"], at["acc"], at["pat"], at["rolled"], at["patch"], at["sems"], at["pat_sems"] = take(7)
        windows_kernel(dict(plan, names=list(at)), *at.values())

    out = pl.pallas_call(
        kernel,
        name=name,
        out_shape=[jax.ShapeDtypeStruct((2, nr, nc), F32) for _, nr, nc, _ in outs]
        + [jax.ShapeDtypeStruct((2, M, M), F32), jax.ShapeDtypeStruct((8, M), F32)],
        in_specs=[sm, sm, hbm, vm, vm, vm, vm, vm, vm] + [hbm] * (n_p + n_c),
        out_specs=[hbm] * n_o + [vm, vm],
        scratch_shapes=[
            pltpu.VMEM((2, nblk, nrows, H), F32),
            pltpu.VMEM((2, nblk, nrows, H), F32),
            pltpu.VMEM((CAP, 2, M, H), F32),
            pltpu.VMEM((2, M, M), F32),
            pltpu.VMEM((2, M, M), F32),
            pltpu.SemaphoreType.DMA((n_sems,)),
            pltpu.SemaphoreType.DMA((CAP, 2)),
        ],
        compiler_params=pltpu.CompilerParams(vmem_limit_bytes=48 << 20),
        cost_estimate=pl.CostEstimate(flops=cost * 26 * 2 * M**3, bytes_accessed=8 << 20, transcendentals=0),
    )(pos, count, patterns, probe, right, left, order, pacc, mis, *[p[0] for p in pieces], *[c[0] for c in carry])
    return out[:n_o], out[n_o], out[n_o + 1]


MESH = pl.DeviceIdType.MESH
NROW, NCOL = 16, 8


def total_kernel(pacc, scal, out, tot, mine1, got1, mine2, got2, part, wide, s1, r1, s2, r2, s3, r3, s4, r4):
    row, col = lax.axis_index("row"), lax.axis_index("col")

    def col_peer(k):
        return row, lax.rem(col + k, NCOL)

    def row_peer(k):
        return lax.rem(row + k, NROW), col

    barrier = pltpu.get_barrier_semaphore()
    for k in range(1, NCOL):
        pl.semaphore_signal(barrier, inc=1, device_id=col_peer(k), device_id_type=MESH)
    for k in range(1, NROW):
        pl.semaphore_signal(barrier, inc=1, device_id=row_peer(k), device_id_type=MESH)
    for p in range(2):
        for b in range(2):
            for h in range(2):
                piece = 4 * p + 2 * b + h
                mine1[piece, :H] = pacc[p, h * H : (h + 1) * H, b * H : (b + 1) * H]
                mine1[piece, H:] = scal[...]
    pl.semaphore_wait(barrier, NCOL + NROW - 2)

    def send(src, dst, ss, rs, peer):
        copy = pltpu.make_async_remote_copy(src, dst, ss, rs, device_id=peer, device_id_type=MESH)
        copy.start()
        return copy

    copies = [
        send(mine1.at[lax.rem(col + k, NCOL)], got1.at[k - 1], s1.at[k - 1], r1.at[k - 1], col_peer(k))
        for k in range(1, NCOL)
    ]
    for copy in copies:
        copy.wait()
    total = mine1[col]
    for k in range(NCOL - 1):
        total = total + got1[k]
    for k in range(NROW):
        mine2[k, :8] = total[8 * k : 8 * k + 8]
        mine2[k, 8:] = total[H:]
    copies = [
        send(mine2.at[lax.rem(row + k, NROW)], got2.at[k - 1], s2.at[k - 1], r2.at[k - 1], row_peer(k))
        for k in range(1, NROW)
    ]
    for copy in copies:
        copy.wait()
    total = mine2[row]
    for k in range(NROW - 1):
        total = total + got2[k]
    tot[...] = total[8:]
    part[row] = total[:8]
    copies = [send(part.at[row], part.at[row], s3.at[k - 1], r3.at[k - 1], row_peer(k)) for k in range(1, NROW)]
    for copy in copies:
        copy.wait()
    copies = [send(part, wide.at[col], s4.at[k - 1], r4.at[k - 1], col_peer(k)) for k in range(1, NCOL)]
    wide[col] = part[...]
    for copy in copies:
        copy.wait()
    for p in range(2):
        for b in range(2):
            for h in range(2):
                out[p, h * H : (h + 1) * H, b * H : (b + 1) * H] = wide[4 * p + 2 * b + h].reshape(H, H)


def total_over_devices(pacc, scal):
    vm = pl.BlockSpec(memory_space=pltpu.VMEM)
    sems = [pltpu.SemaphoreType.DMA((n,)) for n in (NCOL - 1, NCOL - 1, NROW - 1, NROW - 1, NROW - 1, NROW - 1, NCOL - 1, NCOL - 1)]
    return pl.pallas_call(
        total_kernel,
        name="total_over_devices",
        out_shape=[jax.ShapeDtypeStruct((2, M, M), F32), jax.ShapeDtypeStruct((8, H), F32)],
        in_specs=[vm, vm],
        out_specs=[vm, vm],
        scratch_shapes=[
            pltpu.VMEM((NCOL, H + 8, H), F32),
            pltpu.VMEM((NCOL - 1, H + 8, H), F32),
            pltpu.VMEM((NROW, 16, H), F32),
            pltpu.VMEM((NROW - 1, 16, H), F32),
            pltpu.VMEM((NROW, 8, H), F32),
            pltpu.VMEM((NCOL, NROW, 8, H), F32),
        ]
        + sems,
        compiler_params=pltpu.CompilerParams(collective_id=0, has_side_effects=True),
        cost_estimate=pl.CostEstimate(flops=12 * 10**9, bytes_accessed=8 << 20, transcendentals=0),
    )(pacc, scal)


def passed_along(value, axis, steps):
    count = lax.axis_size(axis)
    first, last = (max(0, -steps), min(count, count - steps))
    return lax.ppermute(value, axis, [(source, source + steps) for source in range(first, last)])


def body(sample, probe, patterns, positions, counts):
    tile_rows, tile_cols = sample.shape[1:]
    row_at, col_at = lax.axis_index("row"), lax.axis_index("col")
    own = counts[row_at * NCOL + col_at]
    pos = positions - jnp.stack([row_at * tile_rows, col_at * tile_cols])[None, :]
    count = own.reshape(1)
    visits = jnp.sum(counts).astype(F32)
    low = [None] * 4
    low[0] = passed_along(sample[:, :M, :M], "row", -1)
    right = passed_along(sample[:, :, :M], "col", -1)
    for k in (3, 2, 1):
        low[k] = passed_along(sample[:, :M, k * M : (k + 1) * M], "row", -1)
    corner = passed_along(low[0], "col", -1)
    tables = tuple(jnp.asarray(t) for t in dft_tables())
    live = (jnp.arange(CAP, dtype=jnp.int32) < own).astype(F32)
    measured = jnp.sum(jnp.sum(patterns, axis=(1, 2)) * live)

    args = (pos, count, patterns, probe, tables)
    (inner,), pacc, mis = windows(
        "windows_inside", *args, jnp.zeros((2, M, M), F32), jnp.zeros((8, M), F32),
        [(sample, 0, 0, 512, 1024, 0, 0)], [], [(0, 512, 1024, 0)],
        8, 512, 0, 0, lambda o, c: (o <= M) & (c < 768), cost=16,
    )
    (own4, edge, part3), pacc, mis = windows(
        "windows_right", *args, pacc, mis,
        [(sample, 0, 768, 512, 256, 0, 0), (right, 0, 0, 512, 256, 0, 2), (low[3], 0, 0, M, M, 512, 0), (corner, 0, 0, M, M, 512, 2)],
        [], [(0, 512, M, 0), (0, 768, M, 2), (512, M, M, 0)],
        4, 768, 0, 768, lambda o, c: c >= 768, cost=6,
    )
    came_right = passed_along(edge, "col", 1)
    (own3, halo3, part2), pacc, mis = windows(
        "windows_third", *args, pacc, mis,
        [(sample, 256, 512, 256, 512, 0, 0), (low[2], 0, 0, M, M, 256, 0), (low[3], 0, 0, M, M, 256, 2)],
        [(part3, 0, M, M, 256, 2)], [(0, M, 512, 0), (256, M, M, 2), (256, M, M, 0)],
        4, 512, 256, 512, lambda o, c: (o > M) & (c >= 512) & (c < 768), cost=4,
    )
    down3 = passed_along(halo3, "row", 1)
    (own12, halo12), pacc, mis = windows(
        "windows_left", *args, pacc, mis,
        [(sample, 256, 0, 256, 768, 0, 0), (low[0], 0, 0, M, M, 256, 0), (low[1], 0, 0, M, M, 256, 2), (low[2], 0, 0, M, M, 256, 4)],
        [(part2, 0, M, M, 256, 4), (came_right, 512, M, M, 256, 0)], [(0, M, 768, 0), (256, M, 768, 0)],
        6, 512, 256, 0, lambda o, c: (o > M) & (c < 512), cost=6,
    )
    down12 = passed_along(halo12, "row", 1)
    lane = lax.broadcasted_iota(jnp.int32, (8, H), 1)
    first = lax.broadcasted_iota(jnp.int32, (8, H), 0) == 0
    scal = jnp.where(first & (lane == 0), measured, jnp.where(first & (lane == 1), jnp.sum(mis), 0.0))
    probe_sum, totals = total_over_devices(pacc, scal)
    mean_level = totals[0, 0] / (M * M * visits)
    coeff = 4.0 / (mean_level * mean_level)
    summed = inner
    summed = summed.at[:, :, 768:].add(own4)
    summed = summed.at[:, M:, 512:].add(own3)
    summed = summed.at[:, M:, :768].add(own12)
    summed = summed.at[:, :, :M].add(came_right[:, :512])
    summed = summed.at[:, :M, 768:].add(down3)
    summed = summed.at[:, :M, :768].add(down12)
    mean_misfit = totals[0, 1] / (mean_level * mean_level * M * M * visits)
    return summed * coeff, probe_sum * (coeff / visits), mean_misfit


def solution(mesh):
    in_specs = (
        P(None, "row", "col"),
        P(),
        P(("row", "col"), None, None),
        P(("row", "col"), None),
        P(),
    )
    out_specs = (P(None, "row", "col"), P(), P())
    return jax.shard_map(body, mesh=mesh, in_specs=in_specs, out_specs=out_specs, check_vma=False)
```

time: 842 us -> 192 us (0.23); the launches traced: 831 us -> 191 us
  waiting for transfers between devices: 236 us -> 4.03 us
  local copies, waits for them, and re-layouts: 205 us -> 19.4 us
  matrix products: 158 us -> 0 us
  Pallas kernels: 0 us -> 85 us
  blocking collectives: 70.9 us -> 0 us
  loops' own time: 62.3 us -> 0 us
  other arithmetic: 48.4 us -> 26.1 us
  starting transfers between devices: 31.9 us -> 52.3 us
  between operations: 18 us -> 4.17 us
    dot_general x16 -> x0, matrix products: 158 us -> none  [the longest x2 24.4 us: transform(): jnp.einsum('skn,nm->skm', left_re, cosine, precision=high)]
    psum x1 -> x0, waiting for transfers between devices: 136 us -> none  [body(): lax.psum((probe_acc * (coeff / visits), misfit), ('row', 'col'))]
    dynamic_update_slice x16 -> x0, local copies, waits for them, and re-layouts: 105 us -> none  [place(): return lax.dynamic_update_slice(field, current + updates[index], start)]
    ppermute x4 -> x9, waiting for transfers between devices: 100 us -> 4.03 us  [passed_along(): lax.ppermute(value, axis, [(source, source + steps) for source in range(f...]
    pallas_call x0 -> x5, Pallas kernels: none -> 85 us  [the longest x1 44.5 us: total_over_devices(): pl.pallas_call(total_kernel, name='total_over_devices', out_shape=[jax.Sh...]
    psum x1 -> x0, blocking collectives: 70.9 us -> none  [body(): measured_total = lax.psum(measured, ('row', 'col'))]
    gather x48 -> x0, local copies, waits for them, and re-layouts: 66.7 us -> none
    another operation x2 -> x0, loops' own time: 62.3 us -> none  [the longest x1 62.2 us: body(): grad_field = lax.fori_loop(0, capacity, place, jnp.zeros_like(extended))]
  transfers between devices with their start and end apart: 5 -> 9, of which waited for: 4 -> 1; matrix products, arithmetic and copies ran while one was open for 2% -> 15% of each run, Pallas kernels for 0% -> 44%
where the time goes in v1:
time: 192 us; the launch traced here: 191 us
  Pallas kernels  85 us (44%)
  starting transfers between devices  52.3 us (27%)
  other arithmetic  26.1 us (14%)
  local copies, waits for them, and re-layouts  19.4 us (10%)
  between operations  4.17 us (2%)
  waiting for transfers between devices  4.03 us (2%)
    ppermute x9, starting transfers between devices, passed_along(): lax.ppermute(value, axis, [(source, source + steps) for source in range(f...  52.3 us
    pallas_call x1, Pallas kernels, total_over_devices(): pl.pallas_call(total_kernel, name='total_over_devices', out_shape=[jax.Sh...  44.5 us
    pallas_call x4, Pallas kernels, windows(): pl.pallas_call(kernel, name=name, out_shape=[jax.ShapeDtypeStruct((2, nr,...  40.5 us
    scatter-add x1, local copies, waits for them, and re-layouts, body(): summed = summed.at[:, :M, 768:].add(down3)  6.51 us
    mul x2, other arithmetic, body(): return (summed * coeff, probe_sum * (coeff / visits), mean_misfit)  5.86 us
    unnamed x33, local copies, waits for them, and re-layouts  4.99 us
    another operation x3, other arithmetic  4.04 us
    ppermute x9, waiting for transfers between devices, passed_along(): lax.ppermute(value, axis, [(source, source + steps) for source in range(f...  4.03 us
  transfers between devices with their start and end apart: 9, of which 1 were waited for; matrix products, arithmetic and copies ran while one was open for 15% of the time, Pallas kernels for 44%

profile of v1, /device:TPU:1, one launch (start us, length us, event | category | flops | bytes accessed | tf_op | source)
XLA Modules:
  0.0 191.0 jit_solution(6145770062105433018)
XLA Ops:
  0.7 3.1 %fusion.5 = (f32[2,256,256]{2,1,0:T(8,128)}, f32[2,256,256]{2,1,0:T(8,128)}, f32[2,256,256]{2,1,0:T(8,128)}, f32[2,256,256]{2,1,0:T(8,128)}) fusion(f32[2,512,1024]{2,1,0:T(8,128)} %refs_9_.7), kind=kLoop, calls=%fused_computation.22 | loop fusion | bytes 4194304 | tf_op jit(solution)/shard_map/slice | solution.py:353
  5.1 2.3 %slice.192 = f32[2,512,256]{2,1,0:T(8,128)} slice(f32[2,512,1024]{2,1,0:T(8,128)} %refs_9_.7), slice={[0:2], [0:512], [0:256]} | slice | bytes 2097152 | tf_op jit(solution)/shard_map/slice | solution.py:351
  7.3 3.3 %collective-permute-start = (f32[2,512,256]{2,1,0:T(8,128)}, f32[2,512,256]{2,1,0:T(8,128)}, u32[]{:S(2)}, u32[]{:S(2)}) collective-permute-start(f32[2,512,256]{2,1,0:T(8,128)} %slice.192), channel_id=1, source_target_pairs={{1,0},{2,1},{3,2},{4,3},{5,4},{6,5},{7,6},{9,8},{10,9},{11,10},{12... | collective-permute-start | bytes 3145736 | tf_op jit(solution)/shard_map/ppermute | solution.py:339
  10.7 1.3 collective-permute-start.1
  12.0 1.3 collective-permute-start.4
  15.3 4.0 %collective-permute-done.2.refs_10_ = f32[2,256,256]{2,1,0:T(8,128)} collective-permute-done((f32[2,256,256]{2,1,0:T(8,128)}, f32[2,256,256]{2,1,0:T(8,128)}, u32[]{:S(2)}, u32[]{:S(2)}) %collective-permute-start.2) | collective-permute-done | bytes 524320 | tf_op jit(solution)/shard_map/ppermute | solution.py:339
  19.3 4.8 %collective-permute-start.3 = (f32[2,256,256]{2,1,0:T(8,128)}, f32[2,256,256]{2,1,0:T(8,128)}, u32[]{:S(2)}, u32[]{:S(2)}) collective-permute-start(f32[2,256,256]{2,1,0:T(8,128)} %collective-permute-done.2.refs_10_), channel_id=1, source_target_pairs={{1,0},{2,1},{3,2},{4,3},{5,4},{6,5},{7,6},{9,8},{10,9},{11,10},{12... | collective-permute-start | bytes 1572872 | tf_op jit(solution)/shard_map/ppermute | solution.py:339
  25.2 13.1 %windows_inside.1 = (f32[2,512,1024]{2,1,0:T(8,128)}, f32[2,256,256]{2,1,0:T(8,128)S(1)}, f32[8,256]{1,0:T(8,128)S(1)}) custom-call(s32[16,2]{1,0:T(8,128)S(1)} %broadcast_subtract_fusion.refs_0_, s32[1]{0:T(128)} %dynamic_slice.3.refs_1_, f32[16,256,256]{2,1,0:T(8,128)} %refs_2_.7, f32[2,256,256]{2,1,0:T(8,128)S(1)} %copy-done.2, ...), custom_call_target="tpu_custom_call" | custom-call | flops 13958643712 | bytes 8388608 | tf_op jit(solution)/shard_map/windows_inside/pallas_call | solution.py:224
  39.1 2.6 %reduce_sum.36 = f32[16]{0:T(128)S(1)} reduce(f32[16,256,256]{2,1,0:T(8,128)} %refs_2_.7, f32[]{:T(128)} %constant.203.clone.1), dimensions={1,2}, to_apply=%region_1.0 | reduce | flops 1048560 | bytes 4194372 | tf_op jit(solution)/shard_map/reduce_sum | solution.py:357
  44.1 8.6 %windows_right.1 = (f32[2,512,256]{2,1,0:T(8,128)S(1)}, f32[2,768,256]{2,1,0:T(8,128)}, f32[2,256,256]{2,1,0:T(8,128)S(1)}, f32[2,256,256]{2,1,0:T(8,128)S(1)}, f32[8,256]{1,0:T(8,128)S(1)}) custom-call(s32[16,2]{1,0:T(8,128)S(1)} %broadcast_subtract_fusion.refs_0_, s32[1]{0:T(128)} %dynamic_slice.3.refs_1_, f32[16,256,256]{2,1,0:T(8,128)} %refs_2_.7, ...), custom_call_target="tpu_custom_call" | custom-call | flops 5234491392 | bytes 8388608 | tf_op jit(solution)/shard_map/windows_right/pallas_call | solution.py:224
  52.7 12.1 %collective-permute-start.6 = (f32[2,768,256]{2,1,0:T(8,128)}, f32[2,768,256]{2,1,0:T(8,128)S(1)}, u32[]{:S(2)}, u32[]{:S(2)}) collective-permute-start(f32[2,768,256]{2,1,0:T(8,128)} %get-tuple-element.105), channel_id=1, source_target_pairs={{0,1},{1,2},{2,3},{3,4},{4,5},{5,6},{6,7},{8,9},{9,10},{10,11},{11... | collective-permute-start | bytes 4718600 | tf_op jit(solution)/shard_map/ppermute | solution.py:339
  67.4 7.6 %windows_third.1 = (f32[2,256,512]{2,1,0:T(8,128)S(1)}, f32[2,256,256]{2,1,0:T(8,128)S(1)}, f32[2,256,256]{2,1,0:T(8,128)S(1)}, f32[2,256,256]{2,1,0:T(8,128)S(1)}, f32[8,256]{1,0:T(8,128)S(1)}) custom-call(s32[16,2]{1,0:T(8,128)S(1)} %broadcast_subtract_fusion.refs_0_, s32[1]{0:T(128)} %dynamic_slice.3.refs_1_, f32[16,256,256]{2,1,0:T(8,128)} %refs_2_.7, ...), custom_call_target="tpu_custom_call" | custom-call | flops 3489660928 | bytes 8388608 | tf_op jit(solution)/shard_map/windows_third/pallas_call | solution.py:224
  75.0 10.6 %collective-permute-start.7 = (f32[2,256,256]{2,1,0:T(8,128)S(1)}, f32[2,256,256]{2,1,0:T(8,128)}, u32[]{:S(2)}, u32[]{:S(2)}) collective-permute-start(f32[2,256,256]{2,1,0:T(8,128)S(1)} %get-tuple-element.107), channel_id=1, source_target_pairs={{0,8},{8,16},{16,24},{24,32},{32,40},{40,48},{48,56},{56,64},{64,7... | collective-permute-start | bytes 1572872 | tf_op jit(solution)/shard_map/ppermute | solution.py:339
  87.4 11.2 %windows_left.1 = (f32[2,256,768]{2,1,0:T(8,128)S(1)}, f32[2,256,768]{2,1,0:T(8,128)}, f32[2,256,256]{2,1,0:T(8,128)S(1)}, f32[8,256]{1,0:T(8,128)S(1)}) custom-call(s32[16,2]{1,0:T(8,128)S(1)} %broadcast_subtract_fusion.refs_0_, s32[1]{0:T(128)} %dynamic_slice.3.refs_1_, f32[16,256,256]{2,1,0:T(8,128)} %refs_2_.7, f32[2,256,256]{2,1,0:T(8,128)S(1)} %copy-done.3, ...), custom_call_target="tpu_custom_call" | custom-call | flops 5234491392 | bytes 8388608 | tf_op jit(solution)/shard_map/windows_left/pallas_call | solution.py:224
  99.4 16.4 %collective-permute-start.8 = (f32[2,256,768]{2,1,0:T(8,128)}, f32[2,256,768]{2,1,0:T(8,128)}, u32[]{:S(2)}, u32[]{:S(2)}) collective-permute-start(f32[2,256,768]{2,1,0:T(8,128)} %get-tuple-element.108), channel_id=1, source_target_pairs={{0,8},{8,16},{16,24},{24,32},{32,40},{40,48},{48,56},{56,64},{64,7... | collective-permute-start | bytes 4718600 | tf_op jit(solution)/shard_map/ppermute | solution.py:339
  116.5 2.0 %select_select_fusion.scal = f32[8,128]{1,0:T(8,128)} fusion(f32[]{:T(128)} %reduce_sum.38, f32[]{:T(128)} %fusion.4, pred[128]{0:T(512)(128)(4,1)S(1)} %get-tuple-element.121, pred[128]{0:T(512)(128)(4,1)S(1)} %get-tuple-element.122, pred[8]{0:T(512)(128)(4,1)S(1)} %iota_compare_fusion.2), kind=kLoop, calls=%fused_computation.12 | loop fusion | flops 4096 | bytes 4368 | tf_op jit(solution)/shard_map/jit(_where)/select_n | solution.py:388
  118.4 44.5 %total_over_devices.1 = (f32[2,256,256]{2,1,0:T(8,128)}, f32[8,128]{1,0:T(8,128)}) custom-call(f32[2,256,256]{2,1,0:T(8,128)} %copy-done.5, f32[8,128]{1,0:T(8,128)} %select_select_fusion.scal), custom_call_target="tpu_custom_call" | custom-call | flops 12000000000 | bytes 8388608 | tf_op jit(solution)/shard_map/total_over_devices/pallas_call | solution.py:316
  162.9 1.3 fusion.6
  164.9 2.9 %fusion.1 = f32[2,512,1024]{2,1,0:T(8,128)} fusion(f32[2,512,1024]{2,1,0:T(8,128)} %copy-done.9, f32[2,256,768]{2,1,0:T(8,128)S(1)} %get-tuple-element.106), kind=kLoop, calls=%fused_computation.4 | loop fusion | flops 393216 | bytes 4718592 | tf_op jit(solution)/shard_map/scatter-add | solution.py:395
  167.8 2.3 %fusion.2 = f32[2,512,1024]{2,1,0:T(8,128)} fusion(f32[2,512,1024]{2,1,0:T(8,128)} %fusion.1, f32[2,768,256]{2,1,0:T(8,128)S(1)} %copy-done.11), kind=kLoop, calls=%fused_computation.6 | loop fusion | flops 262144 | bytes 3145728 | tf_op jit(solution)/shard_map/scatter-add | solution.py:396
  170.2 3.3 %add_select_fusion = f32[2,256,256]{2,1,0:T(8,128)S(1)} fusion(f32[2,256,256]{2,1,0:T(8,128)} %collective-permute-done.7, f32[2,512,1024]{2,1,0:T(8,128)} %fusion.2, s32[]{:T(128)} %bitcast.2, s32[]{:T(128)} %bitcast.3, pred[]{:T(512)} %and_reduce_fusion), kind=kLoop, calls=%fused_computation.10 | loop fusion | flops 262144 | bytes 1572873 | tf_op jit(solution)/shard_map/select.10
  173.5 6.5 %scatter-add.26 = f32[2,512,1024]{2,1,0:T(8,128)} dynamic-update-slice(f32[2,512,1024]{2,1,0:T(8,128)} %fusion.2, f32[2,256,256]{2,1,0:T(8,128)S(1)} %add_select_fusion, s32[]{:T(128)} %constant.201.clone.1, s32[]{:T(128)} %bitcast.2, s32[]{:T(128)} %bitcast.3) | dynamic-update-slice | bytes 1048580 | tf_op jit(solution)/shard_map/scatter-add | solution.py:397
  181.6 3.2 %fusion = f32[2,512,1024]{2,1,0:T(8,128)} fusion(f32[2,512,1024]{2,1,0:T(8,128)} %scatter-add.26, f32[2,256,768]{2,1,0:T(8,128)} %collective-permute-done.8), kind=kLoop, calls=%fused_computation.2 | loop fusion | flops 393216 | bytes 4718592 | tf_op jit(solution)/shard_map/scatter-add | solution.py:398
  184.8 5.0 %broadcast_multiply_fusion = f32[2,512,1024]{2,1,0:T(8,128)} fusion(f32[2,512,1024]{2,1,0:T(8,128)} %fusion, f32[]{:T(128)S(6)} %div.13), kind=kLoop, calls=%fused_computation | loop fusion | flops 1048576 | bytes 8388612 | tf_op jit(solution)/shard_map/mul | solution.py:400
  (59 shorter events, 13.6 us)
Async XLA Ops:
  0.6 23.5 %copy-start = (bf16[4,768,256]{2,1,0:T(8,128)(2,1)S(1)}, bf16[4,768,256]{2,1,0:T(8,128)(2,1)}, u32[]{:S(2)}) copy-start(bf16[4,768,256]{2,1,0:T(8,128)(2,1)} %constant.212.clone.refs_4_) | copy-start | bytes 4718596
  0.6 23.5 %copy-start.1 = (bf16[4,256,768]{2,1,0:T(8,128)(2,1)S(1)}, bf16[4,256,768]{2,1,0:T(8,128)(2,1)}, u32[]{:S(2)}) copy-start(bf16[4,256,768]{2,1,0:T(8,128)(2,1)} %constant.213.clone.refs_5_) | copy-start | bytes 4718596
  0.7 23.5 %copy-start.4 = (bf16[512,256]{1,0:T(8,128)(2,1)S(1)}, bf16[512,256]{1,0:T(8,128)(2,1)}, u32[]{:S(2)}) copy-start(bf16[512,256]{1,0:T(8,128)(2,1)} %constant.214.clone.refs_6_) | copy-start | bytes 786436
  0.7 13.9 %copy-start.13 = (s32[16,2]{0,1:T(2,128)S(1)}, s32[16,2]{0,1:T(2,128)}, u32[]{:S(2)}) copy-start(s32[16,2]{0,1:T(2,128)} %param.23) | copy-start | bytes 388
  0.7 14.0 %copy-start.15 = (s32[128]{0:T(128)S(1)}, s32[128]{0:T(128)}, u32[]{:S(2)}) copy-start(s32[128]{0:T(128)} %param.24) | copy-start | bytes 1540
  3.8 15.6 %collective-permute-start.2 = (f32[2,256,256]{2,1,0:T(8,128)}, f32[2,256,256]{2,1,0:T(8,128)}, u32[]{:S(2)}, u32[]{:S(2)}) collective-permute-start(f32[2,256,256]{2,1,0:T(8,128)} %get-tuple-element.115), channel_id=1, source_target_pairs={{8,0},{16,8},{24,16},{32,24},{40,32},{48,40},{56,48},{64,56},{72,6... | collective-permute-start | bytes 1572872 | tf_op jit(solution)/shard_map/ppermute | solution.py:339
  7.3 35.7 %collective-permute-start = (f32[2,512,256]{2,1,0:T(8,128)}, f32[2,512,256]{2,1,0:T(8,128)}, u32[]{:S(2)}, u32[]{:S(2)}) collective-permute-start(f32[2,512,256]{2,1,0:T(8,128)} %slice.192), channel_id=1, source_target_pairs={{1,0},{2,1},{3,2},{4,3},{5,4},{6,5},{7,6},{9,8},{10,9},{11,10},{12... | collective-permute-start | bytes 3145736 | tf_op jit(solution)/shard_map/ppermute | solution.py:339
  10.7 32.3 %collective-permute-start.1 = (f32[2,256,256]{2,1,0:T(8,128)}, f32[2,256,256]{2,1,0:T(8,128)}, u32[]{:S(2)}, u32[]{:S(2)}) collective-permute-start(f32[2,256,256]{2,1,0:T(8,128)} %get-tuple-element.116), channel_id=1, source_target_pairs={{8,0},{16,8},{24,16},{32,24},{40,32},{48,40},{56,48},{64,56},{72,6... | collective-permute-start | bytes 1572872 | tf_op jit(solution)/shard_map/ppermute | solution.py:339
  12.0 55.4 %collective-permute-start.4 = (f32[2,256,256]{2,1,0:T(8,128)}, f32[2,256,256]{2,1,0:T(8,128)}, u32[]{:S(2)}, u32[]{:S(2)}) collective-permute-start(f32[2,256,256]{2,1,0:T(8,128)} %get-tuple-element.114), channel_id=1, source_target_pairs={{8,0},{16,8},{24,16},{32,24},{40,32},{48,40},{56,48},{64,56},{72,6... | collective-permute-start | bytes 1572872 | tf_op jit(solution)/shard_map/ppermute | solution.py:339
  13.3 72.9 %collective-permute-start.5 = (f32[2,256,256]{2,1,0:T(8,128)}, f32[2,256,256]{2,1,0:T(8,128)}, u32[]{:S(2)}, u32[]{:S(2)}) collective-permute-start(f32[2,256,256]{2,1,0:T(8,128)} %get-tuple-element.113), channel_id=1, source_target_pairs={{8,0},{16,8},{24,16},{32,24},{40,32},{48,40},{56,48},{64,56},{72,6... | collective-permute-start | bytes 1572872 | tf_op jit(solution)/shard_map/ppermute | solution.py:339
  19.3 23.7 %collective-permute-start.3 = (f32[2,256,256]{2,1,0:T(8,128)}, f32[2,256,256]{2,1,0:T(8,128)}, u32[]{:S(2)}, u32[]{:S(2)}) collective-permute-start(f32[2,256,256]{2,1,0:T(8,128)} %collective-permute-done.2.refs_10_), channel_id=1, source_target_pairs={{1,0},{2,1},{3,2},{4,3},{5,4},{6,5},{7,6},{9,8},{10,9},{11,10},{12... | collective-permute-start | bytes 1572872 | tf_op jit(solution)/shard_map/ppermute | solution.py:339
  24.2 1.0 copy-start.2
  38.3 0.8 copy-start.6
  39.1 3.9 %copy-start.3 = (f32[2,256,256]{2,1,0:T(8,128)S(1)}, f32[2,256,256]{2,1,0:T(8,128)}, u32[]{:S(2)}) copy-start(f32[2,256,256]{2,1,0:T(8,128)} %refs_3_.7) | copy-start | bytes 1572868
  43.0 1.0 copy-start.7
  44.1 22.6 %copy-start.14 = (s32[3]{0:T(128)S(1)}, s32[3]{0:T(128)}, u32[]{:S(2)}) copy-start(s32[3]{0:T(128)} %constant.207.clone.1) | copy-start | bytes 40
  52.7 33.5 %collective-permute-start.6 = (f32[2,768,256]{2,1,0:T(8,128)}, f32[2,768,256]{2,1,0:T(8,128)S(1)}, u32[]{:S(2)}, u32[]{:S(2)}) collective-permute-start(f32[2,768,256]{2,1,0:T(8,128)} %get-tuple-element.105), channel_id=1, source_target_pairs={{0,1},{1,2},{2,3},{3,4},{4,5},{5,6},{6,7},{8,9},{9,10},{10,11},{11... | collective-permute-start | bytes 4718600 | tf_op jit(solution)/shard_map/ppermute | solution.py:339
  67.4 18.2 %copy-start.8 = (f32[2,512,1024]{2,1,0:T(8,128)S(1)}, f32[2,512,1024]{2,1,0:T(8,128)}, u32[]{:S(2)}) copy-start(f32[2,512,1024]{2,1,0:T(8,128)} %get-tuple-element.94) | copy-start | bytes 12582916
  75.0 95.2 %collective-permute-start.7 = (f32[2,256,256]{2,1,0:T(8,128)S(1)}, f32[2,256,256]{2,1,0:T(8,128)}, u32[]{:S(2)}, u32[]{:S(2)}) collective-permute-start(f32[2,256,256]{2,1,0:T(8,128)S(1)} %get-tuple-element.107), channel_id=1, source_target_pairs={{0,8},{8,16},{16,24},{24,32},{32,40},{40,48},{48,56},{56,64},{64,7... | collective-permute-start | bytes 1572872 | tf_op jit(solution)/shard_map/ppermute | solution.py:339
  86.2 12.5 %copy-start.9 = (f32[2,512,1024]{2,1,0:T(8,128)}, f32[2,512,1024]{2,1,0:T(8,128)S(1)}, u32[]{:S(2)}) copy-start(f32[2,512,1024]{2,1,0:T(8,128)S(1)} %fusion.3) | copy-start | bytes 12582916
  86.2 1.2 copy-start.10
  99.4 82.2 %collective-permute-start.8 = (f32[2,256,768]{2,1,0:T(8,128)}, f32[2,256,768]{2,1,0:T(8,128)}, u32[]{:S(2)}, u32[]{:S(2)}) collective-permute-start(f32[2,256,768]{2,1,0:T(8,128)} %get-tuple-element.108), channel_id=1, source_target_pairs={{0,8},{8,16},{16,24},{24,32},{32,40},{40,48},{48,56},{56,64},{64,7... | collective-permute-start | bytes 4718600 | tf_op jit(solution)/shard_map/ppermute | solution.py:339
  164.9 2.9 %copy-start.11 = (f32[2,768,256]{2,1,0:T(8,128)S(1)}, f32[2,768,256]{2,1,0:T(8,128)}, u32[]{:S(2)}) copy-start(f32[2,768,256]{2,1,0:T(8,128)} %copy-done.10) | copy-start | bytes 4718596
  164.9 15.8 %copy-start.12 = (f32[2,256,256]{2,1,0:T(8,128)S(1)}, f32[2,256,256]{2,1,0:T(8,128)}, u32[]{:S(2)}) copy-start(f32[2,256,256]{2,1,0:T(8,128)} %get-tuple-element.112) | copy-start | bytes 1572868
  (1 other events, 0.8 us)

commit v2 on v1

v2 whole, which is shorter than its diff:
```python
import math

import jax
import jax.numpy as jnp
import numpy as np
from jax import lax
from jax.experimental import pallas as pl
from jax.experimental.pallas import tpu as pltpu
from jax.sharding import PartitionSpec as P

F32 = jnp.float32
BF16 = jnp.bfloat16
M = 256
H = 128
CAP = 16
SIDE = 2
LAG = 0


def split_table(table):
    high = table.astype(np.float32).astype(jnp.bfloat16)
    low = (table - high.astype(np.float64)).astype(np.float32).astype(jnp.bfloat16)
    return high, low


def dft_tables():
    n = np.arange(H)[:, None]
    m = np.arange(H)[None, :]
    right, left = [], []
    for sign in (-1.0, 1.0):
        for odd in (0, 1):
            if sign < 0:
                angle = 2 * math.pi * (n * (2 * m + odd) % M) / M
            else:
                angle = 2 * math.pi * ((2 * n + odd) * m % M) / M
            re, im = np.cos(angle) / 16.0, sign * np.sin(angle) / 16.0
            high, low = split_table(np.block([[re, im], [-im, re]]))
            right.append(np.concatenate([high, high, low], axis=0))
            re, im = re.T, im.T
            high, low = split_table(np.block([[re, -im], [im, re]]))
            left.append(np.concatenate([high, low, high], axis=1))
    order = np.zeros((M, M), np.float32)
    k = np.arange(M)
    order[k, k // 2 + H * (k % 2)] = 1.0
    order = np.concatenate([order, order], axis=0).astype(jnp.bfloat16)
    return np.stack(right), np.stack(left), order


def split(value):
    high = value.astype(BF16)
    return high, (value - high.astype(F32)).astype(BF16)


def dot(a, b):
    return jnp.dot(a, b, preferred_element_type=F32)


def right_dot(value, table):
    high, low = split(value)
    return dot(jnp.concatenate([high, low, high], axis=1), table)


def left_dot(table, value):
    high, low = split(value)
    return dot(table, jnp.concatenate([high, high, low], axis=0))


def lanes(a, b):
    return jnp.concatenate([a, b], axis=1)


def rows(*parts):
    return jnp.concatenate(parts, axis=0)


def one_window(spot, ext, acc, probe, right, left, order, pacc, stats, rolled, patch):
    top, j0, dc, pat = spot
    lane = lax.broadcasted_iota(jnp.int32, (M, H), 1)
    mask = lane >= dc
    at = pl.ds(top, M)

    def turned(a, b, shift, keep):
        a, b = pltpu.roll(a, shift, 1), pltpu.roll(b, shift, 1)
        return jnp.where(keep, a, b), jnp.where(keep, b, a)

    for p in range(2):
        a, b = turned(probe[p, :, :H], probe[p, :, H:], dc, mask)
        rolled[p, :, :H] = a
        rolled[p, :, H:] = b
        patch[p, :, :H] = jnp.where(mask, ext[p, j0, at, :], ext[p, j0 + 2, at, :])
        patch[p, :, H:] = ext[p, j0 + 1, at, :]
    wave_re = rolled[0] * patch[0] - rolled[1] * patch[1]
    wave_im = rolled[0] * patch[1] + rolled[1] * patch[0]
    sums = lanes(wave_re[:, :H] + wave_re[:, H:], wave_im[:, :H] + wave_im[:, H:])
    difs = lanes(wave_re[:, :H] - wave_re[:, H:], wave_im[:, :H] - wave_im[:, H:])
    yield
    even = right_dot(sums, right[0])
    odd = right_dot(difs, right[1])
    yield
    halves = ((even[:H] + even[H:], odd[:H] + odd[H:]), (even[:H] - even[H:], odd[:H] - odd[H:]))
    fars, levels = [], []
    for parity, (e, o) in enumerate(halves):
        fars.append(left_dot(left[parity], rows(lanes(e[:, :H], o[:, :H]), lanes(e[:, H:], o[:, H:]))))
        every = pl.ds(parity, H, 2)
        level = lanes(pat[0, every, :], pat[1, every, :])
        stats[8:] += jnp.sum(level.reshape(16, 8, M), axis=0)
        high, low = split(level)
        levels.append(dot(lanes(high, low), order[...]))
        yield
    back = []
    for parity, far in enumerate(fars):
        far_re, far_im = far[:H], far[H:]
        resid = far_re * far_re + far_im * far_im - levels[parity]
        stats[:8] += jnp.sum((resid * resid).reshape(16, 8, M), axis=0)
        back.append(left_dot(left[2 + parity], rows(resid * far_re, resid * far_im)))
        yield
    half_s, half_d = back[0] + back[1], back[0] - back[1]
    re, im = rows(half_s[:H], half_d[:H]), rows(half_s[H:], half_d[H:])
    even = right_dot(lanes(re[:, :H], im[:, :H]), right[2])
    odd = right_dot(lanes(re[:, H:], im[:, H:]), right[3])
    yield
    first, second = even + odd, even - odd
    back_re = lanes(first[:, :H], second[:, :H])
    back_im = lanes(first[:, H:], second[:, H:])
    unmask = lane < H - dc
    undo = lax.rem(H - dc, H)
    for p in range(2):
        if p == 0:
            update = rolled[0] * back_re + rolled[1] * back_im
            grad = patch[0] * back_re + patch[1] * back_im
        else:
            update = rolled[0] * back_im - rolled[1] * back_re
            grad = patch[0] * back_im - patch[1] * back_re
        acc[p, j0, at, :] += jnp.where(mask, update[:, :H], 0.0)
        acc[p, j0 + 2, at, :] += jnp.where(mask, 0.0, update[:, :H])
        acc[p, j0 + 1, at, :] += update[:, H:]
        a, b = turned(grad[:, :H], grad[:, H:], undo, unmask)
        pacc[p, :, :H] += a
        pacc[p, :, H:] += b
    yield


def some_windows(spots, ext, acc, probe, right, left, order, pacc, stats, rolled, patch):
    runs = [
        one_window(spot, ext, acc, probe, right, left, order, pacc, stats, rolled.at[w], patch.at[w])
        for w, spot in enumerate(spots)
    ]
    steps = 8
    for t in range(steps + LAG * (len(runs) - 1)):
        for w, run in enumerate(runs):
            if 0 <= t - LAG * w < steps:
                next(run)


def windows_kernel(plan, *refs):
    names = plan["names"]
    at = dict(zip(names, refs))
    ext, acc = at["ext"], at["acc"]
    pos, count = at["pos"], at["count"]
    n_pieces, n_carry = len(plan["pieces"]), len(plan["carry"])
    nblk = plan["nblk"]

    def here(s):
        o, c = pos[s, 0], pos[s, 1]
        return (s < count[0]) & plan["cond"](o, c)

    copies = []

    def begin(src, dst):
        copy = pltpu.make_async_copy(src, dst, at["sems"].at[len(copies)])
        copy.start()
        copies.append(copy)

    def pattern_copies(s):
        return [
            pltpu.make_async_copy(at["patterns"].at[s, :, pl.ds(k * H, H)], at["pat"].at[s, k], at["pat_sems"].at[s, k])
            for k in range(2)
        ]

    for ref, (r0, c0, nr, nc, dr, db) in zip(at["pieces"], plan["pieces"]):
        for k in range(nc // H):
            begin(ref.at[:, pl.ds(r0, nr), pl.ds(c0 + k * H, H)], ext.at[:, db + k, pl.ds(dr, nr), :])
    for ref, (r0, c0, nr, nc, dr, db) in zip(at["carry"], plan["carry"]):
        for k in range(nc // H):
            begin(ref.at[:, pl.ds(r0, nr), pl.ds(c0 + k * H, H)], acc.at[:, db + k, pl.ds(dr, nr), :])

    todo = at["todo"]

    def choose(s, n):
        todo[n] = s

        @pl.when(here(s))
        def _():
            for copy in pattern_copies(s):
                copy.start()

        return n + here(s).astype(jnp.int32)

    chosen = lax.fori_loop(0, CAP, choose, jnp.int32(0))
    for b, first, end in plan["zeros"]:
        acc[:, b, first:end] = jnp.zeros_like(acc[:, b, first:end])
    for name in ("pacc", "stats"):
        at[name][...] = at[name + "_in"][...] if plan["sums"] else jnp.zeros_like(at[name])
    for copy in copies:
        copy.wait()

    def spot(i):
        s = todo[i]
        for copy in pattern_copies(s):
            copy.wait()
        o, c = pos[s, 0] - plan["row0"], pos[s, 1] - plan["col0"]
        return o, c // H, c % H, at["pat"].at[s]

    def run(spots):
        some_windows(spots, ext, acc, at["probe"], at["right"], at["left"],
                     at["order"], at["pacc"], at["stats"], at["rolled"], at["patch"])

    @pl.loop(0, chosen // SIDE)
    def _(i):
        run([spot(SIDE * i + w) for w in range(SIDE)])

    @pl.loop(chosen // SIDE * SIDE, chosen)
    def _(i):
        run([spot(i)])

    ends = []
    for ref, (r0, nr, nc, db) in zip(at["outs"], plan["outs"]):
        for k in range(nc // H):
            copy = pltpu.make_async_copy(acc.at[:, db + k, pl.ds(r0, nr), :], ref.at[:, :, pl.ds(k * H, H)],
                                         at["sems"].at[len(copies) + len(ends)])
            copy.start()
            ends.append(copy)
    for copy in ends:
        copy.wait()


def windows(name, pos, count, patterns, probe, tables, sums, pieces, carry, outs, nblk, nrows, row0, col0, cond, cost=8):
    right, left, order = tables
    vm = pl.BlockSpec(memory_space=pltpu.VMEM)
    sm = pl.BlockSpec(memory_space=pltpu.SMEM)
    hbm = pl.BlockSpec(memory_space=pl.ANY)
    zeros = []
    for b in range(nblk):
        full = sorted((c[5], c[5] + c[3]) for c in carry if c[6] <= b < c[6] + c[4] // H)
        ends = [0] + [x for span in full for x in span] + [nrows]
        zeros += [(b, first, end) for first, end in zip(ends[::2], ends[1::2]) if end > first]
    plan = dict(
        pieces=[p[1:] for p in pieces], carry=[c[1:] for c in carry], outs=outs, nblk=nblk, row0=row0, col0=col0, cond=cond, sums=sums,
        zeros=zeros,
    )
    n_p, n_c, n_o = len(pieces), len(carry), len(outs)
    n_sems = sum(p[4] // H for p in pieces) + sum(c[4] // H for c in carry) + sum(o[2] // H for o in outs)

    def kernel(*refs):
        it = iter(refs)
        take = lambda n: [next(it) for _ in range(n)]
        at = {}
        at["pos"], at["count"], at["patterns"], at["probe"], at["right"], at["left"], at["order"] = take(7)
        at["pacc_in"], at["stats_in"] = take(2) if sums else (None, None)
        at["pieces"], at["carry"], at["outs"] = take(n_p), take(n_c), take(n_o)
        at["pacc"], at["stats"] = take(2)
        at["ext"], at["acc"], at["pat"], at["rolled"], at["patch"], at["sems"], at["pat_sems"], at["todo"] = take(8)
        windows_kernel(dict(plan, names=list(at)), *at.values())

    out = pl.pallas_call(
        kernel,
        name=name,
        out_shape=[jax.ShapeDtypeStruct((2, nr, nc), F32) for _, nr, nc, _ in outs]
        + [jax.ShapeDtypeStruct((2, M, M), F32), jax.ShapeDtypeStruct((16, M), F32)],
        in_specs=[sm, sm, hbm, vm, vm, vm, vm] + [vm] * len(sums) + [hbm] * (n_p + n_c),
        out_specs=[hbm] * n_o + [vm, vm],
        scratch_shapes=[
            pltpu.VMEM((2, nblk, nrows, H), F32),
            pltpu.VMEM((2, nblk, nrows, H), F32),
            pltpu.VMEM((CAP, 2, M, H), F32),
            pltpu.VMEM((SIDE, 2, M, M), F32),
            pltpu.VMEM((SIDE, 2, M, M), F32),
            pltpu.SemaphoreType.DMA((n_sems,)),
            pltpu.SemaphoreType.DMA((CAP, 2)),
            pltpu.SMEM((CAP,), jnp.int32),
        ],
        compiler_params=pltpu.CompilerParams(vmem_limit_bytes=48 << 20),
        cost_estimate=pl.CostEstimate(flops=cost, bytes_accessed=1 << 10, transcendentals=0),
    )(pos, count, patterns, probe, right, left, order, *sums, *[p[0] for p in pieces], *[c[0] for c in carry])
    return out[:n_o], tuple(out[n_o:])


MESH = pl.DeviceIdType.MESH
NROW, NCOL = 16, 8


def tail_kernel(visits, pacc, stats, halo, out, coeff, misfit, down, mine1, got1, mine2, got2, part, wide, s1, r1, s2, r2, s3, r3, s4, r4, s5, r5):
    row, col = lax.axis_index("row"), lax.axis_index("col")

    def col_peer(k):
        return row, lax.rem(col + k, NCOL)

    def row_peer(k):
        return lax.rem(row + k, NROW), col

    barrier = pltpu.get_barrier_semaphore()
    for k in range(1, NCOL):
        pl.semaphore_signal(barrier, inc=1, device_id=col_peer(k), device_id_type=MESH)
    for k in range(1, NROW):
        pl.semaphore_signal(barrier, inc=1, device_id=row_peer(k), device_id_type=MESH)
    for p in range(2):
        for b in range(2):
            for h in range(2):
                piece = 4 * p + 2 * b + h
                mine1[piece, :H] = pacc[p, h * H : (h + 1) * H, b * H : (b + 1) * H]
                mine1[piece, H:] = stats[:, :H] + stats[:, H:]
    pl.semaphore_wait(barrier, NCOL + NROW - 2)

    def send(src, dst, ss, rs, peer):
        copy = pltpu.make_async_remote_copy(src, dst, ss, rs, device_id=peer, device_id_type=MESH)
        copy.start()
        return copy

    pieces = []

    def send_pieces(n):
        for _ in range(n):
            k = len(pieces)
            cols = pl.ds(k * H, H)
            pieces.append(send(halo.at[:, :, cols], down.at[:, :, cols], s5.at[k], r5.at[k], row_peer(1)))

    copies = [
        send(mine1.at[lax.rem(col + k, NCOL)], got1.at[k - 1], s1.at[k - 1], r1.at[k - 1], col_peer(k))
        for k in range(1, NCOL)
    ]
    send_pieces(2)
    for copy in copies:
        copy.wait()
    total = mine1[col]
    for k in range(NCOL - 1):
        total = total + got1[k]
    for k in range(NROW):
        mine2[k, :8] = total[8 * k : 8 * k + 8]
        mine2[k, 8:] = total[H:]
    copies = [
        send(mine2.at[lax.rem(row + k, NROW)], got2.at[k - 1], s2.at[k - 1], r2.at[k - 1], row_peer(k))
        for k in range(1, NROW)
    ]
    send_pieces(1)
    for copy in copies:
        copy.wait()
    total = mine2[row]
    for k in range(NROW - 1):
        total = total + got2[k]
    pixels = M * M * visits[0]
    mean = jnp.full((8, H), jnp.sum(total[16:])) / pixels
    factor = 4.0 / (mean * mean)
    coeff[...] = factor
    misfit[...] = jnp.full((8, H), jnp.sum(total[8:16])) / (mean * mean * pixels)
    part[row] = total[:8] * (factor / visits[0])
    copies = [send(part.at[row], part.at[row], s3.at[k - 1], r3.at[k - 1], row_peer(k)) for k in range(1, NROW)]
    send_pieces(1)
    for copy in copies:
        copy.wait()
    copies = [send(part, wide.at[col], s4.at[k - 1], r4.at[k - 1], col_peer(k)) for k in range(1, NCOL)]
    send_pieces(2)
    wide[col] = part[...]
    for copy in copies + pieces:
        copy.wait()
    for p in range(2):
        for b in range(2):
            for h in range(2):
                out[p, h * H : (h + 1) * H, b * H : (b + 1) * H] = wide[4 * p + 2 * b + h].reshape(H, H)


def tail(visits, pacc, stats, halo):
    vm = pl.BlockSpec(memory_space=pltpu.VMEM)
    sm = pl.BlockSpec(memory_space=pltpu.SMEM)
    sems = [pltpu.SemaphoreType.DMA((n,)) for n in (NCOL - 1, NCOL - 1, NROW - 1, NROW - 1, NROW - 1, NROW - 1, NCOL - 1, NCOL - 1, 6, 6)]
    hbm = pl.BlockSpec(memory_space=pl.ANY)
    tile = jax.ShapeDtypeStruct((8, H), F32)
    return pl.pallas_call(
        tail_kernel,
        name="tail",
        out_shape=[jax.ShapeDtypeStruct((2, M, M), F32), tile, tile, jax.ShapeDtypeStruct((2, M, 768), F32)],
        in_specs=[sm, vm, vm, hbm],
        out_specs=[vm, vm, vm, hbm],
        scratch_shapes=[
            pltpu.VMEM((NCOL, H + 16, H), F32),
            pltpu.VMEM((NCOL - 1, H + 16, H), F32),
            pltpu.VMEM((NROW, 24, H), F32),
            pltpu.VMEM((NROW - 1, 24, H), F32),
            pltpu.VMEM((NROW, 8, H), F32),
            pltpu.VMEM((NCOL, NROW, 8, H), F32),
        ]
        + sems,
        compiler_params=pltpu.CompilerParams(collective_id=0, has_side_effects=True),
        cost_estimate=pl.CostEstimate(flops=10**6, bytes_accessed=1 << 20, transcendentals=0),
    )(visits, pacc, stats, halo)


def finish_kernel(upper, coeff, inner, own12, own4, own3, right, down12, down3, out):
    k = pl.program_id(0)
    factor = coeff[0:1, 0:1]

    @pl.when(k < 3)
    def _():
        out[:, :M] = (inner[:, :M] + jnp.where(upper[0] > 0, down12[...], 0.0)) * factor
        out[:, M:] = own12[...] * factor

    @pl.when(k < 2)
    def _():
        out[:, M:] += inner[:, M:] * factor

    @pl.when(k == 3)
    def _():
        out[:, :M] = (own4[...] + down3[...]) * factor
        out[:, M:] = own3[...] * factor

    @pl.when(k == 0)
    def _():
        out[...] += right[...] * factor


def finished(upper, coeff, inner, own12, own4, own3, right, down12, down3):
    block = lambda index: pl.BlockSpec((2, M, M), index)
    return pl.pallas_call(
        finish_kernel,
        name="finished",
        grid=(4,),
        out_shape=jax.ShapeDtypeStruct((2, 512, 1024), F32),
        in_specs=[
            pl.BlockSpec(memory_space=pltpu.SMEM),
            pl.BlockSpec(memory_space=pltpu.VMEM),
            pl.BlockSpec((2, 512, M), lambda k: (0, 0, jnp.minimum(k, 2))),
            block(lambda k: (0, 0, jnp.minimum(k, 2))),
            block(lambda k: (0, 0, 0)),
            block(lambda k: (0, 0, 1)),
            pl.BlockSpec((2, 512, M), lambda k: (0, 0, 0)),
            block(lambda k: (0, 0, jnp.minimum(k, 2))),
            block(lambda k: (0, 0, 0)),
        ],
        out_specs=pl.BlockSpec((2, 512, M), lambda k: (0, 0, k)),
        cost_estimate=pl.CostEstimate(flops=10**7, bytes_accessed=10 << 20, transcendentals=0),
    )(upper, coeff, inner, own12, own4, own3, right, down12, down3)


def passed_along(value, axis, steps):
    count = lax.axis_size(axis)
    first, last = (max(0, -steps), min(count, count - steps))
    return lax.ppermute(value, axis, [(source, source + steps) for source in range(first, last)])


def body(sample, probe, patterns, positions, counts):
    tile_rows, tile_cols = sample.shape[1:]
    row_at, col_at = lax.axis_index("row"), lax.axis_index("col")
    own = counts[row_at * NCOL + col_at]
    pos = positions - jnp.stack([row_at * tile_rows, col_at * tile_cols])[None, :]
    count = own.reshape(1)
    visits = jnp.sum(counts).astype(F32).reshape(1)
    tables = tuple(jnp.asarray(t) for t in dft_tables())
    args = (pos, count, patterns, probe, tables)
    chunk = lambda k: sample[:, :M, k * M : (k + 1) * M]
    first = chunk(0)
    sample, first = lax.optimization_barrier((sample, first))
    low = [passed_along(first, "row", -1), None, None, passed_along(chunk(3), "row", -1)]
    right = passed_along(sample[:, :, :M], "col", -1)
    (inner,), sums = windows(
        "windows_inside", *args, (),
        [(sample, 0, 0, 512, 1024, 0, 0)], [], [(0, 512, 1024, 0)],
        8, 512, 0, 0, lambda o, c: (o <= M) & (c < 768),
    )
    sums, next_low, sample = lax.optimization_barrier((sums, low[0], sample))
    low[2] = passed_along(chunk(2), "row", -1)
    low[1] = passed_along(chunk(1), "row", -1)
    corner = passed_along(next_low, "col", -1)
    (own4, edge, edge_low, part3), sums = windows(
        "windows_right", *args, sums,
        [(sample, 0, 768, 512, M, 0, 0), (right, 0, 0, 512, M, 0, 2), (low[3], 0, 0, M, M, 512, 0), (corner, 0, 0, M, M, 512, 2)],
        [(inner, 0, 768, 512, M, 0, 0)], [(0, 512, M, 0), (0, 512, M, 2), (512, M, M, 2), (512, M, M, 0)],
        4, 768, 0, 768, lambda o, c: c >= 768,
    )
    low_right = passed_along(edge_low, "col", 1)
    came_right = passed_along(edge, "col", 1)
    (own3, halo3, part2), sums = windows(
        "windows_third", *args, sums,
        [(sample, M, 512, M, 512, 0, 0), (low[2], 0, 0, M, M, M, 0), (low[3], 0, 0, M, M, M, 2)],
        [(part3, 0, 0, M, M, M, 2), (own4, M, 0, M, M, 0, 2), (inner, M, 512, M, M, 0, 0)],
        [(0, M, 512, 0), (M, M, M, 2), (M, M, M, 0)],
        4, 512, M, 512, lambda o, c: (o > M) & (c >= 512) & (c < 768),
    )
    down3 = passed_along(halo3, "row", 1)
    (own12, halo12), sums = windows(
        "windows_left", *args, sums,
        [(sample, M, 0, M, 768, 0, 0), (low[0], 0, 0, M, M, M, 0), (low[1], 0, 0, M, M, M, 2), (low[2], 0, 0, M, M, M, 4)],
        [(part2, 0, 0, M, M, M, 4), (low_right, 0, 0, M, M, M, 0), (own3, 0, 0, M, M, 0, 4)],
        [(0, M, 768, 0), (M, M, 768, 0)],
        6, 512, M, 0, lambda o, c: (o > M) & (c < 512),
    )
    probe_grad, coeff, misfit, down12 = tail(visits, *sums, halo12)
    upper = (row_at > 0).astype(jnp.int32).reshape(1)
    object_grad = finished(upper, coeff, inner, own12, own4, own3, came_right, down12, down3)
    return object_grad, probe_grad, misfit[0, 0]


def solution(mesh):
    in_specs = (
        P(None, "row", "col"),
        P(),
        P(("row", "col"), None, None),
        P(("row", "col"), None),
        P(),
    )
    out_specs = (P(None, "row", "col"), P(), P())
    return jax.shard_map(body, mesh=mesh, in_specs=in_specs, out_specs=out_specs, check_vma=False)
```

time: 192 us -> 163 us (0.85)
  the two profiles are of different devices: /device:TPU:1 before, /device:TPU:14 now
where the time goes in v2:
time: 163 us; the launch traced here: 162 us
  Pallas kernels  112 us (69%)
  starting transfers between devices  25.4 us (16%)
  local copies, waits for them, and re-layouts  18.2 us (11%)
  waiting for transfers between devices  4.59 us (3%)
    pallas_call x1, Pallas kernels, tail(): pl.pallas_call(tail_kernel, name='tail', out_shape=[jax.ShapeDtypeStruct(...  56.4 us
    pallas_call x4, Pallas kernels, windows(): pl.pallas_call(kernel, name=name, out_shape=[jax.ShapeDtypeStruct((2, nr,...  48.5 us
    ppermute x9, starting transfers between devices, passed_along(): lax.ppermute(value, axis, [(source, source + steps) for source in range(f...  25.4 us
    unnamed x34, local copies, waits for them, and re-layouts  8.08 us
    pallas_call x1, Pallas kernels, finished(): pl.pallas_call(finish_kernel, name='finished', grid=(4,), out_shape=jax.S...  6.64 us
    slice x3, local copies, waits for them, and re-layouts, body(): chunk = lambda k: sample[:, :M, k * M:(k + 1) * M]  6.05 us
    ppermute x9, waiting for transfers between devices, passed_along(): lax.ppermute(value, axis, [(source, source + steps) for source in range(f...  4.59 us
  transfers between devices with their start and end apart: 9, of which 2 were waited for; matrix products, arithmetic and copies ran while one was open for 5% of the time, Pallas kernels for 65%

profile of v2, /device:TPU:14, one launch (start us, length us, event | category | flops | bytes accessed | tf_op | source)
XLA Modules:
  0.0 162.0 jit_solution(6909222213417862007)
XLA Ops:
  0.7 2.1 %slice.18 = f32[2,256,256]{2,1,0:T(8,128)} slice(f32[2,512,1024]{2,1,0:T(8,128)} %refs_9_.2), slice={[0:2], [0:256], [0:256]} | slice | bytes 1048576 | tf_op jit(solution)/shard_map/slice | solution.py:458
  2.7 2.3 %collective-permute-start = (f32[2,256,256]{2,1,0:T(8,128)}, f32[2,256,256]{2,1,0:T(8,128)}, u32[]{:S(2)}, u32[]{:S(2)}) collective-permute-start(f32[2,256,256]{2,1,0:T(8,128)} %slice.18), channel_id=1, source_target_pairs={{8,0},{16,8},{24,16},{32,24},{40,32},{48,40},{56,48},{64,56},{72,6... | collective-permute-start | bytes 1572872 | tf_op jit(solution)/shard_map/ppermute | solution.py:446
  5.1 2.3 %slice.19 = f32[2,512,256]{2,1,0:T(8,128)} slice(f32[2,512,1024]{2,1,0:T(8,128)} %refs_9_.2), slice={[0:2], [0:512], [0:256]} | slice | bytes 2097152 | tf_op jit(solution)/shard_map/slice | solution.py:462
  7.4 1.9 %collective-permute-start.1 = (f32[2,512,256]{2,1,0:T(8,128)}, f32[2,512,256]{2,1,0:T(8,128)}, u32[]{:S(2)}, u32[]{:S(2)}) collective-permute-start(f32[2,512,256]{2,1,0:T(8,128)} %slice.19), channel_id=1, source_target_pairs={{1,0},{2,1},{3,2},{4,3},{5,4},{6,5},{7,6},{9,8},{10,9},{11,10},{12... | collective-permute-start | bytes 3145736 | tf_op jit(solution)/shard_map/ppermute | solution.py:446
  9.3 1.9 %slice.20 = f32[2,256,256]{2,1,0:T(8,128)} slice(f32[2,512,1024]{2,1,0:T(8,128)} %refs_9_.2), slice={[0:2], [0:256], [768:1024]} | slice | bytes 1048576 | tf_op jit(solution)/shard_map/slice | solution.py:458
  11.2 1.9 %collective-permute-start.2 = (f32[2,256,256]{2,1,0:T(8,128)}, f32[2,256,256]{2,1,0:T(8,128)}, u32[]{:S(2)}, u32[]{:S(2)}) collective-permute-start(f32[2,256,256]{2,1,0:T(8,128)} %slice.20), channel_id=1, source_target_pairs={{8,0},{16,8},{24,16},{32,24},{40,32},{48,40},{56,48},{64,56},{72,6... | collective-permute-start | bytes 1572872 | tf_op jit(solution)/shard_map/ppermute | solution.py:446
  14.9 14.5 %windows_inside.1 = (f32[2,512,1024]{2,1,0:T(8,128)}, f32[2,256,256]{2,1,0:T(8,128)S(1)}, f32[16,256]{1,0:T(8,128)S(1)}) custom-call(s32[16,2]{1,0:T(8,128)S(1)} %broadcast_subtract_fusion.refs_0_, s32[1]{0:T(128)} %dynamic_slice.3.refs_1_, f32[16,256,256]{2,1,0:T(8,128)} %refs_2_.7, f32[2,256,256]{2,1,0:T(8,128)S(1)} %copy-done.2, ...), custom_call_target="tpu_custom_call" | custom-call | flops 8 | bytes 1024 | tf_op jit(solution)/shard_map/windows_inside/pallas_call | solution.py:265
  29.5 5.7 %collective-permute-start.3 = (f32[2,256,256]{2,1,0:T(8,128)}, f32[2,256,256]{2,1,0:T(8,128)S(1)}, u32[]{:S(2)}, u32[]{:S(2)}) collective-permute-start(f32[2,256,256]{2,1,0:T(8,128)} %collective-permute-done.refs_10_), channel_id=1, source_target_pairs={{1,0},{2,1},{3,2},{4,3},{5,4},{6,5},{7,6},{9,8},{10,9},{11,10},{12... | collective-permute-start | bytes 1572872 | tf_op jit(solution)/shard_map/ppermute | solution.py:446
  35.2 2.1 %fusion = (f32[2,256,256]{2,1,0:T(8,128)}, f32[2,256,256]{2,1,0:T(8,128)S(1)}) fusion(f32[2,512,1024]{2,1,0:T(8,128)} %refs_9_.2), kind=kLoop, calls=%fused_computation.2 | loop fusion | bytes 2097152 | tf_op jit(solution)/shard_map/slice | solution.py:458
  37.3 1.9 %collective-permute-start.4 = (f32[2,256,256]{2,1,0:T(8,128)S(1)}, f32[2,256,256]{2,1,0:T(8,128)S(1)}, u32[]{:S(2)}, u32[]{:S(2)}) collective-permute-start(f32[2,256,256]{2,1,0:T(8,128)S(1)} %get-tuple-element.60), channel_id=1, source_target_pairs={{8,0},{16,8},{24,16},{32,24},{40,32},{48,40},{56,48},{64,56},{72,6... | collective-permute-start | bytes 1572872 | tf_op jit(solution)/shard_map/ppermute | solution.py:446
  39.2 2.9 %collective-permute-done.3.refs_12_ = f32[2,256,256]{2,1,0:T(8,128)S(1)} collective-permute-done((f32[2,256,256]{2,1,0:T(8,128)}, f32[2,256,256]{2,1,0:T(8,128)S(1)}, u32[]{:S(2)}, u32[]{:S(2)}) %collective-permute-start.3) | collective-permute-done | bytes 524320 | tf_op jit(solution)/shard_map/ppermute | solution.py:446
  42.2 16.8 %windows_right.1 = (f32[2,512,256]{2,1,0:T(8,128)S(1)}, f32[2,512,256]{2,1,0:T(8,128)}, f32[2,256,256]{2,1,0:T(8,128)}, f32[2,256,256]{2,1,0:T(8,128)S(1)}, f32[...) custom-call(s32[16,2]{1,0:T(8,128)S(1)} %broadcast_subtract_fusion.refs_0_, s32[1]{0:T(128)} %dynamic_slice.3.refs_1_, ...), custom_call_target="tpu_custom_call" | custom-call | flops 8 | bytes 1024 | tf_op jit(solution)/shard_map/windows_right/pallas_call | solution.py:265
  59.0 1.1 copy-done.5
  60.0 1.9 %collective-permute-start.7 = (f32[2,512,256]{2,1,0:T(8,128)}, f32[2,512,256]{2,1,0:T(8,128)}, u32[]{:S(2)}, u32[]{:S(2)}) collective-permute-start(f32[2,512,256]{2,1,0:T(8,128)} %get-tuple-element.54), channel_id=1, source_target_pairs={{0,1},{1,2},{2,3},{3,4},{4,5},{5,6},{6,7},{8,9},{9,10},{10,11},{11... | collective-permute-start | bytes 3145736 | tf_op jit(solution)/shard_map/ppermute | solution.py:446
  61.9 1.9 %collective-permute-start.5 = (f32[2,256,256]{2,1,0:T(8,128)}, f32[2,256,256]{2,1,0:T(8,128)}, u32[]{:S(2)}, u32[]{:S(2)}) collective-permute-start(f32[2,256,256]{2,1,0:T(8,128)} %get-tuple-element.59), channel_id=1, source_target_pairs={{8,0},{16,8},{24,16},{32,24},{40,32},{48,40},{56,48},{64,56},{72,6... | collective-permute-start | bytes 1572872 | tf_op jit(solution)/shard_map/ppermute | solution.py:446
  63.9 1.9 %collective-permute-start.6 = (f32[2,256,256]{2,1,0:T(8,128)}, f32[2,256,256]{2,1,0:T(8,128)}, u32[]{:S(2)}, u32[]{:S(2)}) collective-permute-start(f32[2,256,256]{2,1,0:T(8,128)} %get-tuple-element.47), channel_id=1, source_target_pairs={{0,1},{1,2},{2,3},{3,4},{4,5},{5,6},{6,7},{8,9},{9,10},{10,11},{11... | collective-permute-start | bytes 1572872 | tf_op jit(solution)/shard_map/ppermute | solution.py:446
  65.8 5.8 %windows_third.1 = (f32[2,256,512]{2,1,0:T(8,128)S(1)}, f32[2,256,256]{2,1,0:T(8,128)}, f32[2,256,256]{2,1,0:T(8,128)S(1)}, f32[2,256,256]{2,1,0:T(8,128)S(1)}, f32[16,256]{1,0:T(8,128)S(1)}) custom-call(s32[16,2]{1,0:T(8,128)S(1)} %broadcast_subtract_fusion.refs_0_, s32[1]{0:T(128)} %dynamic_slice.3.refs_1_, f32[16,256,256]{2,1,0:T(8,128)} %refs_2_.7, ...), custom_call_target="tpu_custom_call" | custom-call | flops 8 | bytes 1024 | tf_op jit(solution)/shard_map/windows_third/pallas_call | solution.py:265
  73.2 5.9 %collective-permute-start.8 = (f32[2,256,256]{2,1,0:T(8,128)}, f32[2,256,256]{2,1,0:T(8,128)}, u32[]{:S(2)}, u32[]{:S(2)}) collective-permute-start(f32[2,256,256]{2,1,0:T(8,128)} %get-tuple-element.56), channel_id=1, source_target_pairs={{0,8},{8,16},{16,24},{24,32},{32,40},{40,48},{48,56},{56,64},{64,7... | collective-permute-start | bytes 1572872 | tf_op jit(solution)/shard_map/ppermute | solution.py:446
  80.4 1.6 %collective-permute-done.6.refs_14_ = f32[2,256,256]{2,1,0:T(8,128)} collective-permute-done((f32[2,256,256]{2,1,0:T(8,128)}, f32[2,256,256]{2,1,0:T(8,128)}, u32[]{:S(2)}, u32[]{:S(2)}) %collective-permute-start.6) | collective-permute-done | bytes 524320 | tf_op jit(solution)/shard_map/ppermute | solution.py:446
  82.1 1.0 copy-done.9
  84.1 11.4 %windows_left.1 = (f32[2,256,768]{2,1,0:T(8,128)}, f32[2,256,768]{2,1,0:T(8,128)}, f32[2,256,256]{2,1,0:T(8,128)S(1)}, f32[16,256]{1,0:T(8,128)S(1)}) custom-call(s32[16,2]{1,0:T(8,128)S(1)} %broadcast_subtract_fusion.refs_0_, s32[1]{0:T(128)} %dynamic_slice.3.refs_1_, f32[16,256,256]{2,1,0:T(8,128)} %refs_2_.7, f32[2,256,256]{2,1,0:T(8,128)S(1)} %copy-done.3, ...), custom_call_target="tpu_custom_call" | custom-call | flops 8 | bytes 1024 | tf_op jit(solution)/shard_map/windows_left/pallas_call | solution.py:265
  97.0 56.4 %tail.1 = (f32[2,256,256]{2,1,0:T(8,128)}, f32[8,128]{1,0:T(8,128)}, f32[8,128]{1,0:T(8,128)}, f32[2,256,768]{2,1,0:T(8,128)}) custom-call(f32[1]{0:T(128)} %bitcast.1.visits, f32[2,256,256]{2,1,0:T(8,128)} %copy-done.7, f32[16,256]{1,0:T(8,128)} %copy-done.12, f32[2,256,768]{2,1,0:T(8,128)} %get-tuple-element.51.halo), custom_call_target="tpu_custom_call" | custom-call | flops 1000000 | bytes 1048576 | tf_op jit(solution)/shard_map/tail/pallas_call | solution.py:377
  153.4 1.2 slice.23
  154.6 6.6 %finished.1 = f32[2,512,1024]{2,1,0:T(8,128)} custom-call(s32[1]{0:T(128)} %bitcast.upper, f32[8,128]{1,0:T(8,128)} %get-tuple-element.52.coeff, f32[2,512,1024]{2,1,0:T(8,128)} %get-tuple-element.39.refs_13_.refs_14_.inner, f32[2,256,768]{2,1,0:T(8,128)} %get-tuple-element.53.own12, f32[2,512,256]{2,1,0:T(8,128)} %copy-done.5, f32[2,256,512]{2,1,0:T(8,128)} %copy-done.6, ...), custom_call_target="tpu_custom_call" | custom-call | flops 10000000 | bytes 10485760 | tf_op jit(solution)/shard_map/finished/pallas_call | solution.py:422
  (43 shorter events, 7.3 us)
Async XLA Ops:
  0.6 13.3 %copy-start.4 = (bf16[512,256]{1,0:T(8,128)(2,1)S(1)}, bf16[512,256]{1,0:T(8,128)(2,1)}, u32[]{:S(2)}) copy-start(bf16[512,256]{1,0:T(8,128)(2,1)} %constant.27.clone.refs_6_) | copy-start | bytes 786436
  0.6 13.2 %copy-start = (bf16[4,256,768]{2,1,0:T(8,128)(2,1)S(1)}, bf16[4,256,768]{2,1,0:T(8,128)(2,1)}, u32[]{:S(2)}) copy-start(bf16[4,256,768]{2,1,0:T(8,128)(2,1)} %constant.26.clone.refs_5_) | copy-start | bytes 4718596
  0.7 13.2 %copy-start.1 = (bf16[4,768,256]{2,1,0:T(8,128)(2,1)S(1)}, bf16[4,768,256]{2,1,0:T(8,128)(2,1)}, u32[]{:S(2)}) copy-start(bf16[4,768,256]{2,1,0:T(8,128)(2,1)} %constant.25.clone.refs_4_) | copy-start | bytes 4718596
  0.7 12.4 %copy-start.14 = (s32[16,2]{0,1:T(2,128)S(1)}, s32[16,2]{0,1:T(2,128)}, u32[]{:S(2)}) copy-start(s32[16,2]{0,1:T(2,128)} %param.11) | copy-start | bytes 388
  0.7 12.5 %copy-start.15 = (s32[128]{0:T(128)S(1)}, s32[128]{0:T(128)}, u32[]{:S(2)}) copy-start(s32[128]{0:T(128)} %param.12) | copy-start | bytes 1540
  2.7 26.7 %collective-permute-start = (f32[2,256,256]{2,1,0:T(8,128)}, f32[2,256,256]{2,1,0:T(8,128)}, u32[]{:S(2)}, u32[]{:S(2)}) collective-permute-start(f32[2,256,256]{2,1,0:T(8,128)} %slice.18), channel_id=1, source_target_pairs={{8,0},{16,8},{24,16},{32,24},{40,32},{48,40},{56,48},{64,56},{72,6... | collective-permute-start | bytes 1572872 | tf_op jit(solution)/shard_map/ppermute | solution.py:446
  7.4 31.8 %collective-permute-start.1 = (f32[2,512,256]{2,1,0:T(8,128)}, f32[2,512,256]{2,1,0:T(8,128)}, u32[]{:S(2)}, u32[]{:S(2)}) collective-permute-start(f32[2,512,256]{2,1,0:T(8,128)} %slice.19), channel_id=1, source_target_pairs={{1,0},{2,1},{3,2},{4,3},{5,4},{6,5},{7,6},{9,8},{10,9},{11,10},{12... | collective-permute-start | bytes 3145736 | tf_op jit(solution)/shard_map/ppermute | solution.py:446
  11.2 28.0 %collective-permute-start.2 = (f32[2,256,256]{2,1,0:T(8,128)}, f32[2,256,256]{2,1,0:T(8,128)}, u32[]{:S(2)}, u32[]{:S(2)}) collective-permute-start(f32[2,256,256]{2,1,0:T(8,128)} %slice.20), channel_id=1, source_target_pairs={{8,0},{16,8},{24,16},{32,24},{40,32},{48,40},{56,48},{64,56},{72,6... | collective-permute-start | bytes 1572872 | tf_op jit(solution)/shard_map/ppermute | solution.py:446
  13.9 1.0 copy-start.2
  29.5 12.7 %collective-permute-start.3 = (f32[2,256,256]{2,1,0:T(8,128)}, f32[2,256,256]{2,1,0:T(8,128)S(1)}, u32[]{:S(2)}, u32[]{:S(2)}) collective-permute-start(f32[2,256,256]{2,1,0:T(8,128)} %collective-permute-done.refs_10_), channel_id=1, source_target_pairs={{1,0},{2,1},{3,2},{4,3},{5,4},{6,5},{7,6},{9,8},{10,9},{11,10},{12... | collective-permute-start | bytes 1572872 | tf_op jit(solution)/shard_map/ppermute | solution.py:446
  37.3 28.5 %collective-permute-start.4 = (f32[2,256,256]{2,1,0:T(8,128)S(1)}, f32[2,256,256]{2,1,0:T(8,128)S(1)}, u32[]{:S(2)}, u32[]{:S(2)}) collective-permute-start(f32[2,256,256]{2,1,0:T(8,128)S(1)} %get-tuple-element.60), channel_id=1, source_target_pairs={{8,0},{16,8},{24,16},{32,24},{40,32},{48,40},{56,48},{64,56},{72,6... | collective-permute-start | bytes 1572872 | tf_op jit(solution)/shard_map/ppermute | solution.py:446
  58.9 1.1 copy-start.5
  60.0 94.6 %collective-permute-start.7 = (f32[2,512,256]{2,1,0:T(8,128)}, f32[2,512,256]{2,1,0:T(8,128)}, u32[]{:S(2)}, u32[]{:S(2)}) collective-permute-start(f32[2,512,256]{2,1,0:T(8,128)} %get-tuple-element.54), channel_id=1, source_target_pairs={{0,1},{1,2},{2,3},{3,4},{4,5},{5,6},{6,7},{8,9},{9,10},{10,11},{11... | collective-permute-start | bytes 3145736 | tf_op jit(solution)/shard_map/ppermute | solution.py:446
  61.9 18.5 %collective-permute-start.5 = (f32[2,256,256]{2,1,0:T(8,128)}, f32[2,256,256]{2,1,0:T(8,128)}, u32[]{:S(2)}, u32[]{:S(2)}) collective-permute-start(f32[2,256,256]{2,1,0:T(8,128)} %get-tuple-element.59), channel_id=1, source_target_pairs={{8,0},{16,8},{24,16},{32,24},{40,32},{48,40},{56,48},{64,56},{72,6... | collective-permute-start | bytes 1572872 | tf_op jit(solution)/shard_map/ppermute | solution.py:446
  63.9 18.2 %collective-permute-start.6 = (f32[2,256,256]{2,1,0:T(8,128)}, f32[2,256,256]{2,1,0:T(8,128)}, u32[]{:S(2)}, u32[]{:S(2)}) collective-permute-start(f32[2,256,256]{2,1,0:T(8,128)} %get-tuple-element.47), channel_id=1, source_target_pairs={{0,1},{1,2},{2,3},{3,4},{4,5},{5,6},{6,7},{8,9},{9,10},{10,11},{11... | collective-permute-start | bytes 1572872 | tf_op jit(solution)/shard_map/ppermute | solution.py:446
  65.8 16.3 %copy-start.3 = (f32[2,256,256]{2,1,0:T(8,128)S(1)}, f32[2,256,256]{2,1,0:T(8,128)}, u32[]{:S(2)}) copy-start(f32[2,256,256]{2,1,0:T(8,128)} %refs_3_.7) | copy-start | bytes 1572868
  71.6 0.8 copy-start.8
  72.4 0.8 copy-start.10
  73.2 22.4 %copy-start.6 = (f32[2,256,512]{2,1,0:T(8,128)}, f32[2,256,512]{2,1,0:T(8,128)S(1)}, u32[]{:S(2)}) copy-start(f32[2,256,512]{2,1,0:T(8,128)S(1)} %get-tuple-element.48.refs_15_.own3) | copy-start | bytes 3145732
  73.2 81.3 %collective-permute-start.8 = (f32[2,256,256]{2,1,0:T(8,128)}, f32[2,256,256]{2,1,0:T(8,128)}, u32[]{:S(2)}, u32[]{:S(2)}) collective-permute-start(f32[2,256,256]{2,1,0:T(8,128)} %get-tuple-element.56), channel_id=1, source_target_pairs={{0,8},{8,16},{16,24},{24,32},{32,40},{40,48},{48,56},{56,64},{64,7... | collective-permute-start | bytes 1572872 | tf_op jit(solution)/shard_map/ppermute | solution.py:446
  82.1 1.0 copy-start.9
  83.1 1.0 copy-start.11
  95.6 0.8 copy-start.7
  154.6 6.7 %copy-start.13 = (f32[2,256,256]{2,1,0:T(8,128)S(1)}, f32[2,256,256]{2,1,0:T(8,128)}, u32[]{:S(2)}) copy-start(f32[2,256,256]{2,1,0:T(8,128)} %get-tuple-element.65) | copy-start | bytes 1572868
  (1 other events, 0.6 us)

commit v3 on v2

--- a/solution.py
+++ b/solution.py
@@ -289,7 +289,18 @@
 NROW, NCOL = 16, 8
 
 
-def tail_kernel(visits, pacc, stats, halo, out, coeff, misfit, down, mine1, got1, mine2, got2, part, wide, s1, r1, s2, r2, s3, r3, s4, r4, s5, r5):
+def send(src, dst, ss, rs, peer):
+    copy = pltpu.make_async_remote_copy(src, dst, ss, rs, device_id=peer, device_id_type=MESH)
+    copy.start()
+    return copy
+
+
+def columns(k, n=1):
+    return pl.ds(k * H, n * H)
+
+
+def tail_kernel(visits, pacc, stats, halo, inner, edge, edge_low, out, coeff, misfit, down, came, mine1, got1, mine2, got2, part, wide,
+                turn, low, s1, r1, s2, r2, s3, r3, s4, r4, ss, rs, ls):
     row, col = lax.axis_index("row"), lax.axis_index("col")
 
     def col_peer(k):
@@ -303,6 +314,8 @@
         pl.semaphore_signal(barrier, inc=1, device_id=col_peer(k), device_id_type=MESH)
     for k in range(1, NROW):
         pl.semaphore_signal(barrier, inc=1, device_id=row_peer(k), device_id_type=MESH)
+    own = pltpu.make_async_copy(halo.at[:, :, columns(0, 2)], turn, ls)
+    own.start()
     for p in range(2):
         for b in range(2):
             for h in range(2):
@@ -310,25 +323,21 @@
                 mine1[piece, :H] = pacc[p, h * H : (h + 1) * H, b * H : (b + 1) * H]
                 mine1[piece, H:] = stats[:, :H] + stats[:, H:]
     pl.semaphore_wait(barrier, NCOL + NROW - 2)
-
-    def send(src, dst, ss, rs, peer):
-        copy = pltpu.make_async_remote_copy(src, dst, ss, rs, device_id=peer, device_id_type=MESH)
-        copy.start()
-        return copy
-
-    pieces = []
-
-    def send_pieces(n):
-        for _ in range(n):
-            k = len(pieces)
-            cols = pl.ds(k * H, H)
-            pieces.append(send(halo.at[:, :, cols], down.at[:, :, cols], s5.at[k], r5.at[k], row_peer(1)))
-
+    number = iter(range(32))
+
+    def go(src, dst, peer):
+        n = next(number)
+        return send(src, dst, ss.at[n], rs.at[n], peer)
+
+    def lower(k, n=1):
+        return go(halo.at[:, :, columns(k, n)], down.at[:, :, columns(k, n)], row_peer(1))
+
+    corner = go(edge_low, low, col_peer(1))
+    rest = [lower(5), lower(4)]
     copies = [
         send(mine1.at[lax.rem(col + k, NCOL)], got1.at[k - 1], s1.at[k - 1], r1.at[k - 1], col_peer(k))
         for k in range(1, NCOL)
     ]
-    send_pieces(2)
     for copy in copies:
         copy.wait()
     total = mine1[col]
@@ -341,7 +350,14 @@
         send(mine2.at[lax.rem(row + k, NROW)], got2.at[k - 1], s2.at[k - 1], r2.at[k - 1], row_peer(k))
         for k in range(1, NROW)
     ]
-    send_pieces(1)
+    rest += [
+        go(inner.at[:, pl.ds(0, M), columns(8, 2)], came.at[:, pl.ds(0, M)], col_peer(1)),
+        go(edge, came.at[:, pl.ds(M, M)], col_peer(1)),
+        lower(3),
+    ]
+    own.wait()
+    corner.wait_recv()
+    turn[...] += jnp.where(col > 0, low[...], 0.0)
     for copy in copies:
         copy.wait()
     total = mine2[row]
@@ -354,32 +370,38 @@
     misfit[...] = jnp.full((8, H), jnp.sum(total[8:16])) / (mean * mean * pixels)
     part[row] = total[:8] * (factor / visits[0])
     copies = [send(part.at[row], part.at[row], s3.at[k - 1], r3.at[k - 1], row_peer(k)) for k in range(1, NROW)]
-    send_pieces(1)
+    rest.append(lower(2))
     for copy in copies:
         copy.wait()
     copies = [send(part, wide.at[col], s4.at[k - 1], r4.at[k - 1], col_peer(k)) for k in range(1, NCOL)]
-    send_pieces(2)
+    rest.append(go(turn, down.at[:, :, columns(0, 2)], row_peer(1)))
     wide[col] = part[...]
-    for copy in copies + pieces:
+    for copy in copies:
         copy.wait()
     for p in range(2):
         for b in range(2):
             for h in range(2):
                 out[p, h * H : (h + 1) * H, b * H : (b + 1) * H] = wide[4 * p + 2 * b + h].reshape(H, H)
-
-
-def tail(visits, pacc, stats, halo):
+    corner.wait_send()
+    for copy in rest:
+        copy.wait()
+
+
+def tail(visits, pacc, stats, halo, inner, edge, edge_low):
     vm = pl.BlockSpec(memory_space=pltpu.VMEM)
     sm = pl.BlockSpec(memory_space=pltpu.SMEM)
-    sems = [pltpu.SemaphoreType.DMA((n,)) for n in (NCOL - 1, NCOL - 1, NROW - 1, NROW - 1, NROW - 1, NROW - 1, NCOL - 1, NCOL - 1, 6, 6)]
     hbm = pl.BlockSpec(memory_space=pl.ANY)
+    numbers = (NCOL - 1, NCOL - 1, NROW - 1, NROW - 1, NROW - 1, NROW - 1, NCOL - 1, NCOL - 1, 8, 8)
     tile = jax.ShapeDtypeStruct((8, H), F32)
     return pl.pallas_call(
         tail_kernel,
         name="tail",
-        out_shape=[jax.ShapeDtypeStruct((2, M, M), F32), tile, tile, jax.ShapeDtypeStruct((2, M, 768), F32)],
-        in_specs=[sm, vm, vm, hbm],
-        out_specs=[vm, vm, vm, hbm],
+        out_shape=[
+            jax.ShapeDtypeStruct((2, M, M), F32), tile, tile,
+            jax.ShapeDtypeStruct((2, M, 768), F32), jax.ShapeDtypeStruct((2, 512, M), F32),
+        ],
+        in_specs=[sm, vm, vm, hbm, hbm, hbm, hbm],
+        out_specs=[vm, vm, vm, hbm, hbm],
         scratch_shapes=[
             pltpu.VMEM((NCOL, H + 16, H), F32),
             pltpu.VMEM((NCOL - 1, H + 16, H), F32),
@@ -387,57 +409,77 @@
             pltpu.VMEM((NROW - 1, 24, H), F32),
             pltpu.VMEM((NROW, 8, H), F32),
             pltpu.VMEM((NCOL, NROW, 8, H), F32),
+            pltpu.VMEM((2, M, M), F32),
+            pltpu.VMEM((2, M, M), F32),
         ]
-        + sems,
-        compiler_params=pltpu.CompilerParams(collective_id=0, has_side_effects=True),
-        cost_estimate=pl.CostEstimate(flops=10**6, bytes_accessed=1 << 20, transcendentals=0),
-    )(visits, pacc, stats, halo)
-
-
-def finish_kernel(upper, coeff, inner, own12, own4, own3, right, down12, down3, out):
-    k = pl.program_id(0)
+        + [pltpu.SemaphoreType.DMA((n,)) for n in numbers]
+        + [pltpu.SemaphoreType.DMA],
+        compiler_params=pltpu.CompilerParams(collective_id=0, has_side_effects=True, vmem_limit_bytes=32 << 20),
+        cost_estimate=pl.CostEstimate(flops=40 * 10**9, bytes_accessed=1 << 20, transcendentals=0),
+    )(visits, pacc, stats, halo, inner, edge, edge_low)
+
+
+def finish_kernel(inside, coeff, misfit, probe, inner, own12, own3, came, down12, down3, out, probe_out, misfit_out,
+                  tile, down, right, ins, outs):
+    top, bottom = pl.ds(0, M), pl.ds(M, M)
+    copies = []
+    for k in range(4):
+        cols, at = columns(2 * k, 2), columns(2 * (k % 3), 2)
+        pairs = [
+            (inner.at[:, top, cols], tile.at[:, top, cols]),
+            ((own12 if k < 3 else own3).at[:, :, at], tile.at[:, bottom, cols]),
+            ((down12 if k < 3 else down3).at[:, :, at], down.at[:, :, cols]),
+        ]
+        if k == 0:
+            pairs.append((came, right))
+        copies.append([pltpu.make_async_copy(src, dst, ins.at[k, n]) for n, (src, dst) in enumerate(pairs)])
+    for copy in copies[1] + copies[2] + copies[3] + copies[0]:
+        copy.start()
+    probe_out[...] = probe[...]
+    misfit_out[...] = misfit[0:1, 0:1]
     factor = coeff[0:1, 0:1]
-
-    @pl.when(k < 3)
-    def _():
-        out[:, :M] = (inner[:, :M] + jnp.where(upper[0] > 0, down12[...], 0.0)) * factor
-        out[:, M:] = own12[...] * factor
-
-    @pl.when(k < 2)
-    def _():
-        out[:, M:] += inner[:, M:] * factor
-
-    @pl.when(k == 3)
-    def _():
-        out[:, :M] = (own4[...] + down3[...]) * factor
-        out[:, M:] = own3[...] * factor
-
-    @pl.when(k == 0)
-    def _():
-        out[...] += right[...] * factor
-
-
-def finished(upper, coeff, inner, own12, own4, own3, right, down12, down3):
-    block = lambda index: pl.BlockSpec((2, M, M), index)
+    ends = []
+    for k in (1, 2, 3, 0):
+        cols = columns(2 * k, 2)
+        for copy in copies[k]:
+            copy.wait()
+        came_down = down[:, :, cols] if k == 3 else jnp.where(inside[0] > 0, down[:, :, cols], 0.0)
+        upper, lower = tile[:, top, cols] + came_down, tile[:, bottom, cols]
+        if k == 0:
+            upper = upper + jnp.where(inside[1] > 0, right[:, top], 0.0)
+            lower = lower + jnp.where(inside[1] > 0, right[:, bottom], 0.0)
+        tile[:, top, cols] = upper * factor
+        tile[:, bottom, cols] = lower * factor
+        ends.append(pltpu.make_async_copy(tile.at[:, :, cols], out.at[:, :, cols], outs.at[k]))
+        ends[-1].start()
+    for copy in ends:
+        copy.wait()
+
+
+def finished(inside, coeff, misfit, probe, inner, own12, own3, came, down12, down3):
+    vm = pl.BlockSpec(memory_space=pltpu.VMEM)
+    sm = pl.BlockSpec(memory_space=pltpu.SMEM)
+    hbm = pl.BlockSpec(memory_space=pl.ANY)
     return pl.pallas_call(
         finish_kernel,
         name="finished",
-        grid=(4,),
-        out_shape=jax.ShapeDtypeStruct((2, 512, 1024), F32),
-        in_specs=[
-            pl.BlockSpec(memory_space=pltpu.SMEM),
-            pl.BlockSpec(memory_space=pltpu.VMEM),
-            pl.BlockSpec((2, 512, M), lambda k: (0, 0, jnp.minimum(k, 2))),
-            block(lambda k: (0, 0, jnp.minimum(k, 2))),
-            block(lambda k: (0, 0, 0)),
-            block(lambda k: (0, 0, 1)),
-            pl.BlockSpec((2, 512, M), lambda k: (0, 0, 0)),
-            block(lambda k: (0, 0, jnp.minimum(k, 2))),
-            block(lambda k: (0, 0, 0)),
+        out_shape=[
+            jax.ShapeDtypeStruct((2, 512, 1024), F32),
+            jax.ShapeDtypeStruct((2, M, M), F32),
+            jax.ShapeDtypeStruct((1, 1), F32),
         ],
-        out_specs=pl.BlockSpec((2, 512, M), lambda k: (0, 0, k)),
+        in_specs=[sm, vm, vm, vm] + [hbm] * 6,
+        out_specs=[hbm, vm, vm],
+        scratch_shapes=[
+            pltpu.VMEM((2, 512, 1024), F32),
+            pltpu.VMEM((2, M, 1024), F32),
+            pltpu.VMEM((2, 512, M), F32),
+            pltpu.SemaphoreType.DMA((4, 4)),
+            pltpu.SemaphoreType.DMA((4,)),
+        ],
+        compiler_params=pltpu.CompilerParams(vmem_limit_bytes=32 << 20),
         cost_estimate=pl.CostEstimate(flops=10**7, bytes_accessed=10 << 20, transcendentals=0),
-    )(upper, coeff, inner, own12, own4, own3, right, down12, down3)
+    )(inside, coeff, misfit, probe, inner, own12, own3, came, down12, down3)
 
 
 def passed_along(value, axis, steps):
@@ -447,55 +489,43 @@
 
 
 def body(sample, probe, patterns, positions, counts):
-    tile_rows, tile_cols = sample.shape[1:]
     row_at, col_at = lax.axis_index("row"), lax.axis_index("col")
-    own = counts[row_at * NCOL + col_at]
-    pos = positions - jnp.stack([row_at * tile_rows, col_at * tile_cols])[None, :]
-    count = own.reshape(1)
+    first = sample[:, :M, :M]
+    later, first = lax.optimization_barrier((sample, first))
+    low0 = passed_along(first, "row", -1)
+    low32 = passed_along(later[:, :M, 512:], "row", -1)
+    low1 = passed_along(later[:, :M, M:512], "row", -1)
+    right = passed_along(later[:, :, :M], "col", -1)
+    pos = positions - jnp.stack([row_at * 512, col_at * 1024])[None, :]
+    count = counts[row_at * NCOL + col_at].reshape(1)
     visits = jnp.sum(counts).astype(F32).reshape(1)
-    tables = tuple(jnp.asarray(t) for t in dft_tables())
-    args = (pos, count, patterns, probe, tables)
-    chunk = lambda k: sample[:, :M, k * M : (k + 1) * M]
-    first = chunk(0)
-    sample, first = lax.optimization_barrier((sample, first))
-    low = [passed_along(first, "row", -1), None, None, passed_along(chunk(3), "row", -1)]
-    right = passed_along(sample[:, :, :M], "col", -1)
+    inside = jnp.stack([row_at > 0, col_at > 0]).astype(jnp.int32)
+    args = (pos, count, patterns, probe, tuple(jnp.asarray(t) for t in dft_tables()))
     (inner,), sums = windows(
-        "windows_inside", *args, (),
-        [(sample, 0, 0, 512, 1024, 0, 0)], [], [(0, 512, 1024, 0)],
-        8, 512, 0, 0, lambda o, c: (o <= M) & (c < 768),
+        "windows_upper", *args, (),
+        [(sample, 0, 0, 512, 1024, 0, 0), (right, 0, 0, 512, M, 0, 8)], [], [(0, 512, 1280, 0)],
+        10, 512, 0, 0, lambda o, c: o <= M,
     )
-    sums, next_low, sample = lax.optimization_barrier((sums, low[0], sample))
-    low[2] = passed_along(chunk(2), "row", -1)
-    low[1] = passed_along(chunk(1), "row", -1)
-    corner = passed_along(next_low, "col", -1)
-    (own4, edge, edge_low, part3), sums = windows(
+    sums, low0 = lax.optimization_barrier((sums, low0))
+    corner = passed_along(low0, "col", -1)
+    (own3, halo3, part2, bottom2, edge, edge_low), sums = windows(
         "windows_right", *args, sums,
-        [(sample, 0, 768, 512, M, 0, 0), (right, 0, 0, 512, M, 0, 2), (low[3], 0, 0, M, M, 512, 0), (corner, 0, 0, M, M, 512, 2)],
-        [(inner, 0, 768, 512, M, 0, 0)], [(0, 512, M, 0), (0, 512, M, 2), (512, M, M, 2), (512, M, M, 0)],
-        4, 768, 0, 768, lambda o, c: c >= 768,
-    )
-    low_right = passed_along(edge_low, "col", 1)
-    came_right = passed_along(edge, "col", 1)
-    (own3, halo3, part2), sums = windows(
-        "windows_third", *args, sums,
-        [(sample, M, 512, M, 512, 0, 0), (low[2], 0, 0, M, M, M, 0), (low[3], 0, 0, M, M, M, 2)],
-        [(part3, 0, 0, M, M, M, 2), (own4, M, 0, M, M, 0, 2), (inner, M, 512, M, M, 0, 0)],
-        [(0, M, 512, 0), (M, M, M, 2), (M, M, M, 0)],
-        4, 512, M, 512, lambda o, c: (o > M) & (c >= 512) & (c < 768),
+        [(sample, M, 512, M, 512, 0, 0), (right, M, 0, M, M, 0, 4), (low32, 0, 0, M, 512, M, 0), (corner, 0, 0, M, M, M, 4)],
+        [(inner, M, 512, M, 768, 0, 0)],
+        [(0, M, M, 2), (M, M, M, 2), (M, M, M, 0), (0, M, M, 0), (0, M, M, 4), (M, M, M, 4)],
+        6, 512, M, 512, lambda o, c: (o > M) & (c >= 512),
     )
     down3 = passed_along(halo3, "row", 1)
     (own12, halo12), sums = windows(
         "windows_left", *args, sums,
-        [(sample, M, 0, M, 768, 0, 0), (low[0], 0, 0, M, M, M, 0), (low[1], 0, 0, M, M, M, 2), (low[2], 0, 0, M, M, M, 4)],
-        [(part2, 0, 0, M, M, M, 4), (low_right, 0, 0, M, M, M, 0), (own3, 0, 0, M, M, 0, 4)],
+        [(sample, M, 0, M, 768, 0, 0), (low0, 0, 0, M, M, M, 0), (low1, 0, 0, M, M, M, 2), (low32, 0, 0, M, M, M, 4)],
+        [(part2, 0, 0, M, M, M, 4), (bottom2, 0, 0, M, M, 0, 4), (inner, M, 0, M, 512, 0, 0)],
         [(0, M, 768, 0), (M, M, 768, 0)],
         6, 512, M, 0, lambda o, c: (o > M) & (c < 512),
     )
-    probe_grad, coeff, misfit, down12 = tail(visits, *sums, halo12)
-    upper = (row_at > 0).astype(jnp.int32).reshape(1)
-    object_grad = finished(upper, coeff, inner, own12, own4, own3, came_right, down12, down3)
-    return object_grad, probe_grad, misfit[0, 0]
+    probe_sum, coeff, misfit, down12, came = tail(visits, *sums, halo12, inner, edge, edge_low)
+    object_grad, probe_grad, mean_misfit = finished(inside, coeff, misfit, probe_sum, inner, own12, own3, came, down12, down3)
+    return object_grad, probe_grad, mean_misfit.reshape(())
 
 
 def solution(mesh):

time: 163 us -> 137 us (0.84)
  the two profiles are of different devices: /device:TPU:14 before, /device:TPU:1 now
where the time goes in v3:
time: 137 us
  Pallas kernels  96.3 us (70%)
  local copies, waits for them, and re-layouts  14.5 us (11%)
  waiting for transfers between devices  12.8 us (9%)
  starting transfers between devices  10.5 us (8%)
  between operations  1.63 us (1%)
    pallas_call x1, Pallas kernels, tail(): pl.pallas_call(tail_kernel, name='tail', out_shape=[jax.ShapeDtypeStruct(...  50.2 us
    pallas_call x3, Pallas kernels, windows(): pl.pallas_call(kernel, name=name, out_shape=[jax.ShapeDtypeStruct((2, nr,...  41.5 us
    ppermute x6, waiting for transfers between devices, passed_along(): lax.ppermute(value, axis, [(source, source + steps) for source in range(f...  12.8 us
    ppermute x6, starting transfers between devices, passed_along(): lax.ppermute(value, axis, [(source, source + steps) for source in range(f...  10.5 us
    unnamed x27, local copies, waits for them, and re-layouts  5.42 us
    pallas_call x1, Pallas kernels, finished(): pl.pallas_call(finish_kernel, name='finished', out_shape=[jax.ShapeDtypeS...  4.67 us
  transfers between devices with their start and end apart: 6, of which 2 were waited for; matrix products, arithmetic and copies ran while one was open for 4% of the time, Pallas kernels for 67%

profile of v3, /device:TPU:1, one launch (start us, length us, event | category | flops | bytes accessed | tf_op | source)
XLA Modules:
  0.0 136.6 jit_solution(17335159681280629387)
XLA Ops:
  0.6 1.9 %slice.12 = f32[2,256,256]{2,1,0:T(8,128)} slice(f32[2,512,1024]{2,1,0:T(8,128)} %refs_9_.3), slice={[0:2], [0:256], [0:256]} | slice | bytes 1048576 | tf_op jit(solution)/shard_map/slice | solution.py:493
  2.5 2.4 %slice.13 = f32[2,512,256]{2,1,0:T(8,128)} slice(f32[2,512,1024]{2,1,0:T(8,128)} %refs_9_.3), slice={[0:2], [0:512], [0:256]} | slice | bytes 2097152 | tf_op jit(solution)/shard_map/slice | solution.py:498
  4.9 3.5 %collective-permute-start = (f32[2,512,256]{2,1,0:T(8,128)}, f32[2,512,256]{2,1,0:T(8,128)}, u32[]{:S(2)}, u32[]{:S(2)}) collective-permute-start(f32[2,512,256]{2,1,0:T(8,128)} %slice.13), channel_id=1, source_target_pairs={{1,0},{2,1},{3,2},{4,3},{5,4},{6,5},{7,6},{9,8},{10,9},{11,10},{12... | collective-permute-start | bytes 3145736 | tf_op jit(solution)/shard_map/ppermute | solution.py:488
  8.4 1.3 collective-permute-start.1
  9.7 2.3 %slice.14 = f32[2,256,512]{2,1,0:T(8,128)} slice(f32[2,512,1024]{2,1,0:T(8,128)} %refs_9_.3), slice={[0:2], [0:256], [512:1024]} | slice | bytes 2097152 | tf_op jit(solution)/shard_map/slice | solution.py:496
  12.0 1.3 collective-permute-start.2
  13.4 0.6 dynamic_slice.3.refs_1_
  14.1 8.5 %collective-permute-done.refs_8_.refs_10_ = f32[2,512,256]{2,1,0:T(8,128)} collective-permute-done((f32[2,512,256]{2,1,0:T(8,128)}, f32[2,512,256]{2,1,0:T(8,128)}, u32[]{:S(2)}, u32[]{:S(2)}) %collective-permute-start) | collective-permute-done | bytes 1048608 | tf_op jit(solution)/shard_map/ppermute | solution.py:488
  22.7 1.0 copy-done.2
  23.7 20.8 %windows_upper.1 = (f32[2,512,1280]{2,1,0:T(8,128)}, f32[2,256,256]{2,1,0:T(8,128)S(1)}, f32[16,256]{1,0:T(8,128)S(1)}) custom-call(s32[16,2]{1,0:T(8,128)S(1)} %broadcast_subtract_fusion.refs_0_, s32[1]{0:T(128)} %dynamic_slice.3.refs_1_, f32[16,256,256]{2,1,0:T(8,128)} %refs_2_.5, f32[2,256,256]{2,1,0:T(8,128)S(1)} %copy-done.2, ...), custom_call_target="tpu_custom_call" | custom-call | flops 8 | bytes 1024 | tf_op jit(solution)/shard_map/windows_upper/pallas_call | solution.py:265
  44.6 0.8 copy-done.6
  45.3 1.9 %collective-permute-start.3 = (f32[2,256,256]{2,1,0:T(8,128)}, f32[2,256,256]{2,1,0:T(8,128)S(1)}, u32[]{:S(2)}, u32[]{:S(2)}) collective-permute-start(f32[2,256,256]{2,1,0:T(8,128)} %collective-permute-done.1.refs_10_), channel_id=1, source_target_pairs={{1,0},{2,1},{3,2},{4,3},{5,4},{6,5},{7,6},{9,8},{10,9},{11,10},{12... | collective-permute-start | bytes 1572872 | tf_op jit(solution)/shard_map/ppermute | solution.py:488
  47.3 1.9 %slice.15 = f32[2,256,256]{2,1,0:T(8,128)} slice(f32[2,512,1024]{2,1,0:T(8,128)} %refs_9_.3), slice={[0:2], [0:256], [256:512]} | slice | bytes 1048576 | tf_op jit(solution)/shard_map/slice | solution.py:497
  49.2 1.3 collective-permute-start.4
  50.4 0.7 reduce_sum.9
  51.8 4.2 %collective-permute-done.3.refs_12_ = f32[2,256,256]{2,1,0:T(8,128)S(1)} collective-permute-done((f32[2,256,256]{2,1,0:T(8,128)}, f32[2,256,256]{2,1,0:T(8,128)S(1)}, u32[]{:S(2)}, u32[]{:S(2)}) %collective-permute-start.3) | collective-permute-done | bytes 524320 | tf_op jit(solution)/shard_map/ppermute | solution.py:488
  56.1 1.0 copy-done.3
  57.1 1.0 copy-done.7
  58.1 10.5 %windows_right.1 = (f32[2,256,256]{2,1,0:T(8,128)S(1)}, f32[2,256,256]{2,1,0:T(8,128)S(1)}, f32[2,256,256]{2,1,0:T(8,128)S(1)}, f32[2,256,256]{2,1,0:T(8,128)S(1...) custom-call(s32[16,2]{1,0:T(8,128)S(1)} %broadcast_subtract_fusion.r, ...), custom_call_target="tpu_custom_call" | custom-call | flops 8 | bytes 1024 | tf_op jit(solution)/shard_map/windows_right/pallas_call | solution.py:265
  68.6 1.3 collective-permute-start.5
  70.0 10.1 %windows_left.1 = (f32[2,256,768]{2,1,0:T(8,128)}, f32[2,256,768]{2,1,0:T(8,128)}, f32[2,256,256]{2,1,0:T(8,128)S(1)}, f32[16,256]{1,0:T(8,128)S(1)}) custom-call(s32[16,2]{1,0:T(8,128)S(1)} %broadcast_subtract_fusion.refs_0_, s32[1]{0:T(128)} %dynamic_slice.3.refs_1_, f32[16,256,256]{2,1,0:T(8,128)} %refs_2_.5, f32[2,256,256]{2,1,0:T(8,128)S(1)} %copy-done.3, ...), custom_call_target="tpu_custom_call" | custom-call | flops 8 | bytes 1024 | tf_op jit(solution)/shard_map/windows_left/pallas_call | solution.py:265
  80.1 1.4 %copy-done.8 = f32[2,256,768]{2,1,0:T(8,128)S(1)} copy-done((f32[2,256,768]{2,1,0:T(8,128)S(1)}, f32[2,256,768]{2,1,0:T(8,128)}, u32[]{:S(2)}) %copy-start.8) | copy-done | bytes 1572888
  81.5 50.2 %tail.1 = (f32[2,256,256]{2,1,0:T(8,128)S(1)}, f32[8,128]{1,0:T(8,128)S(1)}, f32[8,128]{1,0:T(8,128)S(1)}, f32[2,256,768]{2,1,0:T(8,128)S(1)}, f32[2,512,256]{2,1,0:T(8,128)S(1)}) custom-call(f32[1]{0:T(128)} %bitcast.2.visits, f32[2,256,256]{2,1,0:T(8,128)S(1)} %get-tuple-element.43.pacc, f32[16,256]{1,0:T(8,128)S(1)} %get-tuple-element.44.stats, ...), custom_call_target="tpu_custom_call" | custom-call | flops 40000000000 | bytes 1048576 | tf_op jit(solution)/shard_map/tail/pallas_call | solution.py:396
  131.8 4.7 %finished.1 = (f32[2,512,1024]{2,1,0:T(8,128)}, f32[2,256,256]{2,1,0:T(8,128)}, f32[1,1]{1,0:T(1,128)}) custom-call(s32[2]{0:T(128)S(1)} %add_convert_fusion.inside, f32[8,128]{1,0:T(8,128)S(1)} %get-tuple-element.48.coeff, f32[8,128]{1,0:T(8,128)S(1)} %get-tuple-element.49.misfit, f32[2,256,256]{2,1,0:T(8,128)S(1)} %get-tuple-element.50.probe, ...), custom_call_target="tpu_custom_call" | custom-call | flops 10000000 | bytes 10485760 | tf_op jit(solution)/shard_map/finished/pallas_call | solution.py:463
  (30 shorter events, 0.3 us)
Async XLA Ops:
  2.5 20.1 %copy-start.1 = (bf16[4,768,256]{2,1,0:T(8,128)(2,1)S(1)}, bf16[4,768,256]{2,1,0:T(8,128)(2,1)}, u32[]{:S(2)}) copy-start(bf16[4,768,256]{2,1,0:T(8,128)(2,1)} %constant.25.clone.refs_4_) | copy-start | bytes 4718596
  4.9 8.4 %copy-start.9 = (s32[16,2]{0,1:T(2,128)S(1)}, s32[16,2]{0,1:T(2,128)}, u32[]{:S(2)}) copy-start(s32[16,2]{0,1:T(2,128)} %param.11) | copy-start | bytes 388
  4.9 8.5 %copy-start.10 = (s32[128]{0:T(128)S(1)}, s32[128]{0:T(128)}, u32[]{:S(2)}) copy-start(s32[128]{0:T(128)} %param.12) | copy-start | bytes 1540
  4.9 17.7 %copy-start = (bf16[4,256,768]{2,1,0:T(8,128)(2,1)S(1)}, bf16[4,256,768]{2,1,0:T(8,128)(2,1)}, u32[]{:S(2)}) copy-start(bf16[4,256,768]{2,1,0:T(8,128)(2,1)} %constant.26.clone.refs_5_) | copy-start | bytes 4718596
  4.9 17.7 %copy-start.4 = (bf16[512,256]{1,0:T(8,128)(2,1)S(1)}, bf16[512,256]{1,0:T(8,128)(2,1)}, u32[]{:S(2)}) copy-start(bf16[512,256]{1,0:T(8,128)(2,1)} %constant.27.clone.refs_6_) | copy-start | bytes 786436
  4.9 17.7 %collective-permute-start = (f32[2,512,256]{2,1,0:T(8,128)}, f32[2,512,256]{2,1,0:T(8,128)}, u32[]{:S(2)}, u32[]{:S(2)}) collective-permute-start(f32[2,512,256]{2,1,0:T(8,128)} %slice.13), channel_id=1, source_target_pairs={{1,0},{2,1},{3,2},{4,3},{5,4},{6,5},{7,6},{9,8},{10,9},{11,10},{12... | collective-permute-start | bytes 3145736 | tf_op jit(solution)/shard_map/ppermute | solution.py:488
  8.4 37.0 %collective-permute-start.1 = (f32[2,256,256]{2,1,0:T(8,128)}, f32[2,256,256]{2,1,0:T(8,128)}, u32[]{:S(2)}, u32[]{:S(2)}) collective-permute-start(f32[2,256,256]{2,1,0:T(8,128)} %slice.12), channel_id=1, source_target_pairs={{8,0},{16,8},{24,16},{32,24},{40,32},{48,40},{56,48},{64,56},{72,6... | collective-permute-start | bytes 1572872 | tf_op jit(solution)/shard_map/ppermute | solution.py:488
  12.0 39.8 %collective-permute-start.2 = (f32[2,256,512]{2,1,0:T(8,128)}, f32[2,256,512]{2,1,0:T(8,128)}, u32[]{:S(2)}, u32[]{:S(2)}) collective-permute-start(f32[2,256,512]{2,1,0:T(8,128)} %slice.14), channel_id=1, source_target_pairs={{8,0},{16,8},{24,16},{32,24},{40,32},{48,40},{56,48},{64,56},{72,6... | collective-permute-start | bytes 3145736 | tf_op jit(solution)/shard_map/ppermute | solution.py:488
  22.6 1.0 copy-start.2
  44.5 0.8 copy-start.6
  45.3 10.7 %collective-permute-start.3 = (f32[2,256,256]{2,1,0:T(8,128)}, f32[2,256,256]{2,1,0:T(8,128)S(1)}, u32[]{:S(2)}, u32[]{:S(2)}) collective-permute-start(f32[2,256,256]{2,1,0:T(8,128)} %collective-permute-done.1.refs_10_), channel_id=1, source_target_pairs={{1,0},{2,1},{3,2},{4,3},{5,4},{6,5},{7,6},{9,8},{10,9},{11,10},{12... | collective-permute-start | bytes 1572872 | tf_op jit(solution)/shard_map/ppermute | solution.py:488
  49.2 20.8 %collective-permute-start.4 = (f32[2,256,256]{2,1,0:T(8,128)}, f32[2,256,256]{2,1,0:T(8,128)S(1)}, u32[]{:S(2)}, u32[]{:S(2)}) collective-permute-start(f32[2,256,256]{2,1,0:T(8,128)} %slice.15), channel_id=1, source_target_pairs={{8,0},{16,8},{24,16},{32,24},{40,32},{48,40},{56,48},{64,56},{72,6... | collective-permute-start | bytes 1572872 | tf_op jit(solution)/shard_map/ppermute | solution.py:488
  56.0 1.0 copy-start.3
  57.1 1.0 copy-start.7
  58.1 22.0 %slice-start = ((s8[5242880]{0:T(1024)(128)(4,1)}), s8[1048576]{0:T(1024)(128)(4,1)S(1)}, s32[]{:S(2)}) async-start(s8[5242880]{0:T(1024)(128)(4,1)} %bitcast.6), calls=%async_computation | async-start | bytes 2097152
  68.6 63.1 %collective-permute-start.5 = (f32[2,256,256]{2,1,0:T(8,128)S(1)}, f32[2,256,256]{2,1,0:T(8,128)S(1)}, u32[]{:S(2)}, u32[]{:S(2)}) collective-permute-start(f32[2,256,256]{2,1,0:T(8,128)S(1)} %get-tuple-element.55), channel_id=1, source_target_pairs={{0,8},{8,16},{16,24},{24,32},{32,40},{40,48},{48,56},{56,64},{64,7... | collective-permute-start | bytes 1572872 | tf_op jit(solution)/shard_map/ppermute | solution.py:488
  70.0 10.1 %slice-start.1 = ((s8[5242880]{0:T(1024)(128)(4,1)}), s8[4194304]{0:T(1024)(128)(4,1)S(1)}, s32[]{:S(2)}) async-start(s8[5242880]{0:T(1024)(128)(4,1)} %bitcast.6), calls=%async_computation.1 | async-start | bytes 8388608
  80.1 1.4 %copy-start.8 = (f32[2,256,768]{2,1,0:T(8,128)S(1)}, f32[2,256,768]{2,1,0:T(8,128)}, u32[]{:S(2)}) copy-start(f32[2,256,768]{2,1,0:T(8,128)} %get-tuple-element.45.halo) | copy-start | bytes 4718596
  81.5 50.2 %copy-start.5 = (f32[2,256,768]{2,1,0:T(8,128)S(1)}, f32[2,256,768]{2,1,0:T(8,128)}, u32[]{:S(2)}) copy-start(f32[2,256,768]{2,1,0:T(8,128)} %get-tuple-element.51.own12) | copy-start | bytes 4718596

commit v4 on v3

v4 whole, which is shorter than its diff:
```python
import math

import jax
import jax.numpy as jnp
import numpy as np
from jax import lax
from jax.experimental import pallas as pl
from jax.experimental.pallas import tpu as pltpu
from jax.sharding import PartitionSpec as P

F32 = jnp.float32
BF16 = jnp.bfloat16
M = 256
H = 128
CAP = 16
SIDE = 2
LAG = 0


def dft_tables():
    n = np.arange(H)[:, None]
    m = np.arange(H)[None, :]
    right, left = [], []
    for sign in (-1.0, 1.0):
        for odd in (0, 1):
            if sign < 0:
                angle = 2 * math.pi * (n * (2 * m + odd) % M) / M
            else:
                angle = 2 * math.pi * ((2 * n + odd) * m % M) / M
            re, im = np.cos(angle) / 16.0, sign * np.sin(angle) / 16.0
            right.append(np.block([[re, im], [-im, re]]))
            left.append(right[-1].T)
    order = np.zeros((M, M), np.float32)
    k = np.arange(M)
    order[k, k // 2 + H * (k % 2)] = 1.0
    return np.stack(right).astype(np.float32), np.stack(left).astype(np.float32), order


def split(value):
    high = value.astype(BF16)
    return high, (value - high.astype(F32)).astype(BF16)


def dot(a, b):
    return jnp.dot(a, b, preferred_element_type=F32)


def right_dot(value, table):
    high, low = split(value)
    return dot(high, table[0]) + dot(low, table[0]) + dot(high, table[1])


def left_dot(table, value):
    high, low = split(value)
    return dot(table[0], high) + dot(table[0], low) + dot(table[1], high)


def lanes(a, b):
    return jnp.concatenate([a, b], axis=1)


def rows(*parts):
    return jnp.concatenate(parts, axis=0)


def one_window(spot, ext, acc, probe, right, left, order, pacc, stats, rolled, patch):
    top, j0, dc, pat = spot
    lane = lax.broadcasted_iota(jnp.int32, (M, H), 1)
    mask = lane >= dc
    at = pl.ds(top, M)

    def turned(a, b, shift, keep):
        a, b = pltpu.roll(a, shift, 1), pltpu.roll(b, shift, 1)
        return jnp.where(keep, a, b), jnp.where(keep, b, a)

    for p in range(2):
        a, b = turned(probe[p, :, :H], probe[p, :, H:], dc, mask)
        rolled[p, :, :H] = a
        rolled[p, :, H:] = b
        patch[p, :, :H] = jnp.where(mask, ext[p, j0, at, :], ext[p, j0 + 2, at, :])
        patch[p, :, H:] = ext[p, j0 + 1, at, :]
    wave_re = rolled[0] * patch[0] - rolled[1] * patch[1]
    wave_im = rolled[0] * patch[1] + rolled[1] * patch[0]
    sums = lanes(wave_re[:, :H] + wave_re[:, H:], wave_im[:, :H] + wave_im[:, H:])
    difs = lanes(wave_re[:, :H] - wave_re[:, H:], wave_im[:, :H] - wave_im[:, H:])
    yield
    even = right_dot(sums, right[0])
    odd = right_dot(difs, right[1])
    yield
    halves = ((even[:H] + even[H:], odd[:H] + odd[H:]), (even[:H] - even[H:], odd[:H] - odd[H:]))
    fars, levels = [], []
    for parity, (e, o) in enumerate(halves):
        fars.append(left_dot(left[parity], rows(lanes(e[:, :H], o[:, :H]), lanes(e[:, H:], o[:, H:]))))
        every = pl.ds(parity, H, 2)
        level = lanes(pat[0, every, :], pat[1, every, :])
        stats[8:] += jnp.sum(level.reshape(16, 8, M), axis=0)
        high, low = split(level)
        levels.append(dot(high, order[...]) + dot(low, order[...]))
        yield
    back = []
    for parity, far in enumerate(fars):
        far_re, far_im = far[:H], far[H:]
        resid = far_re * far_re + far_im * far_im - levels[parity]
        stats[:8] += jnp.sum((resid * resid).reshape(16, 8, M), axis=0)
        back.append(left_dot(left[2 + parity], rows(resid * far_re, resid * far_im)))
        yield
    half_s, half_d = back[0] + back[1], back[0] - back[1]
    re, im = rows(half_s[:H], half_d[:H]), rows(half_s[H:], half_d[H:])
    even = right_dot(lanes(re[:, :H], im[:, :H]), right[2])
    odd = right_dot(lanes(re[:, H:], im[:, H:]), right[3])
    yield
    first, second = even + odd, even - odd
    back_re = lanes(first[:, :H], second[:, :H])
    back_im = lanes(first[:, H:], second[:, H:])
    unmask = lane < H - dc
    undo = lax.rem(H - dc, H)
    for p in range(2):
        if p == 0:
            update = rolled[0] * back_re + rolled[1] * back_im
            grad = patch[0] * back_re + patch[1] * back_im
        else:
            update = rolled[0] * back_im - rolled[1] * back_re
            grad = patch[0] * back_im - patch[1] * back_re
        acc[p, j0, at, :] += jnp.where(mask, update[:, :H], 0.0)
        acc[p, j0 + 2, at, :] += jnp.where(mask, 0.0, update[:, :H])
        acc[p, j0 + 1, at, :] += update[:, H:]
        a, b = turned(grad[:, :H], grad[:, H:], undo, unmask)
        pacc[p, :, :H] += a
        pacc[p, :, H:] += b
    yield


def some_windows(spots, ext, acc, probe, right, left, order, pacc, stats, rolled, patch):
    runs = [
        one_window(spot, ext, acc, probe, right, left, order, pacc, stats, rolled.at[w], patch.at[w])
        for w, spot in enumerate(spots)
    ]
    steps = 8
    for t in range(steps + LAG * (len(runs) - 1)):
        for w, run in enumerate(runs):
            if 0 <= t - LAG * w < steps:
                next(run)


def windows_kernel(plan, at):
    ext, acc = at["ext"], at["acc"]
    row, col = lax.axis_index("row"), lax.axis_index("col")
    first_row, first_col = row * 512, col * 1024
    count = at["counts"][row * 8 + col]

    def corner(s):
        return at["pos"][s, 0] - first_row, at["pos"][s, 1] - first_col

    copies = []

    def begin(src, dst):
        copy = pltpu.make_async_copy(src, dst, at["sems"].at[len(copies)])
        copy.start()
        copies.append(copy)

    def pattern_copies(s):
        return [
            pltpu.make_async_copy(at["patterns"].at[s, :, pl.ds(k * H, H)], at["pat"].at[s, k], at["pat_sems"].at[s, k])
            for k in range(2)
        ]

    for ref, (r0, c0, nr, nc, dr, db) in zip(at["pieces"], plan["pieces"]):
        for k in range(nc // H):
            begin(ref.at[:, pl.ds(r0, nr), pl.ds(c0 + k * H, H)], ext.at[:, db + k, pl.ds(dr, nr), :])

    @pl.loop(0, count)
    def _(s):
        for copy in pattern_copies(s):
            copy.start()

    for k in range(4):
        for name in ("right", "left"):
            at[name][k, 0], at[name][k, 1] = split(at[name + "_in"][k])
    at["order"][...] = at["order_in"][...].astype(BF16)
    for name in ("acc", "pacc", "stats"):
        at[name][...] = jnp.zeros_like(at[name])
    for copy in copies:
        copy.wait()

    @pl.when(row == 15)
    def _():
        ext[:, :, 512:] = jnp.zeros_like(ext[:, :, 512:])

    @pl.when(col == 7)
    def _():
        ext[:, 8:] = jnp.zeros_like(ext[:, 8:])

    def spot(i):
        for copy in pattern_copies(i):
            copy.wait()
        o, c = corner(i)
        return o, c // H, c % H, at["pat"].at[i]

    def run(spots):
        some_windows(spots, ext, acc, at["probe"], at["right"], at["left"],
                     at["order"], at["pacc"], at["stats"], at["rolled"], at["patch"])

    @pl.loop(0, count // SIDE)
    def _(i):
        run([spot(SIDE * i + w) for w in range(SIDE)])

    @pl.loop(count // SIDE * SIDE, count)
    def _(i):
        run([spot(i)])

    ends = []
    for ref, (r0, nr, nc, db) in zip(at["outs"], plan["outs"]):
        for k in range(nc // H):
            copy = pltpu.make_async_copy(acc.at[:, db + k, pl.ds(r0, nr), :], ref.at[:, :, pl.ds(k * H, H)],
                                         at["sems"].at[len(copies) + len(ends)])
            copy.start()
            ends.append(copy)
    for copy in ends:
        copy.wait()


def windows(pos, counts, patterns, probe, tables, pieces, outs, nblk, nrows):
    vm = pl.BlockSpec(memory_space=pltpu.VMEM)
    sm = pl.BlockSpec(memory_space=pltpu.SMEM)
    hbm = pl.BlockSpec(memory_space=pl.ANY)
    plan = dict(pieces=[p[1:] for p in pieces], outs=outs)
    n_p, n_o = len(pieces), len(outs)
    n_sems = sum(p[4] // H for p in pieces) + sum(o[2] // H for o in outs)

    def kernel(*refs):
        it = iter(refs)
        take = lambda n: [next(it) for _ in range(n)]
        at = {}
        at["pos"], at["counts"], at["patterns"], at["probe"], at["right_in"], at["left_in"], at["order_in"] = take(7)
        at["pieces"], at["outs"] = take(n_p), take(n_o)
        at["pacc"], at["stats"] = take(2)
        at["ext"], at["acc"], at["pat"], at["rolled"], at["patch"], at["right"], at["left"], at["order"] = take(8)
        at["sems"], at["pat_sems"] = take(2)
        windows_kernel(plan, at)

    out = pl.pallas_call(
        kernel,
        name="windows",
        out_shape=[jax.ShapeDtypeStruct((2, nr, nc), F32) for _, nr, nc, _ in outs]
        + [jax.ShapeDtypeStruct((2, M, M), F32), jax.ShapeDtypeStruct((16, M), F32)],
        in_specs=[sm, sm, hbm, vm, vm, vm, vm] + [hbm] * n_p,
        out_specs=[hbm] * n_o + [vm, vm],
        scratch_shapes=[
            pltpu.VMEM((2, nblk, nrows, H), F32),
            pltpu.VMEM((2, nblk, nrows, H), F32),
            pltpu.VMEM((CAP, 2, M, H), F32),
            pltpu.VMEM((SIDE, 2, M, M), F32),
            pltpu.VMEM((SIDE, 2, M, M), F32),
            pltpu.VMEM((4, 2, M, M), BF16),
            pltpu.VMEM((4, 2, M, M), BF16),
            pltpu.VMEM((M, M), BF16),
            pltpu.SemaphoreType.DMA((n_sems,)),
            pltpu.SemaphoreType.DMA((CAP, 2)),
        ],
        compiler_params=pltpu.CompilerParams(vmem_limit_bytes=34 << 20),
        cost_estimate=pl.CostEstimate(flops=12 * 10**9, bytes_accessed=8 << 20, transcendentals=0),
    )(pos, counts, patterns, probe, *tables, *[p[0] for p in pieces])
    return out[:n_o], tuple(out[n_o:])


MESH = pl.DeviceIdType.MESH
NROW, NCOL = 16, 8


def send(src, dst, ss, rs, peer):
    copy = pltpu.make_async_remote_copy(src, dst, ss, rs, device_id=peer, device_id_type=MESH)
    copy.start()
    return copy


def ring(row, step):
    return row // 4 * 4 + lax.rem(row + step + 4, 4)


def columns(k, n=1):
    return pl.ds(k * H, n * H)


def halo_kernel(sample, low, right, corner, held1, held2, ss, rs):
    row, col = lax.axis_index("row"), lax.axis_index("col")
    above, below = lax.rem(row + NROW - 1, NROW), lax.rem(row + 1, NROW)
    before, after = lax.rem(col + NCOL - 1, NCOL), lax.rem(col + 1, NCOL)
    across, back = ring(above, 2), lax.rem(ring(row, 2) + 1, NROW)
    barrier = pltpu.get_barrier_semaphore()
    for peer in ((below, col), (ring(row, -1), col), (back, col), (row, after)):
        pl.semaphore_signal(barrier, inc=1, device_id=peer, device_id_type=MESH)
    pl.semaphore_wait(barrier, 4)
    number = iter(range(32))

    def go(src, dst, peer):
        n = next(number)
        return send(src, dst, ss.at[n], rs.at[n], peer)

    top = pl.ds(0, M)
    up = ring(row, 1), col
    hop1 = [go(sample.at[:, top, columns(2 + i)], held1.at[i], (across, col)) for i in range(2)]
    first = go(sample.at[:, top, columns(0, 2)], low.at[:, :, columns(0, 2)], (above, col))
    rest = [go(sample.at[:, :, columns(0, 2)], right, (row, before))]
    rest += [go(sample.at[:, top, columns(k, 2)], low.at[:, :, columns(k, 2)], (above, col)) for k in (4, 6)]
    hop1[0].wait_recv()
    hop2 = [go(held1.at[0], held2.at[0], up)]
    first.wait_recv()
    rest.append(go(low.at[:, :, columns(0, 2)], corner, (row, before)))
    hop1[1].wait_recv()
    hop2.append(go(held1.at[1], held2.at[1], up))
    hop3 = []
    for i in range(2):
        hop2[i].wait_recv()
        hop3.append(go(held2.at[i], low.at[:, :, columns(2 + i)], up))
    for copy in [first] + hop1 + hop2:
        copy.wait_send()
    for copy in rest + hop3:
        copy.wait()


def halos(sample):
    hbm = pl.BlockSpec(memory_space=pl.ANY)
    return pl.pallas_call(
        halo_kernel,
        name="halos",
        out_shape=[
            jax.ShapeDtypeStruct((2, M, 1024), F32),
            jax.ShapeDtypeStruct((2, 512, M), F32),
            jax.ShapeDtypeStruct((2, M, M), F32),
        ],
        in_specs=[pl.BlockSpec(memory_space=pltpu.HBM)],
        out_specs=[hbm] * 3,
        scratch_shapes=[
            pltpu.VMEM((2, 2, M, H), F32),
            pltpu.VMEM((2, 2, M, H), F32),
            pltpu.SemaphoreType.DMA((11,)),
            pltpu.SemaphoreType.DMA((11,)),
        ],
        compiler_params=pltpu.CompilerParams(collective_id=1, has_side_effects=True, vmem_limit_bytes=14 << 20),
        cost_estimate=pl.CostEstimate(flops=40 * 10**9, bytes_accessed=1 << 20, transcendentals=0),
    )(sample)


def tail_kernel(counts, pacc, stats, halo, edge, edge_low, out, coeff, misfit, down, came, mine1, got1, mine2, got2, part, wide,
                turn, low, held1, held2, s1, r1, s2, r2, s3, r3, s4, r4, ss, rs, ls):
    row, col = lax.axis_index("row"), lax.axis_index("col")

    def col_peer(k):
        return row, lax.rem(col + k, NCOL)

    def row_peer(k):
        return lax.rem(row + k, NROW), col

    barrier = pltpu.get_barrier_semaphore()
    for k in range(1, NCOL):
        pl.semaphore_signal(barrier, inc=1, device_id=col_peer(k), device_id_type=MESH)
    for k in range(1, NROW):
        pl.semaphore_signal(barrier, inc=1, device_id=row_peer(k), device_id_type=MESH)
    own = pltpu.make_async_copy(halo.at[:, :, columns(0, 2)], turn, ls)
    own.start()
    for p in range(2):
        for b in range(2):
            for h in range(2):
                piece = 4 * p + 2 * b + h
                mine1[piece, :H] = pacc[p, h * H : (h + 1) * H, b * H : (b + 1) * H]
                mine1[piece, H:] = stats[:, :H] + stats[:, H:]
    pl.semaphore_wait(barrier, NCOL + NROW - 2)
    number = iter(range(32))

    def go(src, dst, peer):
        n = next(number)
        return send(src, dst, ss.at[n], rs.at[n], peer)

    def lower(k, n=1):
        return go(halo.at[:, :, columns(k, n)], down.at[:, :, columns(k, n)], row_peer(1))

    across, back = (ring(lax.rem(row + 1, NROW), 2), col), (ring(row, -1), col)
    hop1 = [go(halo.at[:, :, columns(2 + i)], held1.at[i], across) for i in range(2)]
    rest = [lower(7), lower(6)]
    copies = [
        send(mine1.at[lax.rem(col + k, NCOL)], got1.at[k - 1], s1.at[k - 1], r1.at[k - 1], col_peer(k))
        for k in range(1, NCOL)
    ]
    hop1[0].wait_recv()
    hop2 = [go(held1.at[0], held2.at[0], back)]
    for copy in copies:
        copy.wait()
    total = mine1[col]
    for k in range(NCOL - 1):
        total = total + got1[k]
    for k in range(NROW):
        mine2[k, :8] = total[8 * k : 8 * k + 8]
        mine2[k, 8:] = total[H:]
    copies = [
        send(mine2.at[lax.rem(row + k, NROW)], got2.at[k - 1], s2.at[k - 1], r2.at[k - 1], row_peer(k))
        for k in range(1, NROW)
    ]
    corner = go(edge_low, low, col_peer(1))
    rest.append(lower(5))
    hop1[1].wait_recv()
    hop2.append(go(held1.at[1], held2.at[1], back))
    rest.append(go(edge, came, col_peer(1)))
    for copy in copies:
        copy.wait()
    total = mine2[row]
    for k in range(NROW - 1):
        total = total + got2[k]
    visits = jnp.sum(counts[...].astype(F32))
    pixels = M * M * visits
    mean = jnp.full((8, H), jnp.sum(total[16:])) / pixels
    factor = 4.0 / (mean * mean)
    coeff[...] = factor
    misfit[...] = jnp.full((8, H), jnp.sum(total[8:16])) / (mean * mean * pixels)
    part[row] = total[:8] * (factor / visits)
    copies = [send(part.at[row], part.at[row], s3.at[k - 1], r3.at[k - 1], row_peer(k)) for k in range(1, NROW)]
    rest.append(lower(4))
    hop2[0].wait_recv()
    hop3 = [go(held2.at[0], down.at[:, :, columns(2)], back)]
    own.wait()
    corner.wait_recv()
    turn[...] += jnp.where(col > 0, low[...], 0.0)
    rest.append(go(turn, down.at[:, :, columns(0, 2)], row_peer(1)))
    for copy in copies:
        copy.wait()
    copies = [send(part, wide.at[col], s4.at[k - 1], r4.at[k - 1], col_peer(k)) for k in range(1, NCOL)]
    wide[col] = part[...]
    hop2[1].wait_recv()
    hop3.append(go(held2.at[1], down.at[:, :, columns(3)], back))
    for copy in copies:
        copy.wait()
    for p in range(2):
        for b in range(2):
            for h in range(2):
                out[p, h * H : (h + 1) * H, b * H : (b + 1) * H] = wide[4 * p + 2 * b + h].reshape(H, H)
    for copy in [corner] + hop1 + hop2:
        copy.wait_send()
    for copy in rest + hop3:
        copy.wait()


def tail(counts, pacc, stats, halo, edge, edge_low):
    vm = pl.BlockSpec(memory_space=pltpu.VMEM)
    sm = pl.BlockSpec(memory_space=pltpu.SMEM)
    hbm = pl.BlockSpec(memory_space=pl.ANY)
    numbers = (NCOL - 1, NCOL - 1, NROW - 1, NROW - 1, NROW - 1, NROW - 1, NCOL - 1, NCOL - 1, 13, 13)
    tile = jax.ShapeDtypeStruct((8, H), F32)
    return pl.pallas_call(
        tail_kernel,
        name="tail",
        out_shape=[
            jax.ShapeDtypeStruct((2, M, M), F32), tile, tile,
            jax.ShapeDtypeStruct((2, M, 1024), F32), jax.ShapeDtypeStruct((2, 512, M), F32),
        ],
        in_specs=[vm, vm, vm, hbm, hbm, hbm],
        out_specs=[vm, vm, vm, hbm, hbm],
        scratch_shapes=[
            pltpu.VMEM((NCOL, H + 16, H), F32),
            pltpu.VMEM((NCOL - 1, H + 16, H), F32),
            pltpu.VMEM((NROW, 24, H), F32),
            pltpu.VMEM((NROW - 1, 24, H), F32),
            pltpu.VMEM((NROW, 8, H), F32),
            pltpu.VMEM((NCOL, NROW, 8, H), F32),
            pltpu.VMEM((2, M, M), F32),
            pltpu.VMEM((2, M, M), F32),
            pltpu.VMEM((2, 2, M, H), F32),
            pltpu.VMEM((2, 2, M, H), F32),
        ]
        + [pltpu.SemaphoreType.DMA((n,)) for n in numbers]
        + [pltpu.SemaphoreType.DMA],
        compiler_params=pltpu.CompilerParams(collective_id=0, has_side_effects=True, vmem_limit_bytes=14 << 20),
        cost_estimate=pl.CostEstimate(flops=40 * 10**9, bytes_accessed=1 << 20, transcendentals=0),
    )(counts, pacc, stats, halo, edge, edge_low)


def finish_kernel(coeff, misfit, probe, own, came, came_down, out, probe_out, misfit_out,
                  tile, down, right, ins, outs):
    row, col = lax.axis_index("row"), lax.axis_index("col")
    top, bottom = pl.ds(0, M), pl.ds(M, M)
    copies = []
    for k in range(4):
        cols = columns(2 * k, 2)
        pairs = [(own.at[:, :, cols], tile.at[:, :, cols]), (came_down.at[:, :, cols], down.at[:, :, cols])]
        if k == 0:
            pairs.append((came, right))
        copies.append([pltpu.make_async_copy(src, dst, ins.at[k, n]) for n, (src, dst) in enumerate(pairs)])
    for copy in copies[1] + copies[2] + copies[3] + copies[0]:
        copy.start()
    probe_out[...] = probe[...]
    misfit_out[...] = misfit[0:1, 0:1]
    factor = coeff[0:1, 0:1]
    ends = []
    for k in (1, 2, 3, 0):
        cols = columns(2 * k, 2)
        for copy in copies[k]:
            copy.wait()
        upper = tile[:, top, cols] + jnp.where(row > 0, down[:, :, cols], 0.0)
        lower = tile[:, bottom, cols]
        if k == 0:
            upper = upper + jnp.where(col > 0, right[:, top], 0.0)
            lower = lower + jnp.where(col > 0, right[:, bottom], 0.0)
        tile[:, top, cols] = upper * factor
        tile[:, bottom, cols] = lower * factor
        ends.append(pltpu.make_async_copy(tile.at[:, :, cols], out.at[:, :, cols], outs.at[k]))
        ends[-1].start()
    for copy in ends:
        copy.wait()


def finished(coeff, misfit, probe, own, came, down):
    vm = pl.BlockSpec(memory_space=pltpu.VMEM)
    hbm = pl.BlockSpec(memory_space=pl.ANY)
    return pl.pallas_call(
        finish_kernel,
        name="finished",
        out_shape=[
            jax.ShapeDtypeStruct((2, 512, 1024), F32),
            jax.ShapeDtypeStruct((2, M, M), F32),
            jax.ShapeDtypeStruct((1, 1), F32),
        ],
        in_specs=[vm, vm, vm] + [hbm] * 3,
        out_specs=[hbm, vm, vm],
        scratch_shapes=[
            pltpu.VMEM((2, 512, 1024), F32),
            pltpu.VMEM((2, M, 1024), F32),
            pltpu.VMEM((2, 512, M), F32),
            pltpu.SemaphoreType.DMA((4, 3)),
            pltpu.SemaphoreType.DMA((4,)),
        ],
        compiler_params=pltpu.CompilerParams(vmem_limit_bytes=14 << 20),
        cost_estimate=pl.CostEstimate(flops=10**7, bytes_accessed=10 << 20, transcendentals=0),
    )(coeff, misfit, probe, own, came, down)


def body(sample, probe, patterns, positions, counts):
    tables = tuple(jnp.asarray(t) for t in dft_tables())
    low, right, corner = halos(sample)
    (own, halo, edge, edge_low), sums = windows(
        positions, counts, patterns, probe, tables,
        [(sample, 0, 0, 512, 1024, 0, 0), (right, 0, 0, 512, M, 0, 8), (low, 0, 0, M, 1024, 512, 0), (corner, 0, 0, M, M, 512, 8)],
        [(0, 512, 1024, 0), (512, M, 1024, 0), (0, 512, M, 8), (512, M, M, 8)],
        10, 768,
    )
    probe_sum, coeff, misfit, down, came = tail(counts.reshape(1, H), *sums, halo, edge, edge_low)
    object_grad, probe_grad, mean_misfit = finished(coeff, misfit, probe_sum, own, came, down)
    return object_grad, probe_grad, mean_misfit.reshape(())


def solution(mesh):
    in_specs = (
        P(None, "row", "col"),
        P(),
        P(("row", "col"), None, None),
        P(("row", "col"), None),
        P(),
    )
    out_specs = (P(None, "row", "col"), P(), P())
    return jax.shard_map(body, mesh=mesh, in_specs=in_specs, out_specs=out_specs, check_vma=False)
```

time: 137 us -> 123 us (0.90)
  Pallas kernels: 96.3 us -> 119 us
  waiting for transfers between devices: 12.8 us -> 0 us
  local copies, waits for them, and re-layouts: 14.5 us -> 2.97 us
  starting transfers between devices: 10.5 us -> 0 us
    ppermute x6 -> x0, waiting for transfers between devices: 12.8 us -> none  [passed_along(): lax.ppermute(value, axis, [(source, source + steps) for source in range(f...]
    pallas_call x3 -> x2, Pallas kernels: 41.5 us -> 53.1 us  [the longest x1 40.3 us: halos(): pl.pallas_call(halo_kernel, name='halos', out_shape=[jax.ShapeDtypeStruct...]
    pallas_call x1, Pallas kernels: 50.2 us -> 61.5 us  [tail(): pl.pallas_call(tail_kernel, name='tail', out_shape=[jax.ShapeDtypeStruct(...]
    ppermute x6 -> x0, starting transfers between devices: 10.5 us -> none  [passed_along(): lax.ppermute(value, axis, [(source, source + steps) for source in range(f...]
    slice x4 -> x0, local copies, waits for them, and re-layouts: 8.5 us -> none  [the longest x1 2.38 us: body(): right = passed_along(later[:, :, :M], 'col', -1)]
    unnamed x27 -> x15, local copies, waits for them, and re-layouts: 5.42 us -> 2.97 us
  transfers between devices with their start and end apart: 6 -> 0, of which waited for: 2 -> 0; matrix products, arithmetic and copies ran while one was open for 4% -> 0% of each run, Pallas kernels for 67% -> 0%
where the time goes in v4:
time: 123 us; the launch traced here: 122 us
  Pallas kernels  119 us (97%)
  local copies, waits for them, and re-layouts  2.97 us (2%)
    pallas_call x1, Pallas kernels, tail(): pl.pallas_call(tail_kernel, name='tail', out_shape=[jax.ShapeDtypeStruct(...  61.5 us
    pallas_call x1, Pallas kernels, halos(): pl.pallas_call(halo_kernel, name='halos', out_shape=[jax.ShapeDtypeStruct...  40.3 us
    pallas_call x1, Pallas kernels, windows(): pl.pallas_call(kernel, name='windows', out_shape=[jax.ShapeDtypeStruct((2...  12.8 us
    pallas_call x1, Pallas kernels, finished(): pl.pallas_call(finish_kernel, name='finished', out_shape=[jax.ShapeDtypeS...  4.06 us
    unnamed x15, local copies, waits for them, and re-layouts  2.97 us

profile of v4, /device:TPU:1, one launch (start us, length us, event | category | flops | bytes accessed | tf_op | source)
XLA Modules:
  0.0 122.4 jit_solution(11021905087147635064)
XLA Ops:
  0.6 0.8 copy.11.refs_0_
  1.4 0.0 copy-start.1
  1.4 2.2 %copy-done.1 = f32[2,512,1024]{2,1,0:T(8,128)S(1)} copy-done((f32[2,512,1024]{2,1,0:T(8,128)S(1)}, f32[2,512,1024]{2,1,0:T(8,128)}, u32[]{:S(2)}) %copy-start.1) | copy-done | bytes 4194328
  3.6 0.0 copy-start
  3.6 0.0 copy-start.2
  3.6 0.0 copy-start.3
  3.6 0.0 copy-start.4
  3.6 0.0 copy-start.5
  3.6 0.0 copy-start.6
  3.6 40.3 %halos.1 = (f32[2,256,1024]{2,1,0:T(8,128)S(1)}, f32[2,512,256]{2,1,0:T(8,128)S(1)}, f32[2,256,256]{2,1,0:T(8,128)S(1)}) custom-call(f32[2,512,1024]{2,1,0:T(8,128)S(1)} %copy-done.1), custom_call_target="tpu_custom_call" | custom-call | flops 40000000000 | bytes 1048576 | tf_op jit(solution)/shard_map/halos/pallas_call | solution.py:323
  44.0 0.0 copy-done
  44.0 0.0 copy-done.2
  44.0 0.0 copy-done.3
  44.0 0.0 copy-done.4
  44.0 0.0 copy-done.5
  44.0 0.0 copy-done.6
  44.0 12.8 %windows.1 = (f32[2,512,1024]{2,1,0:T(8,128)S(1)}, f32[2,256,1024]{2,1,0:T(8,128)S(1)}, f32[2,512,256]{2,1,0:T(8,128)S(1)}, f32[2,256,256]{2,1,0:T(8,128)S(1)}, ...) custom-call(s32[16,2]{1,0:T(8,128)S(1)} %copy.11.refs_0_, s32[128]{0:T(128)S(1)} %copy-done.3, ...), custom_call_target="tpu_custom_call" | custom-call | flops 12000000000 | bytes 8388608 | tf_op jit(solution)/shard_map/windows/pallas_call | solution.py:241
  56.8 61.5 %tail.1 = (f32[2,256,256]{2,1,0:T(8,128)S(1)}, f32[8,128]{1,0:T(8,128)S(1)}, f32[8,128]{1,0:T(8,128)S(1)}, f32[2,256,1024]{2,1,0:T(8,128)S(1)}, f32[2,512,256]{2,1,0:T(8,128)S(1)}) custom-call(s32[1,128]{1,0:T(1,128)S(1)} %bitcast.2, f32[2,256,256]{2,1,0:T(8,128)S(1)} %get-tuple-element.23.pacc, f32[16,256]{1,0:T(8,128)S(1)} %get-tuple-element.24.stats, ...), custom_call_target="tpu_custom_call" | custom-call | flops 40000000000 | bytes 1048576 | tf_op jit(solution)/shard_map/tail/pallas_call | solution.py:447
  118.3 4.1 %finished.1 = (f32[2,512,1024]{2,1,0:T(8,128)}, f32[2,256,256]{2,1,0:T(8,128)}, f32[1,1]{1,0:T(1,128)}) custom-call(f32[8,128]{1,0:T(8,128)S(1)} %get-tuple-element.28.coeff, f32[8,128]{1,0:T(8,128)S(1)} %get-tuple-element.29.misfit, f32[2,256,256]{2,1,0:T(8,128)S(1)} %get-tuple-element.30.probe, f32[2,512,1024]{2,1,0:T(8,128)S(1)} %get-tuple-element.31.own, ...), custom_call_target="tpu_custom_call" | custom-call | flops 10000000 | bytes 10485760 | tf_op jit(solution)/shard_map/finished/pallas_call | solution.py:512
Async XLA Ops:
  1.4 2.2 %copy-start.1 = (f32[2,512,1024]{2,1,0:T(8,128)S(1)}, f32[2,512,1024]{2,1,0:T(8,128)}, u32[]{:S(2)}) copy-start(f32[2,512,1024]{2,1,0:T(8,128)} %refs_7_.1) | copy-start | bytes 12582916
  3.6 40.4 %copy-start = (f32[16,256,256]{2,1,0:T(8,128)S(1)}, f32[16,256,256]{2,1,0:T(8,128)}, u32[]{:S(2)}) copy-start(f32[16,256,256]{2,1,0:T(8,128)} %refs_2_.1) | copy-start | bytes 12582916
  3.6 40.4 %copy-start.2 = (f32[2,256,256]{2,1,0:T(8,128)S(1)}, f32[2,256,256]{2,1,0:T(8,128)}, u32[]{:S(2)}) copy-start(f32[2,256,256]{2,1,0:T(8,128)} %refs_3_.1) | copy-start | bytes 1572868
  3.6 40.4 %copy-start.3 = (s32[128]{0:T(128)S(1)}, s32[128]{0:T(128)}, u32[]{:S(2)}) copy-start(s32[128]{0:T(128)} %refs_1_.1) | copy-start | bytes 1540
  3.6 40.4 %copy-start.4 = (f32[4,256,256]{2,1,0:T(8,128)S(1)}, f32[4,256,256]{2,1,0:T(8,128)}, u32[]{:S(2)}) copy-start(f32[4,256,256]{2,1,0:T(8,128)} %constant.7.clone.refs_5_) | copy-start | bytes 3145732
  3.6 40.4 %copy-start.5 = (f32[4,256,256]{2,1,0:T(8,128)S(1)}, f32[4,256,256]{2,1,0:T(8,128)}, u32[]{:S(2)}) copy-start(f32[4,256,256]{2,1,0:T(8,128)} %constant.6.clone.refs_4_) | copy-start | bytes 3145732
  3.6 40.4 %copy-start.6 = (f32[256,256]{1,0:T(8,128)S(1)}, f32[256,256]{1,0:T(8,128)}, u32[]{:S(2)}) copy-start(f32[256,256]{1,0:T(8,128)} %constant.8.clone.refs_6_) | copy-start | bytes 786436

commit v5 on v4

v5 whole, which is shorter than its diff:
```python
import math

import jax
import jax.numpy as jnp
import numpy as np
from jax import lax
from jax.experimental import pallas as pl
from jax.experimental.pallas import tpu as pltpu
from jax.sharding import PartitionSpec as P

F32 = jnp.float32
BF16 = jnp.bfloat16
M = 256
H = 128
CAP = 16
SIDE = 2
LAG = 0


def dft_tables():
    n = np.arange(H)[:, None]
    m = np.arange(H)[None, :]
    right, left = [], []
    for sign in (-1.0, 1.0):
        for odd in (0, 1):
            if sign < 0:
                angle = 2 * math.pi * (n * (2 * m + odd) % M) / M
            else:
                angle = 2 * math.pi * ((2 * n + odd) * m % M) / M
            re, im = np.cos(angle) / 16.0, sign * np.sin(angle) / 16.0
            right.append(np.block([[re, im], [-im, re]]))
            left.append(right[-1].T)
    order = np.zeros((M, M), np.float32)
    k = np.arange(M)
    order[k, k // 2 + H * (k % 2)] = 1.0
    return np.stack(right).astype(np.float32), np.stack(left).astype(np.float32), order


def split(value):
    high = value.astype(BF16)
    return high, (value - high.astype(F32)).astype(BF16)


def dot(a, b):
    return jnp.dot(a, b, preferred_element_type=F32)


def right_dot(value, table):
    high, low = split(value)
    return dot(high, table[0]) + dot(low, table[0]) + dot(high, table[1])


def left_dot(table, value):
    high, low = split(value)
    return dot(table[0], high) + dot(table[0], low) + dot(table[1], high)


def lanes(a, b):
    return jnp.concatenate([a, b], axis=1)


def rows(*parts):
    return jnp.concatenate(parts, axis=0)


def one_window(spot, ext, acc, probe, right, left, order, pacc, stats, rolled, patch):
    top, j0, dc, pat = spot
    lane = lax.broadcasted_iota(jnp.int32, (M, H), 1)
    mask = lane >= dc
    at = pl.ds(top, M)

    def turned(a, b, shift, keep):
        a, b = pltpu.roll(a, shift, 1), pltpu.roll(b, shift, 1)
        return jnp.where(keep, a, b), jnp.where(keep, b, a)

    for p in range(2):
        a, b = turned(probe[p, :, :H], probe[p, :, H:], dc, mask)
        rolled[p, :, :H] = a
        rolled[p, :, H:] = b
        patch[p, :, :H] = jnp.where(mask, ext[p, j0, at, :], ext[p, j0 + 2, at, :])
        patch[p, :, H:] = ext[p, j0 + 1, at, :]
    wave_re = rolled[0] * patch[0] - rolled[1] * patch[1]
    wave_im = rolled[0] * patch[1] + rolled[1] * patch[0]
    sums = lanes(wave_re[:, :H] + wave_re[:, H:], wave_im[:, :H] + wave_im[:, H:])
    difs = lanes(wave_re[:, :H] - wave_re[:, H:], wave_im[:, :H] - wave_im[:, H:])
    yield
    even = right_dot(sums, right[0])
    odd = right_dot(difs, right[1])
    yield
    halves = ((even[:H] + even[H:], odd[:H] + odd[H:]), (even[:H] - even[H:], odd[:H] - odd[H:]))
    fars, levels = [], []
    for parity, (e, o) in enumerate(halves):
        fars.append(left_dot(left[parity], rows(lanes(e[:, :H], o[:, :H]), lanes(e[:, H:], o[:, H:]))))
        every = pl.ds(parity, H, 2)
        level = lanes(pat[0, every, :], pat[1, every, :])
        stats[8:] += jnp.sum(level.reshape(16, 8, M), axis=0)
        high, low = split(level)
        levels.append(dot(high, order[...]) + dot(low, order[...]))
    yield
    back = []
    for parity, far in enumerate(fars):
        far_re, far_im = far[:H], far[H:]
        resid = far_re * far_re + far_im * far_im - levels[parity]
        stats[:8] += jnp.sum((resid * resid).reshape(16, 8, M), axis=0)
        back.append(left_dot(left[2 + parity], rows(resid * far_re, resid * far_im)))
    yield
    half_s, half_d = back[0] + back[1], back[0] - back[1]
    re, im = rows(half_s[:H], half_d[:H]), rows(half_s[H:], half_d[H:])
    even = right_dot(lanes(re[:, :H], im[:, :H]), right[2])
    odd = right_dot(lanes(re[:, H:], im[:, H:]), right[3])
    yield
    first, second = even + odd, even - odd
    back_re = lanes(first[:, :H], second[:, :H])
    back_im = lanes(first[:, H:], second[:, H:])
    unmask = lane < H - dc
    undo = lax.rem(H - dc, H)
    for p in range(2):
        if p == 0:
            update = rolled[0] * back_re + rolled[1] * back_im
            grad = patch[0] * back_re + patch[1] * back_im
        else:
            update = rolled[0] * back_im - rolled[1] * back_re
            grad = patch[0] * back_im - patch[1] * back_re
        acc[p, j0, at, :] += jnp.where(mask, update[:, :H], 0.0)
        acc[p, j0 + 2, at, :] += jnp.where(mask, 0.0, update[:, :H])
        acc[p, j0 + 1, at, :] += update[:, H:]
        a, b = turned(grad[:, :H], grad[:, H:], undo, unmask)
        pacc[p, :, :H] += a
        pacc[p, :, H:] += b
    yield


def some_windows(spots, ext, acc, probe, right, left, order, pacc, stats, rolled, patch):
    runs = [
        one_window(spot, ext, acc, probe, right, left, order, pacc, stats, rolled.at[w], patch.at[w])
        for w, spot in enumerate(spots)
    ]
    steps = 6
    for t in range(steps + LAG * (len(runs) - 1)):
        for w, run in enumerate(runs):
            if 0 <= t - LAG * w < steps:
                next(run)


def windows_kernel(pos, counts, patterns, probe, right_in, left_in, order_in, ext, acc, pacc, stats, pat, rolled, patch,
                   right, left, order, sems):
    row, col = lax.axis_index("row"), lax.axis_index("col")
    count = counts[row * 8 + col]

    def pattern_copies(s):
        return [
            pltpu.make_async_copy(patterns.at[s, :, pl.ds(k * H, H)], pat.at[s, k], sems.at[s, k]) for k in range(2)
        ]

    @pl.loop(0, count)
    def _(s):
        for copy in pattern_copies(s):
            copy.start()

    for k in range(4):
        right[k, 0], right[k, 1] = split(right_in[k])
        left[k, 0], left[k, 1] = split(left_in[k])
    order[...] = order_in[...].astype(BF16)
    for ref in (acc, pacc, stats):
        ref[...] = jnp.zeros_like(ref)

    def spot(s):
        for copy in pattern_copies(s):
            copy.wait()
        o, c = pos[0, s] - row * 512, pos[1, s] - col * 1024
        return o, c // H, c % H, pat.at[s]

    def run(spots):
        some_windows(spots, ext, acc, probe, right, left, order, pacc, stats, rolled, patch)

    @pl.loop(0, count // SIDE)
    def _(i):
        run([spot(SIDE * i + w) for w in range(SIDE)])

    @pl.loop(count // SIDE * SIDE, count)
    def _(i):
        run([spot(i)])


def windows(pos, counts, patterns, probe, tables, ext):
    vm = pl.BlockSpec(memory_space=pltpu.VMEM)
    sm = pl.BlockSpec(memory_space=pltpu.SMEM)
    hbm = pl.BlockSpec(memory_space=pl.ANY)
    return pl.pallas_call(
        windows_kernel,
        name="windows",
        out_shape=[
            jax.ShapeDtypeStruct((2, 10, 768, H), F32),
            jax.ShapeDtypeStruct((2, M, M), F32),
            jax.ShapeDtypeStruct((16, M), F32),
        ],
        in_specs=[sm, sm, hbm, vm, vm, vm, vm, vm],
        out_specs=[vm, vm, vm],
        scratch_shapes=[
            pltpu.VMEM((CAP, 2, M, H), F32),
            pltpu.VMEM((SIDE, 2, M, M), F32),
            pltpu.VMEM((SIDE, 2, M, M), F32),
            pltpu.VMEM((4, 2, M, M), BF16),
            pltpu.VMEM((4, 2, M, M), BF16),
            pltpu.VMEM((M, M), BF16),
            pltpu.SemaphoreType.DMA((CAP, 2)),
        ],
        compiler_params=pltpu.CompilerParams(vmem_limit_bytes=29 << 20),
        cost_estimate=pl.CostEstimate(flops=12 * 10**9, bytes_accessed=8 << 20, transcendentals=0),
    )(pos, counts, patterns, probe, *tables, ext)


MESH = pl.DeviceIdType.MESH
NROW, NCOL = 16, 8


def send(src, dst, ss, rs, peer):
    copy = pltpu.make_async_remote_copy(src, dst, ss, rs, device_id=peer, device_id_type=MESH)
    copy.start()
    return copy


def ring(row, step):
    return row // 4 * 4 + lax.rem(row + step + 4, 4)


def columns(k, n=1):
    return pl.ds(k * H, n * H)


def halo_kernel(sample, ext, held1, held2, ss, rs, ls):
    row, col = lax.axis_index("row"), lax.axis_index("col")
    above, below = lax.rem(row + NROW - 1, NROW), lax.rem(row + 1, NROW)
    before, after = lax.rem(col + NCOL - 1, NCOL), lax.rem(col + 1, NCOL)
    across, back = ring(above, 2), lax.rem(ring(row, 2) + 1, NROW)
    barrier = pltpu.get_barrier_semaphore()
    for peer in ((below, col), (ring(row, -1), col), (back, col), (row, after)):
        pl.semaphore_signal(barrier, inc=1, device_id=peer, device_id_type=MESH)
    pl.semaphore_wait(barrier, 4)
    number = iter(range(32))

    def go(src, dst, peer):
        n = next(number)
        return send(src, dst, ss.at[n], rs.at[n], peer)

    up = ring(row, 1), col
    top, tile, beyond = pl.ds(0, M), pl.ds(0, 512), pl.ds(512, M)

    def lower(k):
        return go(sample.at[:, top, columns(k)], ext.at[:, k, beyond], (above, col))

    hop1 = [go(sample.at[:, top, columns(2 + i)], held1.at[i], (across, col)) for i in range(2)]
    first = [lower(0), lower(1)]
    rest = [go(sample.at[:, tile, columns(k)], ext.at[:, 8 + k, tile], (row, before)) for k in range(2)]
    rest += [lower(k) for k in (4, 5, 6, 7)]
    own = [pltpu.make_async_copy(sample.at[:, tile, columns(k)], ext.at[:, k, tile], ls.at[k]) for k in range(8)]
    for copy in own:
        copy.start()
    hop1[0].wait_recv()
    hop2 = [go(held1.at[0], held2.at[0], up)]
    for k in range(2):
        first[k].wait_recv()
        rest.append(go(ext.at[:, k, beyond], ext.at[:, 8 + k, beyond], (row, before)))
    hop1[1].wait_recv()
    hop2.append(go(held1.at[1], held2.at[1], up))
    hop3 = []
    for i in range(2):
        hop2[i].wait_recv()
        hop3.append(go(held2.at[i], ext.at[:, 2 + i, beyond], up))
    for copy in first + hop1 + hop2:
        copy.wait_send()
    for copy in rest + hop3 + own:
        copy.wait()

    @pl.when(row == NROW - 1)
    def _():
        ext[:, :, 512:] = jnp.zeros_like(ext[:, :, 512:])

    @pl.when(col == NCOL - 1)
    def _():
        ext[:, 8:] = jnp.zeros_like(ext[:, 8:])


def halos(sample):
    return pl.pallas_call(
        halo_kernel,
        name="halos",
        out_shape=jax.ShapeDtypeStruct((2, 10, 768, H), F32),
        in_specs=[pl.BlockSpec(memory_space=pltpu.HBM)],
        out_specs=pl.BlockSpec(memory_space=pltpu.VMEM),
        scratch_shapes=[
            pltpu.VMEM((2, 2, M, H), F32),
            pltpu.VMEM((2, 2, M, H), F32),
            pltpu.SemaphoreType.DMA((16,)),
            pltpu.SemaphoreType.DMA((16,)),
            pltpu.SemaphoreType.DMA((8,)),
        ],
        compiler_params=pltpu.CompilerParams(collective_id=1, has_side_effects=True, vmem_limit_bytes=14 << 20),
        cost_estimate=pl.CostEstimate(flops=40 * 10**9, bytes_accessed=1 << 20, transcendentals=0),
    )(sample)


def tail_kernel(counts, pacc, stats, acc, out, coeff, misfit, down, came, mine1, got1, mine2, got2, part, wide,
                turn, low, held1, held2, s1, r1, s2, r2, s3, r3, s4, r4, ss, rs, ls):
    row, col = lax.axis_index("row"), lax.axis_index("col")

    def col_peer(k):
        return row, lax.rem(col + k, NCOL)

    def row_peer(k):
        return lax.rem(row + k, NROW), col

    barrier = pltpu.get_barrier_semaphore()
    for k in range(1, NCOL):
        pl.semaphore_signal(barrier, inc=1, device_id=col_peer(k), device_id_type=MESH)
    for k in range(1, NROW):
        pl.semaphore_signal(barrier, inc=1, device_id=row_peer(k), device_id_type=MESH)
    beyond, tile, edge = pl.ds(512, M), pl.ds(0, 512), pl.ds(8, 2)
    own = pltpu.make_async_copy(acc.at[:, pl.ds(0, 2), beyond], turn, ls)
    own.start()
    for p in range(2):
        for b in range(2):
            for h in range(2):
                piece = 4 * p + 2 * b + h
                mine1[piece, :H] = pacc[p, h * H : (h + 1) * H, b * H : (b + 1) * H]
                mine1[piece, H:] = stats[:, :H] + stats[:, H:]
    pl.semaphore_wait(barrier, NCOL + NROW - 2)
    number = iter(range(32))

    def go(src, dst, peer):
        n = next(number)
        return send(src, dst, ss.at[n], rs.at[n], peer)

    def lower(k):
        return go(acc.at[:, k, beyond], down.at[:, k], row_peer(1))

    across, back = (ring(lax.rem(row + 1, NROW), 2), col), (ring(row, -1), col)
    hop1 = [go(acc.at[:, 2 + i, beyond], held1.at[i], across) for i in range(2)]
    rest = [lower(7), lower(6), lower(5)]
    copies = [
        send(mine1.at[lax.rem(col + k, NCOL)], got1.at[k - 1], s1.at[k - 1], r1.at[k - 1], col_peer(k))
        for k in range(1, NCOL)
    ]
    hop1[0].wait_recv()
    hop2 = [go(held1.at[0], held2.at[0], back)]
    for copy in copies:
        copy.wait()
    total = mine1[col]
    for k in range(NCOL - 1):
        total = total + got1[k]
    for k in range(NROW):
        mine2[k, :8] = total[8 * k : 8 * k + 8]
        mine2[k, 8:] = total[H:]
    copies = [
        send(mine2.at[lax.rem(row + k, NROW)], got2.at[k - 1], s2.at[k - 1], r2.at[k - 1], row_peer(k))
        for k in range(1, NROW)
    ]
    corner = go(acc.at[:, edge, beyond], low, col_peer(1))
    rest.append(lower(4))
    hop1[1].wait_recv()
    hop2.append(go(held1.at[1], held2.at[1], back))
    rest.append(go(acc.at[:, edge, tile], came, col_peer(1)))
    for copy in copies:
        copy.wait()
    total = mine2[row]
    for k in range(NROW - 1):
        total = total + got2[k]
    visits = jnp.sum(counts[...].astype(F32))
    pixels = M * M * visits
    mean = jnp.full((8, H), jnp.sum(total[16:])) / pixels
    factor = 4.0 / (mean * mean)
    coeff[...] = factor
    misfit[...] = jnp.full((8, H), jnp.sum(total[8:16])) / (mean * mean * pixels)
    part[row] = total[:8] * (factor / visits)
    copies = [send(part.at[row], part.at[row], s3.at[k - 1], r3.at[k - 1], row_peer(k)) for k in range(1, NROW)]
    hop2[0].wait_recv()
    hop3 = [go(held2.at[0], down.at[:, 2], back)]
    own.wait()
    corner.wait_recv()
    turn[...] += jnp.where(col > 0, low[...], 0.0)
    rest.append(go(turn, down.at[:, pl.ds(0, 2)], row_peer(1)))
    for copy in copies:
        copy.wait()
    copies = [send(part, wide.at[col], s4.at[k - 1], r4.at[k - 1], col_peer(k)) for k in range(1, NCOL)]
    wide[col] = part[...]
    hop2[1].wait_recv()
    hop3.append(go(held2.at[1], down.at[:, 3], back))
    for copy in copies:
        copy.wait()
    for p in range(2):
        for b in range(2):
            for h in range(2):
                out[p, h * H : (h + 1) * H, b * H : (b + 1) * H] = wide[4 * p + 2 * b + h].reshape(H, H)
    for copy in [corner] + hop1 + hop2:
        copy.wait_send()
    for copy in rest + hop3:
        copy.wait()


def tail(counts, pacc, stats, acc):
    vm = pl.BlockSpec(memory_space=pltpu.VMEM)
    sm = pl.BlockSpec(memory_space=pltpu.SMEM)
    hbm = pl.BlockSpec(memory_space=pl.ANY)
    numbers = (NCOL - 1, NCOL - 1, NROW - 1, NROW - 1, NROW - 1, NROW - 1, NCOL - 1, NCOL - 1, 13, 13)
    tile = jax.ShapeDtypeStruct((8, H), F32)
    return pl.pallas_call(
        tail_kernel,
        name="tail",
        out_shape=[
            jax.ShapeDtypeStruct((2, M, M), F32), tile, tile,
            jax.ShapeDtypeStruct((2, 8, M, H), F32), jax.ShapeDtypeStruct((2, 2, 512, H), F32),
        ],
        in_specs=[vm, vm, vm, hbm],
        out_specs=[vm, vm, vm, hbm, hbm],
        scratch_shapes=[
            pltpu.VMEM((NCOL, H + 16, H), F32),
            pltpu.VMEM((NCOL - 1, H + 16, H), F32),
            pltpu.VMEM((NROW, 24, H), F32),
            pltpu.VMEM((NROW - 1, 24, H), F32),
            pltpu.VMEM((NROW, 8, H), F32),
            pltpu.VMEM((NCOL, NROW, 8, H), F32),
            pltpu.VMEM((2, 2, M, H), F32),
            pltpu.VMEM((2, 2, M, H), F32),
            pltpu.VMEM((2, 2, M, H), F32),
            pltpu.VMEM((2, 2, M, H), F32),
        ]
        + [pltpu.SemaphoreType.DMA((n,)) for n in numbers]
        + [pltpu.SemaphoreType.DMA],
        compiler_params=pltpu.CompilerParams(collective_id=0, has_side_effects=True, vmem_limit_bytes=14 << 20),
        cost_estimate=pl.CostEstimate(flops=40 * 10**9, bytes_accessed=1 << 20, transcendentals=0),
    )(counts, pacc, stats, acc)


def finish_kernel(coeff, misfit, probe, acc, came, down, out, probe_out, misfit_out, tile, sems):
    row, col = lax.axis_index("row"), lax.axis_index("col")
    factor = coeff[0:1, 0:1]
    ends = []
    for k in (2, 3, 4, 5, 6, 7, 0, 1):
        upper, lower = acc[:, k, :M] + jnp.where(row > 0, down[:, k], 0.0), acc[:, k, M:512]
        if k < 2:
            upper = upper + jnp.where(col > 0, came[:, k, :M], 0.0)
            lower = lower + jnp.where(col > 0, came[:, k, M:], 0.0)
        tile[k, :, :M] = upper * factor
        tile[k, :, M:] = lower * factor
        ends.append(pltpu.make_async_copy(tile.at[k], out.at[:, :, columns(k)], sems.at[k]))
        ends[-1].start()
    probe_out[...] = probe[...]
    misfit_out[...] = misfit[0:1, 0:1]
    for copy in ends:
        copy.wait()


def finished(coeff, misfit, probe, acc, came, down):
    vm = pl.BlockSpec(memory_space=pltpu.VMEM)
    return pl.pallas_call(
        finish_kernel,
        name="finished",
        out_shape=[
            jax.ShapeDtypeStruct((2, 512, 1024), F32),
            jax.ShapeDtypeStruct((2, M, M), F32),
            jax.ShapeDtypeStruct((1, 1), F32),
        ],
        in_specs=[vm] * 6,
        out_specs=[pl.BlockSpec(memory_space=pl.ANY), vm, vm],
        scratch_shapes=[pltpu.VMEM((8, 2, 512, H), F32), pltpu.SemaphoreType.DMA((8,))],
        compiler_params=pltpu.CompilerParams(vmem_limit_bytes=28 << 20),
        cost_estimate=pl.CostEstimate(flops=10**7, bytes_accessed=10 << 20, transcendentals=0),
    )(coeff, misfit, probe, acc, came, down)


def body(sample, probe, patterns, positions, counts):
    tables = tuple(jnp.asarray(t) for t in dft_tables())
    ext = halos(pltpu.with_memory_space_constraint(sample, pltpu.HBM))
    acc, pacc, stats = windows(positions.T, counts, patterns, probe, tables, ext)
    probe_sum, coeff, misfit, down, came = tail(counts.reshape(1, H), pacc, stats, acc)
    object_grad, probe_grad, mean_misfit = finished(coeff, misfit, probe_sum, acc, came, down)
    return object_grad, probe_grad, mean_misfit.reshape(())


def solution(mesh):
    in_specs = (
        P(None, "row", "col"),
        P(),
        P(("row", "col"), None, None),
        P(("row", "col"), None),
        P(),
    )
    out_specs = (P(None, "row", "col"), P(), P())
    return jax.shard_map(body, mesh=mesh, in_specs=in_specs, out_specs=out_specs, check_vma=False)
```

time: 123 us -> 119 us (0.967)
  local copies, waits for them, and re-layouts: 2.97 us -> 0.04 us
    unnamed x15 -> x14, local copies, waits for them, and re-layouts: 2.97 us -> 0.04 us
where the time goes in v5:
time: 119 us
  Pallas kernels  118 us (99%)
    pallas_call x1, Pallas kernels, tail(): pl.pallas_call(tail_kernel, name='tail', out_shape=[jax.ShapeDtypeStruct(...  61.6 us
    pallas_call x1, Pallas kernels, halos(): pl.pallas_call(halo_kernel, name='halos', out_shape=jax.ShapeDtypeStruct(...  40.8 us
    pallas_call x1, Pallas kernels, windows(): pl.pallas_call(windows_kernel, name='windows', out_shape=[jax.ShapeDtypeS...  12.4 us
    pallas_call x1, Pallas kernels, finished(): pl.pallas_call(finish_kernel, name='finished', out_shape=[jax.ShapeDtypeS...  2.94 us

profile of v5, /device:TPU:1, one launch (start us, length us, event | category | flops | bytes accessed | tf_op | source)
XLA Modules:
  0.0 118.6 jit_solution(15006698530208038966)
XLA Ops:
  0.6 0.0 copy-start
  0.6 0.0 copy-start.1
  0.7 0.0 copy-start.2
  0.7 0.0 copy-start.3
  0.7 0.0 copy-start.4
  0.7 0.0 copy-start.5
  0.7 0.0 copy-start.6
  0.7 40.8 %halos.1.ext = f32[2,10,768,128]{3,2,1,0:T(8,128)S(1)} custom-call(f32[2,512,1024]{2,1,0:T(8,128)} %sample.1), custom_call_target="tpu_custom_call" | custom-call | flops 40000000000 | bytes 1048576 | tf_op jit(solution)/shard_map/halos/pallas_call | solution.py:285
  41.6 0.0 copy-done
  41.6 0.0 copy-done.1
  41.6 0.0 copy-done.2
  41.6 0.0 copy-done.3
  41.6 0.0 copy-done.4
  41.6 0.0 copy-done.5
  41.6 0.0 copy-done.6
  41.6 12.4 %windows.1 = (f32[2,10,768,128]{3,2,1,0:T(8,128)S(1)}, f32[2,256,256]{2,1,0:T(8,128)S(1)}, f32[16,256]{1,0:T(8,128)S(1)}) custom-call(s32[2,16]{1,0:T(2,128)S(1)} %bitcast.3, s32[128]{0:T(128)S(1)} %copy-done.3, f32[16,256,256]{2,1,0:T(8,128)S(1)} %copy-done, f32[2,256,256]{2,1,0:T(8,128)S(1)} %copy-done.1, f32[4,256,256]{2,1,0:T(8,128)S(1)} %copy-done.5, ...), custom_call_target="tpu_custom_call" | custom-call | flops 12000000000 | bytes 8388608 | tf_op jit(solution)/shard_map/windows/pallas_call | solution.py:189
  54.0 61.6 %tail.1 = (f32[2,256,256]{2,1,0:T(8,128)S(1)}, f32[8,128]{1,0:T(8,128)S(1)}, f32[8,128]{1,0:T(8,128)S(1)}, f32[2,8,256,128]{3,2,1,0:T(8,128)S(1)}, f32[2,2,512,128]{3,2,1,0:T(8,128)S(1)}) custom-call(s32[1,128]{1,0:T(1,128)S(1)} %bitcast.4, f32[2,256,256]{2,1,0:T(8,128)S(1)} %get-tuple-element.14.pacc, f32[16,256]{1,0:T(8,128)S(1)} %get-tuple-element.15.stats, ...), custom_call_target="tpu_custom_call" | custom-call | flops 40000000000 | bytes 1048576 | tf_op jit(solution)/shard_map/tail/pallas_call | solution.py:406
  115.6 2.9 %finished.1 = (f32[2,512,1024]{2,1,0:T(8,128)}, f32[2,256,256]{2,1,0:T(8,128)}, f32[1,1]{1,0:T(1,128)}) custom-call(f32[8,128]{1,0:T(8,128)S(1)} %get-tuple-element.17.coeff, f32[8,128]{1,0:T(8,128)S(1)} %get-tuple-element.18.misfit, f32[2,256,256]{2,1,0:T(8,128)S(1)} %get-tuple-element.19.probe, f32[2,10,768,128]{3,2,1,0:T(8,128)S(1)} %get-tuple-element.16.acc, ...), custom_call_target="tpu_custom_call" | custom-call | flops 10000000 | bytes 10485760 | tf_op jit(solution)/shard_map/finished/pallas_call | solution.py:455
Async XLA Ops:
  0.6 40.9 %copy-start = (f32[16,256,256]{2,1,0:T(8,128)S(1)}, f32[16,256,256]{2,1,0:T(8,128)}, u32[]{:S(2)}) copy-start(f32[16,256,256]{2,1,0:T(8,128)} %patterns.1) | copy-start | bytes 12582916
  0.6 40.9 %copy-start.1 = (f32[2,256,256]{2,1,0:T(8,128)S(1)}, f32[2,256,256]{2,1,0:T(8,128)}, u32[]{:S(2)}) copy-start(f32[2,256,256]{2,1,0:T(8,128)} %probe.1) | copy-start | bytes 1572868
  0.7 40.9 %copy-start.2 = (s32[16,2]{0,1:T(2,128)S(1)}, s32[16,2]{0,1:T(2,128)}, u32[]{:S(2)}) copy-start(s32[16,2]{0,1:T(2,128)} %param.11) | copy-start | bytes 388
  0.7 40.9 %copy-start.3 = (s32[128]{0:T(128)S(1)}, s32[128]{0:T(128)}, u32[]{:S(2)}) copy-start(s32[128]{0:T(128)} %counts.1) | copy-start | bytes 1540
  0.7 40.9 %copy-start.4 = (f32[4,256,256]{2,1,0:T(8,128)S(1)}, f32[4,256,256]{2,1,0:T(8,128)}, u32[]{:S(2)}) copy-start(f32[4,256,256]{2,1,0:T(8,128)} %constant.7.clone.left_in) | copy-start | bytes 3145732
  0.7 40.9 %copy-start.5 = (f32[4,256,256]{2,1,0:T(8,128)S(1)}, f32[4,256,256]{2,1,0:T(8,128)}, u32[]{:S(2)}) copy-start(f32[4,256,256]{2,1,0:T(8,128)} %constant.6.clone.right_in) | copy-start | bytes 3145732
  0.7 40.9 %copy-start.6 = (f32[256,256]{1,0:T(8,128)S(1)}, f32[256,256]{1,0:T(8,128)}, u32[]{:S(2)}) copy-start(f32[256,256]{1,0:T(8,128)} %constant.8.clone.order_in) | copy-start | bytes 786436
